TPU v7x, 1024 devices: a whole 4x8x16 slice. The times are simulated.
1024 devices in a mesh: dp: 256 (over z, y_lo, x), mp: 4 (over y_hi, core).
Axes of the slice: x: 4, y: 8 (y_hi: 2, y_lo: 4; y = y_hi * 4 + y_lo), z: 16, core: 2. Of those that a mesh axis runs over, the one named last changes fastest.
Arguments:
- images: bfloat16 [32768, 1152], P('dp'), may hold values from -6 to 6
- texts: bfloat16 [32768, 1152], P('dp', 'mp'), may hold values from -6 to 6
- fc_in: bfloat16 [1152, 4304], P(None, 'mp'), may hold values from -0.1875 to 0.1875
- fc_out: bfloat16 [4304, 1152], P('mp'), may hold values from -0.09375 to 0.09375
- head: bfloat16 [1152, 1152], P('mp'), may hold values from -0.1875 to 0.1875
- partner: int32 [32768], P('dp'), may hold values from 0 to 127
Outputs:
- hidden_grad: bfloat16 [32768, 4304], P('dp', 'mp')
- text_grad: bfloat16 [32768, 1152], P('dp', 'mp')
- image_loss: float32 [32768], P('dp')
All inputs are finite; a program needn't handle non-finite values.
Results may differ from a plain program's by a relative error of at most 0.024.
Values may be sent and summed in bfloat16 or wider, within the bound.
No kernel may reach another device: no remote copies, remote signals or barrier semaphores. Data moves between devices by JAX's collectives and lax.ppermute only.
A program may use at most 32 MiB of HBM per device.

v0:
```python
import jax
import jax.numpy as jnp
from jax import lax
from jax.sharding import PartitionSpec as P

WINDOW = 8


logit_scale = 32.0
logit_bias = -2.0
loss_scale = 16.0
epsilon = 1e-06


def from_behind(value, axis, steps):
    count = lax.axis_size(axis)
    pairs = [(source, (source + steps) % count) for source in range(count)]
    return lax.ppermute(value, axis, pairs)


def unit_rows(embed):
    inverse = lax.rsqrt(jnp.sum(embed * embed, axis=1, keepdims=True) + epsilon)
    return (embed * inverse, inverse)


def tangent_rows(grad, unit, inverse):
    return ((grad - unit * jnp.sum(unit * grad, axis=1, keepdims=True)) * inverse).astype(
        jnp.bfloat16
    )


def positives(partner, first_row, count, sub_rows):
    columns = lax.iota(jnp.int32, count)
    hits = (first_row + columns)[None, :] == partner[:, None]
    return hits & (columns < sub_rows)[None, :]


def pair_terms(image_unit, visiting, positive):
    logits = (
        logit_scale
        * lax.dot_general(
            image_unit,
            visiting,
            (((1,), (1,)), ((), ())),
            precision=lax.Precision.HIGHEST,
            preferred_element_type=jnp.float32,
        )
        + logit_bias
    )
    label_sign = jnp.where(positive, 1.0, -1.0).astype(jnp.float32)
    flipped = -label_sign * logits
    loss_part = jnp.sum(jax.nn.softplus(flipped), axis=1)
    pair_grad = -loss_scale * label_sign * jax.nn.sigmoid(flipped)
    image_part = logit_scale * jnp.dot(
        pair_grad, visiting, precision=lax.Precision.HIGHEST, preferred_element_type=jnp.float32
    )
    block_part = logit_scale * lax.dot_general(
        pair_grad,
        image_unit,
        (((0,), (0,)), ((), ())),
        precision=lax.Precision.HIGHEST,
        preferred_element_type=jnp.float32,
    )
    return (loss_part, image_part, block_part)


def local(images, texts, fc_in, fc_out, head, partner):
    mp_parts = lax.axis_size("mp")
    mp_rank = lax.axis_index("mp")
    row_count = images.shape[0]
    sub_rows = row_count // mp_parts
    first_row = mp_rank * sub_rows
    pre_act = jnp.dot(images, fc_in, preferred_element_type=jnp.float32)
    activation = jax.nn.gelu(pre_act, approximate=True).astype(jnp.bfloat16)
    image_term = jnp.dot(activation, fc_out, preferred_element_type=jnp.float32)
    text_term = jnp.dot(texts, head, preferred_element_type=jnp.float32)
    image_sum, text_sum = (
        lax.psum(image_term.astype(jnp.bfloat16), "mp").astype(jnp.float32),
        lax.psum(text_term.astype(jnp.bfloat16), "mp").astype(jnp.float32),
    )
    text_unit, text_inv = unit_rows(text_sum)
    own_rows = lax.dynamic_slice_in_dim(text_unit, first_row, sub_rows, 0)
    image_unit, image_inv = unit_rows(images.astype(jnp.float32) + image_sum)
    visiting = own_rows
    carried = jnp.zeros((sub_rows, own_rows.shape[1]), jnp.float32)
    loss_sum = jnp.zeros((row_count,), jnp.float32)
    image_acc = jnp.zeros_like(image_unit)
    for offset in range(WINDOW):
        if offset == 0:
            positive = positives(partner, first_row, sub_rows, sub_rows)
        else:
            positive = jnp.zeros((row_count, sub_rows), jnp.bool_)
        loss_part, image_part, block_part = pair_terms(image_unit, visiting, positive)
        loss_sum = loss_sum + loss_part
        image_acc = image_acc + image_part
        carried = carried + block_part
        if offset + 1 < WINDOW:
            visiting, carried = (
                from_behind(visiting.astype(jnp.bfloat16), "dp", 1).astype(visiting.dtype),
                from_behind(carried.astype(jnp.bfloat16), "dp", 1).astype(carried.dtype),
            )
    own_grad = from_behind(carried.astype(jnp.bfloat16), "dp", 1 - WINDOW).astype(carried.dtype)
    placed = lax.dynamic_update_slice_in_dim(jnp.zeros_like(text_unit), own_grad, first_row, 0)
    unit_grad, text_unit_grad, loss_all = (
        lax.psum(image_acc.astype(jnp.bfloat16), "mp").astype(jnp.float32),
        lax.psum(placed.astype(jnp.bfloat16), "mp").astype(jnp.float32),
        lax.psum(loss_sum.astype(jnp.bfloat16), "mp").astype(jnp.float32),
    )
    text_emb_grad = tangent_rows(text_unit_grad, text_unit, text_inv)
    image_emb_grad = tangent_rows(unit_grad, image_unit, image_inv)
    act_grad = lax.dot_general(
        image_emb_grad, fc_out, (((1,), (1,)), ((), ())), preferred_element_type=jnp.float32
    )
    unused, pullback = jax.vjp(lambda value: jax.nn.gelu(value, approximate=True), pre_act)
    hidden_grad = pullback(act_grad)[0].astype(jnp.bfloat16)
    text_grad = lax.dot_general(
        text_emb_grad, head, (((1,), (1,)), ((), ())), preferred_element_type=jnp.float32
    ).astype(jnp.bfloat16)
    image_loss = loss_all / (WINDOW * row_count)
    return (hidden_grad, text_grad, image_loss)


def solution(mesh):
    return jax.shard_map(
        local,
        mesh=mesh,
        in_specs=(
            P("dp", None),
            P("dp", "mp"),
            P(None, "mp"),
            P("mp", None),
            P("mp", None),
            P("dp"),
        ),
        out_specs=(P("dp", "mp"), P("dp", "mp"), P("dp")),
        check_vma=False,
    )
```

profile of v0, /device:TPU:1, one launch (start us, length us, event | category | flops | bytes accessed | tf_op | source)
XLA Modules:
  0.0 307.1 jit_solution(12422243043237503790)
XLA Ops:
  7.2 2.3 convolution_convert_fusion
  9.6 2.7 fusion.105
  14.6 83.9 %all-reduce.7.cloned.1.call-done = (bf16[128,1152]{1,0:T(8,128)(2,1)}, bf16[128,1152]{1,0:T(8,128)(2,1)}) async-done(((bf16[128,1152]{1,0:T(8,128)(2,1)}, bf16[128,1152]{1,0:T(8,128)(2,1)}), (bf16[128,1152]{1,0:T(8,128)(2,1)}, bf16[128,1152]{1,0:T(8,128)(2,1)})) %all-reduce.7.cloned.1.call-update) | async-done | bytes 589840 | tf_op jit(solution)/shard_map/psum | solution.py:79
  104.3 3.1 collective-permute-start
  108.1 3.1 %collective-permute-start.7 = (bf16[32,1152]{1,0:T(8,128)(2,1)S(1)}, bf16[32,1152]{1,0:T(8,128)(2,1)S(1)}, u32[]{:S(2)}, u32[]{:S(2)}) collective-permute-start(bf16[32,1152]{1,0:T(8,128)(2,1)S(1)} %fusion.2), channel_id=1, source_target_pairs={{0,4},{4,8},{8,12},{12,16},{16,20},{20,24},{24,28},{28,32},{32,36}... | collective-permute-start | bytes 221192 | tf_op jit(solution)/shard_map/ppermute | solution.py:18
  111.2 6.2 %collective-permute-done = bf16[32,1152]{1,0:T(8,128)(2,1)S(1)} collective-permute-done((bf16[32,1152]{1,0:T(8,128)(2,1)S(1)}, bf16[32,1152]{1,0:T(8,128)(2,1)S(1)}, u32[]{:S(2)}, u32[]{:S(2)}) %collective-permute-start) | collective-permute-done | bytes 73760 | tf_op jit(solution)/shard_map/ppermute | solution.py:18
  120.0 1.9 collective-permute-start.8
  122.0 1.9 collective-permute-start.1
  124.4 9.7 %collective-permute-done.1 = bf16[32,1152]{1,0:T(8,128)(2,1)S(1)} collective-permute-done((bf16[32,1152]{1,0:T(8,128)(2,1)S(1)}, bf16[32,1152]{1,0:T(8,128)(2,1)S(1)}, u32[]{:S(2)}, u32[]{:S(2)}) %collective-permute-start.1) | collective-permute-done | bytes 73760 | tf_op jit(solution)/shard_map/ppermute | solution.py:18
  135.3 1.9 collective-permute-start.9
  139.6 9.6 %collective-permute-done.2 = bf16[32,1152]{1,0:T(8,128)(2,1)S(1)} collective-permute-done((bf16[32,1152]{1,0:T(8,128)(2,1)S(1)}, bf16[32,1152]{1,0:T(8,128)(2,1)S(1)}, u32[]{:S(2)}, u32[]{:S(2)}) %collective-permute-start.2) | collective-permute-done | bytes 73760 | tf_op jit(solution)/shard_map/ppermute | solution.py:18
  150.4 1.9 collective-permute-start.10
  154.7 9.5 %collective-permute-done.3 = bf16[32,1152]{1,0:T(8,128)(2,1)S(1)} collective-permute-done((bf16[32,1152]{1,0:T(8,128)(2,1)S(1)}, bf16[32,1152]{1,0:T(8,128)(2,1)S(1)}, u32[]{:S(2)}, u32[]{:S(2)}) %collective-permute-start.3) | collective-permute-done | bytes 73760 | tf_op jit(solution)/shard_map/ppermute | solution.py:18
  165.3 1.9 collective-permute-start.11
  167.3 1.9 collective-permute-start.4
  169.7 8.7 %collective-permute-done.4 = bf16[32,1152]{1,0:T(8,128)(2,1)S(1)} collective-permute-done((bf16[32,1152]{1,0:T(8,128)(2,1)S(1)}, bf16[32,1152]{1,0:T(8,128)(2,1)S(1)}, u32[]{:S(2)}, u32[]{:S(2)}) %collective-permute-start.4) | collective-permute-done | bytes 73760 | tf_op jit(solution)/shard_map/ppermute | solution.py:18
  183.9 8.7 %collective-permute-done.5 = bf16[32,1152]{1,0:T(8,128)(2,1)S(1)} collective-permute-done((bf16[32,1152]{1,0:T(8,128)(2,1)S(1)}, bf16[32,1152]{1,0:T(8,128)(2,1)S(1)}, u32[]{:S(2)}, u32[]{:S(2)}) %collective-permute-start.5) | collective-permute-done | bytes 73760 | tf_op jit(solution)/shard_map/ppermute | solution.py:18
  193.8 2.1 collective-permute-start.13
  195.8 2.1 collective-permute-start.6
  198.4 8.5 %collective-permute-done.6 = bf16[32,1152]{1,0:T(8,128)(2,1)S(1)} collective-permute-done((bf16[32,1152]{1,0:T(8,128)(2,1)S(1)}, bf16[32,1152]{1,0:T(8,128)(2,1)S(1)}, u32[]{:S(2)}, u32[]{:S(2)}) %collective-permute-start.6) | collective-permute-done | bytes 73760 | tf_op jit(solution)/shard_map/ppermute | solution.py:18
  211.2 4.1 %collective-permute-done.14 = bf16[32,1152]{1,0:T(8,128)(2,1)S(1)} collective-permute-done((bf16[32,1152]{1,0:T(8,128)(2,1)S(1)}, bf16[32,1152]{1,0:T(8,128)(2,1)S(1)}, u32[]{:S(2)}, u32[]{:S(2)}) %collective-permute-start.14) | collective-permute-done | bytes 73760 | tf_op jit(solution)/shard_map/ppermute | solution.py:18
  216.8 15.8 %psum.39 = bf16[128]{0:T(256)(128)(2,1)S(1)} all-reduce(bf16[128]{0:T(256)(128)(2,1)S(1)} %add_convert_fusion.7), channel_id=1, replica_groups=mesh['dp'=256,'mp'=4] {'mp'}, use_global_device_ids=true, to_apply=%region_16.17 | all-reduce | flops 128 | bytes 512 | tf_op jit(solution)/shard_map/psum | solution.py:107
  233.1 61.6 %all-reduce.5.cloned.1.call-done = (bf16[128,1152]{1,0:T(8,128)(2,1)}, bf16[128,1152]{1,0:T(8,128)(2,1)}) async-done(((bf16[128,1152]{1,0:T(8,128)(2,1)}, bf16[128,1152]{1,0:T(8,128)(2,1)}), (bf16[128,1152]{1,0:T(8,128)(2,1)}, bf16[128,1152]{1,0:T(8,128)(2,1)})) %all-reduce.5.cloned.1.call-update) | async-done | bytes 589840 | tf_op jit(solution)/shard_map/psum | solution.py:105
  296.2 2.3 convolution_convert_fusion.2
  (77 shorter events, 37.1 us)
Async XLA Ops:
  7.2 5.9 %copy-start = (bf16[1076,1152]{1,0:T(8,128)(2,1)S(1)}, bf16[1076,1152]{1,0:T(8,128)(2,1)}, u32[]{:S(2)}) copy-start(bf16[1076,1152]{1,0:T(8,128)(2,1)} %param.9) | copy-start | bytes 7437316
  7.2 91.3 %all-reduce.7.cloned.1.call-start = ((), (), s32[]{:S(2)}) async-start(), calls=%async_computation.1 | async-start | bytes 1179648 | tf_op jit(solution)/shard_map/psum | solution.py:79
  13.1 86.6 %copy-start.1 = (bf16[128,1152]{1,0:T(8,128)(2,1)S(1)}, bf16[128,1152]{1,0:T(8,128)(2,1)}, u32[]{:S(2)}) copy-start(bf16[128,1152]{1,0:T(8,128)(2,1)} %param.6) | copy-start | bytes 884740
  13.1 88.9 %copy-start.7 = (s32[128]{0:T(128)S(1)}, s32[128]{0:T(128)}, u32[]{:S(2)}) copy-start(s32[128]{0:T(128)} %param.11) | copy-start | bytes 1540
  14.5 280.3 %all-reduce.5.cloned.1.call-start = ((), (), s32[]{:S(2)}) async-start(), calls=%async_computation | async-start | bytes 1179648 | tf_op jit(solution)/shard_map/psum | solution.py:105
  98.5 5.2 %copy-start.2 = (bf16[128,1152]{1,0:T(8,128)(2,1)S(1)}, bf16[128,1152]{1,0:T(8,128)(2,1)}, u32[]{:S(2)}) copy-start(bf16[128,1152]{1,0:T(8,128)(2,1)} %get-tuple-element.6) | copy-start | bytes 884740
  104.3 13.1 %collective-permute-start = (bf16[32,1152]{1,0:T(8,128)(2,1)S(1)}, bf16[32,1152]{1,0:T(8,128)(2,1)S(1)}, u32[]{:S(2)}, u32[]{:S(2)}) collective-permute-start(bf16[32,1152]{1,0:T(8,128)(2,1)S(1)} %dynamic-slice_convert_fusion), channel_id=1, source_target_pairs={{0,4},{4,8},{8,12},{12,16},{16,20},{20,24},{24,28},{28,32},{32,36}... | collective-permute-start | bytes 221192 | tf_op jit(solution)/shard_map/ppermute | solution.py:18
  108.1 11.4 %collective-permute-start.7 = (bf16[32,1152]{1,0:T(8,128)(2,1)S(1)}, bf16[32,1152]{1,0:T(8,128)(2,1)S(1)}, u32[]{:S(2)}, u32[]{:S(2)}) collective-permute-start(bf16[32,1152]{1,0:T(8,128)(2,1)S(1)} %fusion.2), channel_id=1, source_target_pairs={{0,4},{4,8},{8,12},{12,16},{16,20},{20,24},{24,28},{28,32},{32,36}... | collective-permute-start | bytes 221192 | tf_op jit(solution)/shard_map/ppermute | solution.py:18
  120.0 15.2 %collective-permute-start.8 = (bf16[32,1152]{1,0:T(8,128)(2,1)S(1)}, bf16[32,1152]{1,0:T(8,128)(2,1)S(1)}, u32[]{:S(2)}, u32[]{:S(2)}) collective-permute-start(bf16[32,1152]{1,0:T(8,128)(2,1)S(1)} %add_convert_fusion.6), channel_id=1, source_target_pairs={{0,4},{4,8},{8,12},{12,16},{16,20},{20,24},{24,28},{28,32},{32,36}... | collective-permute-start | bytes 221192 | tf_op jit(solution)/shard_map/ppermute | solution.py:18
  122.0 12.1 %collective-permute-start.1 = (bf16[32,1152]{1,0:T(8,128)(2,1)S(1)}, bf16[32,1152]{1,0:T(8,128)(2,1)S(1)}, u32[]{:S(2)}, u32[]{:S(2)}) collective-permute-start(bf16[32,1152]{1,0:T(8,128)(2,1)S(1)} %collective-permute-done), channel_id=1, source_target_pairs={{0,4},{4,8},{8,12},{12,16},{16,20},{20,24},{24,28},{28,32},{32,36}... | collective-permute-start | bytes 221192 | tf_op jit(solution)/shard_map/ppermute | solution.py:18
  135.3 15.1 %collective-permute-start.9 = (bf16[32,1152]{1,0:T(8,128)(2,1)S(1)}, bf16[32,1152]{1,0:T(8,128)(2,1)S(1)}, u32[]{:S(2)}, u32[]{:S(2)}) collective-permute-start(bf16[32,1152]{1,0:T(8,128)(2,1)S(1)} %add_convert_fusion.5), channel_id=1, source_target_pairs={{0,4},{4,8},{8,12},{12,16},{16,20},{20,24},{24,28},{28,32},{32,36}... | collective-permute-start | bytes 221192 | tf_op jit(solution)/shard_map/ppermute | solution.py:18
  137.2 12.0 %collective-permute-start.2 = (bf16[32,1152]{1,0:T(8,128)(2,1)S(1)}, bf16[32,1152]{1,0:T(8,128)(2,1)S(1)}, u32[]{:S(2)}, u32[]{:S(2)}) collective-permute-start(bf16[32,1152]{1,0:T(8,128)(2,1)S(1)} %collective-permute-done.1), channel_id=1, source_target_pairs={{0,4},{4,8},{8,12},{12,16},{16,20},{20,24},{24,28},{28,32},{32,36}... | collective-permute-start | bytes 221192 | tf_op jit(solution)/shard_map/ppermute | solution.py:18
  150.4 14.9 %collective-permute-start.10 = (bf16[32,1152]{1,0:T(8,128)(2,1)S(1)}, bf16[32,1152]{1,0:T(8,128)(2,1)S(1)}, u32[]{:S(2)}, u32[]{:S(2)}) collective-permute-start(bf16[32,1152]{1,0:T(8,128)(2,1)S(1)} %add_convert_fusion.4), channel_id=1, source_target_pairs={{0,4},{4,8},{8,12},{12,16},{16,20},{20,24},{24,28},{28,32},{32,36}... | collective-permute-start | bytes 221192 | tf_op jit(solution)/shard_map/ppermute | solution.py:18
  152.3 11.9 %collective-permute-start.3 = (bf16[32,1152]{1,0:T(8,128)(2,1)S(1)}, bf16[32,1152]{1,0:T(8,128)(2,1)S(1)}, u32[]{:S(2)}, u32[]{:S(2)}) collective-permute-start(bf16[32,1152]{1,0:T(8,128)(2,1)S(1)} %collective-permute-done.2), channel_id=1, source_target_pairs={{0,4},{4,8},{8,12},{12,16},{16,20},{20,24},{24,28},{28,32},{32,36}... | collective-permute-start | bytes 221192 | tf_op jit(solution)/shard_map/ppermute | solution.py:18
  165.3 14.2 %collective-permute-start.11 = (bf16[32,1152]{1,0:T(8,128)(2,1)S(1)}, bf16[32,1152]{1,0:T(8,128)(2,1)S(1)}, u32[]{:S(2)}, u32[]{:S(2)}) collective-permute-start(bf16[32,1152]{1,0:T(8,128)(2,1)S(1)} %add_convert_fusion.3), channel_id=1, source_target_pairs={{0,4},{4,8},{8,12},{12,16},{16,20},{20,24},{24,28},{28,32},{32,36}... | collective-permute-start | bytes 221192 | tf_op jit(solution)/shard_map/ppermute | solution.py:18
  167.3 11.1 %collective-permute-start.4 = (bf16[32,1152]{1,0:T(8,128)(2,1)S(1)}, bf16[32,1152]{1,0:T(8,128)(2,1)S(1)}, u32[]{:S(2)}, u32[]{:S(2)}) collective-permute-start(bf16[32,1152]{1,0:T(8,128)(2,1)S(1)} %collective-permute-done.3), channel_id=1, source_target_pairs={{0,4},{4,8},{8,12},{12,16},{16,20},{20,24},{24,28},{28,32},{32,36}... | collective-permute-start | bytes 221192 | tf_op jit(solution)/shard_map/ppermute | solution.py:18
  179.6 14.2 %collective-permute-start.12 = (bf16[32,1152]{1,0:T(8,128)(2,1)S(1)}, bf16[32,1152]{1,0:T(8,128)(2,1)S(1)}, u32[]{:S(2)}, u32[]{:S(2)}) collective-permute-start(bf16[32,1152]{1,0:T(8,128)(2,1)S(1)} %add_convert_fusion.2), channel_id=1, source_target_pairs={{0,4},{4,8},{8,12},{12,16},{16,20},{20,24},{24,28},{28,32},{32,36}... | collective-permute-start | bytes 221192 | tf_op jit(solution)/shard_map/ppermute | solution.py:18
  181.5 11.1 %collective-permute-start.5 = (bf16[32,1152]{1,0:T(8,128)(2,1)S(1)}, bf16[32,1152]{1,0:T(8,128)(2,1)S(1)}, u32[]{:S(2)}, u32[]{:S(2)}) collective-permute-start(bf16[32,1152]{1,0:T(8,128)(2,1)S(1)} %collective-permute-done.4), channel_id=1, source_target_pairs={{0,4},{4,8},{8,12},{12,16},{16,20},{20,24},{24,28},{28,32},{32,36}... | collective-permute-start | bytes 221192 | tf_op jit(solution)/shard_map/ppermute | solution.py:18
  193.8 101.0 %copy-start.3 = (bf16[128,1152]{1,0:T(8,128)(2,1)S(1)}, bf16[128,1152]{1,0:T(8,128)(2,1)}, u32[]{:S(2)}) copy-start(bf16[128,1152]{1,0:T(8,128)(2,1)} %get-tuple-element.5) | copy-start | bytes 884740
  193.8 14.3 %collective-permute-start.13 = (bf16[32,1152]{1,0:T(8,128)(2,1)S(1)}, bf16[32,1152]{1,0:T(8,128)(2,1)S(1)}, u32[]{:S(2)}, u32[]{:S(2)}) collective-permute-start(bf16[32,1152]{1,0:T(8,128)(2,1)S(1)} %add_convert_fusion.1), channel_id=1, source_target_pairs={{0,4},{4,8},{8,12},{12,16},{16,20},{20,24},{24,28},{28,32},{32,36}... | collective-permute-start | bytes 221192 | tf_op jit(solution)/shard_map/ppermute | solution.py:18
  195.8 11.1 %collective-permute-start.6 = (bf16[32,1152]{1,0:T(8,128)(2,1)S(1)}, bf16[32,1152]{1,0:T(8,128)(2,1)S(1)}, u32[]{:S(2)}, u32[]{:S(2)}) collective-permute-start(bf16[32,1152]{1,0:T(8,128)(2,1)S(1)} %collective-permute-done.5), channel_id=1, source_target_pairs={{0,4},{4,8},{8,12},{12,16},{16,20},{20,24},{24,28},{28,32},{32,36}... | collective-permute-start | bytes 221192 | tf_op jit(solution)/shard_map/ppermute | solution.py:18
  208.1 7.2 %collective-permute-start.14 = (bf16[32,1152]{1,0:T(8,128)(2,1)S(1)}, bf16[32,1152]{1,0:T(8,128)(2,1)S(1)}, u32[]{:S(2)}, u32[]{:S(2)}) collective-permute-start(bf16[32,1152]{1,0:T(8,128)(2,1)S(1)} %add_convert_fusion), channel_id=1, source_target_pairs={{0,996},{4,1000},{8,1004},{12,1008},{16,1012},{20,1016},{24,1020},... | collective-permute-start | bytes 221192 | tf_op jit(solution)/shard_map/ppermute | solution.py:18
  294.7 3.7 %copy-start.5 = (f32[128,1076]{0,1:T(8,128)S(1)}, f32[128,1076]{0,1:T(8,128)}, u32[]{:S(2)}) copy-start(f32[128,1076]{0,1:T(8,128)} %copy-done.4) | copy-start | bytes 1652740
  294.7 3.7 %copy-start.6 = (bf16[128,1152]{1,0:T(8,128)(2,1)S(1)}, bf16[128,1152]{1,0:T(8,128)(2,1)}, u32[]{:S(2)}) copy-start(bf16[128,1152]{1,0:T(8,128)(2,1)} %get-tuple-element.3) | copy-start | bytes 884740
  (1 other events, 0.8 us)
Sparse Core Ops, SparseCore 0:
  14.6 83.8 all-reduce.6
  216.9 77.8 all-reduce.4
where the time goes:
time: 308 us; the launch traced here: 307 us
  waiting for transfers between devices  212 us (69%)
  starting transfers between devices  31.5 us (10%)
  matrix products  25.4 us (8%)
  blocking collectives  15.8 us (5%)
  between operations  14.4 us (5%)
  other arithmetic  6.16 us (2%)
    psum x1, waiting for transfers between devices, local(): lax.psum(text_term.astype(jnp.bfloat16), 'mp').astype(jnp.float32)  83.9 us
    ppermute x15, waiting for transfers between devices, from_behind(): return lax.ppermute(value, axis, pairs)  66.6 us
    psum x1, waiting for transfers between devices, local(): lax.psum(image_acc.astype(jnp.bfloat16), 'mp').astype(jnp.float32)  61.6 us
    ppermute x15, starting transfers between devices, from_behind(): return lax.ppermute(value, axis, pairs)  31.4 us
    psum x1, blocking collectives, local(): lax.psum(loss_sum.astype(jnp.bfloat16), 'mp').astype(jnp.float32)  15.8 us
  transfers between devices with their start and end apart: 17, of which 11 were waited for; matrix products, arithmetic and copies ran while one was open for 4% of the time, Pallas kernels for 0%

commit v1 on v0

v1 whole, which is shorter than its diff:
```python
import jax
import jax.numpy as jnp
from jax import lax
from jax.sharding import Mesh, PartitionSpec as P

WINDOW = 8


logit_scale = 32.0
logit_bias = -2.0
loss_scale = 16.0
epsilon = 1e-06

AXES = ("z", "y_lo", "x", "y_hi", "core")
SIZES = (16, 4, 4, 2, 2)
MP = ("y_hi", "core")
NEAR = 4


def place(block, role):
    z = block // 16
    y_hi = (role // 2) ^ (z & 1)
    return block * 4 + y_hi * 2 + role % 2


def moves(shift):
    return [
        (place(block, role), place((block + shift(role)) % 256, role))
        for block in range(256)
        for role in range(4)
    ]


def move(value, shift):
    return lax.ppermute(value, AXES, moves(shift))


def unit_rows(embed):
    inverse = lax.rsqrt(jnp.sum(embed * embed, axis=1, keepdims=True) + epsilon)
    return (embed * inverse, inverse)


def tangent_rows(grad, unit, inverse):
    return ((grad - unit * jnp.sum(unit * grad, axis=1, keepdims=True)) * inverse).astype(
        jnp.bfloat16
    )


def core_sum(term):
    halves = term.astype(jnp.bfloat16).reshape(2, term.shape[0] // 2, term.shape[1])
    got = lax.all_to_all(halves, "core", 0, 0).astype(jnp.float32)
    return (got[0] + got[1]).astype(jnp.bfloat16)


def chip_sum(gathered):
    both = gathered[:2].astype(jnp.float32) + gathered[2:].astype(jnp.float32)
    return both.reshape(both.shape[0] * both.shape[1], both.shape[2])


def local(images, texts, fc_in, fc_out, head, partner):
    rows, width = images.shape
    shift = 2 * (lax.axis_index("y_hi") ^ (lax.axis_index("z") & 1)) + lax.axis_index("core")

    text_term = jnp.dot(texts, head, preferred_element_type=jnp.float32)
    pre_act = jnp.dot(images, fc_in, preferred_element_type=jnp.float32)
    activation = jax.nn.gelu(pre_act, approximate=True).astype(jnp.bfloat16)
    image_term = jnp.dot(activation, fc_out, preferred_element_type=jnp.float32)

    text_emb = chip_sum(lax.all_gather(core_sum(text_term), MP))
    text_unit, text_inv = unit_rows(text_emb)
    text_own = text_unit.astype(jnp.bfloat16)
    text_far = move(text_own, lambda role: NEAR)
    image_emb = images.astype(jnp.float32) + chip_sum(lax.all_gather(core_sum(image_term), MP))
    image_unit, image_inv = unit_rows(image_emb)
    scored = move(image_unit.astype(jnp.bfloat16), lambda role: -role)
    visiting = jnp.concatenate([text_own, text_far], 0)

    logits = (
        logit_scale
        * lax.dot_general(
            scored, visiting, (((1,), (1,)), ((), ())), preferred_element_type=jnp.float32
        )
        + logit_bias
    )
    columns = lax.broadcasted_iota(jnp.int32, logits.shape, 1)
    positive = (columns == partner[:, None]) & (shift == 0)
    label_sign = jnp.where(positive, 1.0, -1.0).astype(jnp.float32)
    flipped = -label_sign * logits
    loss_part = jnp.sum(jax.nn.softplus(flipped), axis=1, keepdims=True)
    pair_grad = (-loss_scale * label_sign * jax.nn.sigmoid(flipped)).astype(jnp.bfloat16)
    image_part = logit_scale * jnp.dot(pair_grad, visiting, preferred_element_type=jnp.float32)
    text_part = logit_scale * lax.dot_general(
        pair_grad, scored, (((0,), (0,)), ((), ())), preferred_element_type=jnp.float32
    )

    loss_high = loss_part.astype(jnp.bfloat16)
    loss_low = (loss_part - loss_high.astype(jnp.float32)).astype(jnp.bfloat16)
    lanes = lax.broadcasted_iota(jnp.int32, (rows, 128), 1)
    loss_lanes = jnp.where(lanes == 0, loss_high, jnp.where(lanes == 1, loss_low, 0))
    image_sent = jnp.concatenate([image_part.astype(jnp.bfloat16), loss_lanes], 1)
    image_back = move(image_sent, lambda role: role)
    text_back = move(text_part[rows:].astype(jnp.bfloat16), lambda role: -NEAR)
    text_total = text_part[:rows] + text_back.astype(jnp.float32)

    image_half = core_sum(image_back.astype(jnp.float32))
    text_half = core_sum(text_total)
    image_sums, text_sums = lax.all_gather((image_half, text_half), MP)
    image_all = chip_sum(image_sums)
    loss_all = image_all[:, width] + image_all[:, width + 1]
    image_emb_grad = tangent_rows(image_all[:, :width], image_unit, image_inv)
    text_emb_grad = tangent_rows(chip_sum(text_sums), text_unit, text_inv)

    act_grad = lax.dot_general(
        image_emb_grad, fc_out, (((1,), (1,)), ((), ())), preferred_element_type=jnp.float32
    )
    unused, pullback = jax.vjp(lambda value: jax.nn.gelu(value, approximate=True), pre_act)
    hidden_grad = pullback(act_grad)[0].astype(jnp.bfloat16)
    text_grad = lax.dot_general(
        text_emb_grad, head, (((1,), (1,)), ((), ())), preferred_element_type=jnp.float32
    ).astype(jnp.bfloat16)
    image_loss = loss_all / (WINDOW * rows)
    return (hidden_grad, text_grad, image_loss)


def solution(mesh):
    dp = ("z", "y_lo", "x")
    return jax.shard_map(
        local,
        mesh=Mesh(mesh.devices.reshape(SIZES), AXES),
        in_specs=(P(dp, None), P(dp, MP), P(None, MP), P(MP, None), P(MP, None), P(dp)),
        out_specs=(P(dp, MP), P(dp, MP), P(dp)),
        check_vma=False,
    )
```

time: 308 us -> 144 us (0.47)
  waiting for transfers between devices: 212 us -> 11.8 us
  blocking collectives: 15.8 us -> 58 us
  between operations: 14.4 us -> 0.88 us
  starting transfers between devices: 31.5 us -> 44.7 us
  matrix products: 25.4 us -> 14.7 us
  other arithmetic: 6.16 us -> 10.4 us
    psum x2 -> x0, waiting for transfers between devices: 146 us -> none  [the longest x1 83.9 us: local(): lax.psum(text_term.astype(jnp.bfloat16), 'mp').astype(jnp.float32)]
    ppermute x15 -> x4, waiting for transfers between devices: 66.6 us -> 11.8 us  [move(): return lax.ppermute(value, AXES, moves(shift))]
    all_gather x0 -> x4, blocking collectives: none -> 44.7 us  [the longest x2 23.6 us: local(): image_sums, text_sums = lax.all_gather((image_half, text_half), MP)]
    all_to_all x0 -> x2, starting transfers between devices: none -> 21.7 us  [core_sum(): got = lax.all_to_all(halves, 'core', 0, 0).astype(jnp.float32)]
    psum x1 -> x0, blocking collectives: 15.8 us -> none  [local(): lax.psum(loss_sum.astype(jnp.bfloat16), 'mp').astype(jnp.float32)]
    all_to_all x0 -> x2, blocking collectives: none -> 13.3 us  [core_sum(): got = lax.all_to_all(halves, 'core', 0, 0).astype(jnp.float32)]
    dot_general x24 -> x3, matrix products: 14.9 us -> 4.39 us  [the longest x1 1.62 us: local(): lax.dot_general(scored, visiting, (((1,), (1,)), ((), ())), preferred_ele...]
    ppermute x15 -> x4, starting transfers between devices: 31.4 us -> 23 us  [move(): return lax.ppermute(value, AXES, moves(shift))]
  transfers between devices with their start and end apart: 17 -> 6, of which waited for: 11 -> 1; matrix products, arithmetic and copies ran while one was open for 4% -> 11% of each run, Pallas kernels for 0% -> 0%
where the time goes in v1:
time: 144 us; the launch traced here: 142 us
  blocking collectives  58 us (40%)
  starting transfers between devices  44.7 us (31%)
  matrix products  14.7 us (10%)
  waiting for transfers between devices  11.8 us (8%)
  other arithmetic  10.4 us (7%)
  local copies, waits for them, and re-layouts  1.76 us (1%)
    all_gather x2, blocking collectives, local(): image_sums, text_sums = lax.all_gather((image_half, text_half), MP)  23.6 us
    ppermute x4, starting transfers between devices, move(): return lax.ppermute(value, AXES, moves(shift))  23 us
    all_to_all x2, starting transfers between devices, core_sum(): got = lax.all_to_all(halves, 'core', 0, 0).astype(jnp.float32)  21.7 us
    all_to_all x2, blocking collectives, core_sum(): got = lax.all_to_all(halves, 'core', 0, 0).astype(jnp.float32)  13.3 us
    ppermute x4, waiting for transfers between devices, move(): return lax.ppermute(value, AXES, moves(shift))  11.8 us
    all_gather x1, blocking collectives, local(): lax.all_gather(core_sum(image_term), MP)  11.6 us
    all_gather x1, blocking collectives, local(): text_emb = chip_sum(lax.all_gather(core_sum(text_term), MP))  9.56 us
  transfers between devices with their start and end apart: 6, of which 1 were waited for; matrix products, arithmetic and copies ran while one was open for 11% of the time, Pallas kernels for 0%

profile of v1, /device:TPU:1, one launch (start us, length us, event | category | flops | bytes accessed | tf_op | source)
XLA Modules:
  0.0 142.3 jit_solution(7051619918806876017)
XLA Ops:
  0.6 2.8 %fusion.40 = f32[128,1076]{0,1:T(8,128)S(1)} fusion(bf16[128,1152]{1,0:T(8,128)(2,1)} %param.6, bf16[1152,1076]{0,1:T(8,128)(2,1)} %param.8), kind=kOutput, calls=%fused_computation.79 | convolution fusion | flops 317325312 | bytes 3324928 | tf_op jit(solution)/shard_map/dot_general | solution.py:65
  3.5 1.4 convolution_convert_fusion.1
  4.9 17.6 %all-to-all-start = ((bf16[2,64,1152]{2,1,0:T(8,128)(2,1)}), bf16[2,64,1152]{2,1,0:T(8,128)(2,1)S(1)}, u32[]{:S(2)}, u32[]{:S(2)}) async-start(bf16[2,64,1152]{2,1,0:T(8,128)(2,1)} %bitcast), calls=%async_computation | async-start | bytes 589824 | tf_op jit(solution)/shard_map/all_to_all | solution.py:51
  22.5 2.2 %convolution_convert_fusion = bf16[128,1152]{1,0:T(8,128)(2,1)} fusion(bf16[128,288]{0,1:T(8,128)(2,1)S(1)} %copy-done.7, bf16[288,1152]{1,0:T(8,128)(2,1)} %param.10), kind=kOutput, calls=%fused_computation.3 | convolution fusion | flops 85082112 | bytes 1032192 | tf_op jit(solution)/shard_map/dot_general | solution.py:64
  25.4 4.1 %all-to-all-start.1 = ((bf16[2,64,1152]{2,1,0:T(8,128)(2,1)}), bf16[2,64,1152]{2,1,0:T(8,128)(2,1)}, u32[]{:S(2)}, u32[]{:S(2)}) async-start(bf16[2,64,1152]{2,1,0:T(8,128)(2,1)} %bitcast.38), calls=%async_computation.1 | async-start | bytes 589824 | tf_op jit(solution)/shard_map/all_to_all | solution.py:51
  30.6 11.6 %all_gather.16 = bf16[4,64,1152]{2,1,0:T(8,128)(2,1)S(1)} all-gather(bf16[1,64,1152]{2,1,0:T(8,128)(2,1)S(1)} %fusion.18), channel_id=1, replica_groups=mesh['z'=16,'y_lo'=4,'x'=4,'y_hi'=2,'core'=2] {'y_hi','core'}, dimensions={0}, use_global_device_ids=true | all-gather | bytes 737280 | tf_op jit(solution)/shard_map/all_gather | solution.py:73
  43.2 13.7 %collective-permute-start = (bf16[128,1152]{1,0:T(8,128)(2,1)}, bf16[128,1152]{1,0:T(8,128)(2,1)}, u32[]{:S(2)}, u32[]{:S(2)}) collective-permute-start(bf16[128,1152]{1,0:T(8,128)(2,1)} %multiply_convert_fusion.2), channel_id=1, source_target_pairs={{0,0},{1,1023},{2,1016},{3,1013},{4,4},{5,1},{6,1020},{7,1017},{8,... | collective-permute-start | bytes 884744 | tf_op jit(solution)/shard_map/ppermute | solution.py:35
  57.0 1.0 convert_element_type.135
  58.0 9.6 %all_gather.17 = bf16[4,64,1152]{2,1,0:T(8,128)(2,1)S(1)} all-gather(bf16[1,64,1152]{2,1,0:T(8,128)(2,1)S(1)} %fusion.17), channel_id=1, replica_groups=mesh['z'=16,'y_lo'=4,'x'=4,'y_hi'=2,'core'=2] {'y_hi','core'}, dimensions={0}, use_global_device_ids=true | all-gather | bytes 737280 | tf_op jit(solution)/shard_map/all_gather | solution.py:69
  69.4 1.9 %fusion.6 = bf16[128,1152]{1,0:T(8,128)(2,1)} fusion(f32[2,64,1152]{2,1,0:T(8,128)} %get-tuple-element.8, f32[128]{0:T(128)S(1)} %rsqrt.22), kind=kLoop, calls=%fused_computation.29 | loop fusion | flops 294912 | bytes 885248 | tf_op jit(solution)/shard_map/convert_element_type | solution.py:71
  71.3 1.9 %collective-permute-start.1 = (bf16[128,1152]{1,0:T(8,128)(2,1)}, bf16[128,1152]{1,0:T(8,128)(2,1)}, u32[]{:S(2)}, u32[]{:S(2)}) collective-permute-start(bf16[128,1152]{1,0:T(8,128)(2,1)} %fusion.6), channel_id=1, source_target_pairs={{0,16},{1,17},{2,18},{3,19},{4,20},{5,21},{6,22},{7,23},{8,24},{9,... | collective-permute-start | bytes 884744 | tf_op jit(solution)/shard_map/ppermute | solution.py:35
  73.2 11.8 %collective-permute-done.1 = bf16[128,1152]{1,0:T(8,128)(2,1)} collective-permute-done((bf16[128,1152]{1,0:T(8,128)(2,1)}, bf16[128,1152]{1,0:T(8,128)(2,1)}, u32[]{:S(2)}, u32[]{:S(2)}) %collective-permute-start.1) | collective-permute-done | bytes 294944 | tf_op jit(solution)/shard_map/ppermute | solution.py:35
  85.1 1.6 %fusion.27 = (f32[128]{0:T(128)S(1)}, f32[128,256]{1,0:T(8,128)S(1)}) fusion(bf16[128,1152]{1,0:T(8,128)(2,1)} %collective-permute-done, bf16[128,1152]{1,0:T(8,128)(2,1)} %collective-permute-done.1, bf16[128,1152]{1,0:T(8,128)(2,1)} %fusion.6, pred[]{:T(512)S(6)} %eq.27, s32[128]{0:T(128)S(1)} %copy-done.8), kind=kOutput, calls=%fused_computation.60 | convolution fusion | flops 77135744 | bytes 1016833 | tf_op jit(solution)/shard_map/dot_general | solution.py:80
  86.7 1.4 convolution_multiply_fusion
  88.1 3.0 %collective-permute-start.3 = (bf16[128,1152]{1,0:T(8,128)(2,1)S(1)}, bf16[128,1152]{1,0:T(8,128)(2,1)S(1)}, u32[]{:S(2)}, u32[]{:S(2)}) collective-permute-start(bf16[128,1152]{1,0:T(8,128)(2,1)S(1)} %slice.157), channel_id=1, source_target_pairs={{0,1010},{1,1011},{2,1008},{3,1009},{4,1014},{5,1015},{6,1012},{7,... | collective-permute-start | bytes 884744 | tf_op jit(solution)/shard_map/ppermute | solution.py:35
  91.2 1.4 fusion
  93.4 4.3 %collective-permute-start.2 = (bf16[128,1280]{1,0:T(8,128)(2,1)}, bf16[128,1280]{1,0:T(8,128)(2,1)}, u32[]{:S(2)}, u32[]{:S(2)}) collective-permute-start(bf16[128,1280]{1,0:T(8,128)(2,1)} %pad_maximum_fusion.3), channel_id=1, source_target_pairs={{0,0},{1,5},{2,10},{3,15},{4,4},{5,9},{6,14},{7,19},{8,8},{9,13},{... | collective-permute-start | bytes 983048 | tf_op jit(solution)/shard_map/ppermute | solution.py:35
  97.9 8.4 %all_to_all.20 = bf16[2,64,1152]{2,1,0:T(8,128)(2,1)S(1)} all-to-all(bf16[2,64,1152]{2,1,0:T(8,128)(2,1)S(1)} %bitcast.39), channel_id=1, replica_groups=mesh['z'=16,'y_lo'=4,'x'=4,'y_hi'=2,'core'=2] {'core'}, dimensions={0} | all-to-all | bytes 589824 | tf_op jit(solution)/shard_map/all_to_all | solution.py:51
  106.4 11.6 %all_gather.19 = bf16[4,64,1152]{2,1,0:T(8,128)(2,1)S(1)} all-gather(bf16[1,64,1152]{2,1,0:T(8,128)(2,1)S(1)} %fusion.16), channel_id=1, replica_groups=mesh['z'=16,'y_lo'=4,'x'=4,'y_hi'=2,'core'=2] {'y_hi','core'}, dimensions={0}, use_global_device_ids=true | all-gather | bytes 737280 | tf_op jit(solution)/shard_map/all_gather | solution.py:107
  119.0 1.4 fusion.5
  120.4 2.1 %convolution_convert_fusion.2 = bf16[128,288]{0,1:T(8,128)(2,1)} fusion(bf16[128,1152]{1,0:T(8,128)(2,1)S(1)} %fusion.5, bf16[288,1152]{1,0:T(8,128)(2,1)} %param.10), kind=kOutput, calls=%fused_computation.8 | convolution fusion | flops 84971520 | bytes 1032192 | tf_op jit(solution)/shard_map/dot_general | solution.py:118
  122.5 4.8 %all_to_all.21 = bf16[2,64,1280]{2,1,0:T(8,128)(2,1)S(1)} all-to-all(bf16[2,64,1280]{2,1,0:T(8,128)(2,1)} %bitcast.4), channel_id=1, replica_groups=mesh['z'=16,'y_lo'=4,'x'=4,'y_hi'=2,'core'=2] {'core'}, dimensions={0} | all-to-all | bytes 655360 | tf_op jit(solution)/shard_map/all_to_all | solution.py:51
  127.4 12.0 %all_gather.18 = bf16[4,64,1280]{2,1,0:T(8,128)(2,1)S(1)} all-gather(bf16[1,64,1280]{2,1,0:T(8,128)(2,1)S(1)} %fusion.14), channel_id=1, replica_groups=mesh['z'=16,'y_lo'=4,'x'=4,'y_hi'=2,'core'=2] {'y_hi','core'}, dimensions={0}, use_global_device_ids=true | all-gather | bytes 819200 | tf_op jit(solution)/shard_map/all_gather | solution.py:107
  140.4 1.8 %fusion.13 = bf16[128,1076]{0,1:T(8,128)(2,1)} fusion(f32[128,1076]{0,1:T(8,128)S(1)} %copy-done.5, bf16[1076,1152]{1,0:T(8,128)(2,1)S(1)} %copy-done, f32[128,1280]{1,0:T(8,128)S(1)} %bitcast.37, f32[128,1152]{1,0:T(8,128)S(1)} %get-tuple-element.4, f32[128]{0:T(128)S(1)} %get-tuple-element.3, f32[128]{0:T(128)S(1)} %add_rsqrt_fusion.1), kind=kOutput, calls=%fused_computation.36 | convolution fusion | flops 320817152 | bytes 4497408 | tf_op jit(solution)/shard_map/dot_general | solution.py:113
  (48 shorter events, 7.9 us)
Async XLA Ops:
  0.6 2.9 %copy-start = (bf16[1076,1152]{1,0:T(8,128)(2,1)S(1)}, bf16[1076,1152]{1,0:T(8,128)(2,1)}, u32[]{:S(2)}) copy-start(bf16[1076,1152]{1,0:T(8,128)(2,1)} %param.9) | copy-start | bytes 7437316
  3.5 1.4 %copy-start.4 = (f32[128,1076]{0,1:T(8,128)}, f32[128,1076]{0,1:T(8,128)S(1)}, u32[]{:S(2)}) copy-start(f32[128,1076]{0,1:T(8,128)S(1)} %fusion.40) | copy-start | bytes 1652740
  3.5 19.0 %copy-start.7 = (bf16[128,288]{0,1:T(8,128)(2,1)S(1)}, bf16[128,288]{0,1:T(8,128)(2,1)}, u32[]{:S(2)}) copy-start(bf16[128,288]{0,1:T(8,128)(2,1)} %param.7) | copy-start | bytes 221188
  4.9 19.8 %all-to-all-start = ((bf16[2,64,1152]{2,1,0:T(8,128)(2,1)}), bf16[2,64,1152]{2,1,0:T(8,128)(2,1)S(1)}, u32[]{:S(2)}, u32[]{:S(2)}) async-start(bf16[2,64,1152]{2,1,0:T(8,128)(2,1)} %bitcast), calls=%async_computation | async-start | bytes 589824 | tf_op jit(solution)/shard_map/all_to_all | solution.py:51
  22.5 19.7 %copy-start.3 = (bf16[128,1152]{1,0:T(8,128)(2,1)S(1)}, bf16[128,1152]{1,0:T(8,128)(2,1)}, u32[]{:S(2)}) copy-start(bf16[128,1152]{1,0:T(8,128)(2,1)} %param.6) | copy-start | bytes 884740
  24.7 0.7 copy-start.6
  25.4 31.5 %all-to-all-start.1 = ((bf16[2,64,1152]{2,1,0:T(8,128)(2,1)}), bf16[2,64,1152]{2,1,0:T(8,128)(2,1)}, u32[]{:S(2)}, u32[]{:S(2)}) async-start(bf16[2,64,1152]{2,1,0:T(8,128)(2,1)} %bitcast.38), calls=%async_computation.1 | async-start | bytes 589824 | tf_op jit(solution)/shard_map/all_to_all | solution.py:51
  43.2 41.8 %copy-start.8 = (s32[128]{0:T(128)S(1)}, s32[128]{0:T(128)}, u32[]{:S(2)}) copy-start(s32[128]{0:T(128)} %param.11) | copy-start | bytes 1540
  43.2 30.0 %collective-permute-start = (bf16[128,1152]{1,0:T(8,128)(2,1)}, bf16[128,1152]{1,0:T(8,128)(2,1)}, u32[]{:S(2)}, u32[]{:S(2)}) collective-permute-start(bf16[128,1152]{1,0:T(8,128)(2,1)} %multiply_convert_fusion.2), channel_id=1, source_target_pairs={{0,0},{1,1023},{2,1016},{3,1013},{4,4},{5,1},{6,1020},{7,1017},{8,... | collective-permute-start | bytes 884744 | tf_op jit(solution)/shard_map/ppermute | solution.py:35
  67.6 0.8 copy-start.1
  71.3 13.8 %collective-permute-start.1 = (bf16[128,1152]{1,0:T(8,128)(2,1)}, bf16[128,1152]{1,0:T(8,128)(2,1)}, u32[]{:S(2)}, u32[]{:S(2)}) collective-permute-start(bf16[128,1152]{1,0:T(8,128)(2,1)} %fusion.6), channel_id=1, source_target_pairs={{0,16},{1,17},{2,18},{3,19},{4,20},{5,21},{6,22},{7,23},{8,24},{9,... | collective-permute-start | bytes 884744 | tf_op jit(solution)/shard_map/ppermute | solution.py:35
  88.1 9.6 %collective-permute-start.3 = (bf16[128,1152]{1,0:T(8,128)(2,1)S(1)}, bf16[128,1152]{1,0:T(8,128)(2,1)S(1)}, u32[]{:S(2)}, u32[]{:S(2)}) collective-permute-start(bf16[128,1152]{1,0:T(8,128)(2,1)S(1)} %slice.157), channel_id=1, source_target_pairs={{0,1010},{1,1011},{2,1008},{3,1009},{4,1014},{5,1015},{6,1012},{7,... | collective-permute-start | bytes 884744 | tf_op jit(solution)/shard_map/ppermute | solution.py:35
  92.6 25.4 %copy-start.2 = (bf16[4,64,1152]{2,1,0:T(8,128)(2,1)S(1)}, bf16[4,64,1152]{2,1,0:T(8,128)(2,1)}, u32[]{:S(2)}) copy-start(bf16[4,64,1152]{2,1,0:T(8,128)(2,1)} %copy-done.1) | copy-start | bytes 1769476
  93.4 29.1 %collective-permute-start.2 = (bf16[128,1280]{1,0:T(8,128)(2,1)}, bf16[128,1280]{1,0:T(8,128)(2,1)}, u32[]{:S(2)}, u32[]{:S(2)}) collective-permute-start(bf16[128,1280]{1,0:T(8,128)(2,1)} %pad_maximum_fusion.3), channel_id=1, source_target_pairs={{0,0},{1,5},{2,10},{3,15},{4,4},{5,9},{6,14},{7,19},{8,8},{9,13},{... | collective-permute-start | bytes 983048 | tf_op jit(solution)/shard_map/ppermute | solution.py:35
  127.4 13.1 %copy-start.5 = (f32[128,1076]{0,1:T(8,128)S(1)}, f32[128,1076]{0,1:T(8,128)}, u32[]{:S(2)}) copy-start(f32[128,1076]{0,1:T(8,128)} %copy-done.4) | copy-start | bytes 1652740

commit v2 on v1

--- a/solution.py
+++ b/solution.py
@@ -46,33 +46,55 @@
     )
 
 
-def core_sum(term):
-    halves = term.astype(jnp.bfloat16).reshape(2, term.shape[0] // 2, term.shape[1])
-    got = lax.all_to_all(halves, "core", 0, 0).astype(jnp.float32)
-    return (got[0] + got[1]).astype(jnp.bfloat16)
+def core_halves(term, core):
+    half = term.shape[0] // 2
+    return (
+        lax.dynamic_slice_in_dim(term, core * half, half, 0),
+        lax.dynamic_slice_in_dim(term, (1 - core) * half, half, 0),
+    )
 
 
-def chip_sum(gathered):
-    both = gathered[:2].astype(jnp.float32) + gathered[2:].astype(jnp.float32)
-    return both.reshape(both.shape[0] * both.shape[1], both.shape[2])
+def reduced(image_term, text_term, core):
+    halves = [core_halves(term, core) for term in (image_term, text_term)]
+    kept = jnp.concatenate([half[0] for half in halves], 0)
+    sent = jnp.concatenate([half[1].astype(jnp.bfloat16) for half in halves], 0)
+    got = lax.ppermute(sent, "core", [(0, 1), (1, 0)])
+    chip = (kept.astype(jnp.float32) + got.astype(jnp.float32)).astype(jnp.bfloat16)
+    both = lax.all_gather(chip, "y_hi").astype(jnp.float32)
+    return both[0] + both[1]
+
+
+def core_gather(image_half, text_half):
+    half = image_half.shape[0]
+    both = lax.all_gather(jnp.concatenate([image_half, text_half], 0), "core")
+    return both[:, :half].reshape(2 * half, -1), both[:, half:].reshape(2 * half, -1)
+
+
+def split_loss(loss):
+    high = loss.astype(jnp.bfloat16)
+    low = (loss - high.astype(jnp.float32)).astype(jnp.bfloat16)
+    lanes = lax.broadcasted_iota(jnp.int32, (loss.shape[0], 128), 1)
+    return jnp.where(lanes == 0, high, jnp.where(lanes == 1, low, 0)).astype(jnp.bfloat16)
 
 
 def local(images, texts, fc_in, fc_out, head, partner):
     rows, width = images.shape
-    shift = 2 * (lax.axis_index("y_hi") ^ (lax.axis_index("z") & 1)) + lax.axis_index("core")
+    half = rows // 2
+    core = lax.axis_index("core")
+    shift = 2 * (lax.axis_index("y_hi") ^ (lax.axis_index("z") & 1)) + core
 
     text_term = jnp.dot(texts, head, preferred_element_type=jnp.float32)
     pre_act = jnp.dot(images, fc_in, preferred_element_type=jnp.float32)
     activation = jax.nn.gelu(pre_act, approximate=True).astype(jnp.bfloat16)
     image_term = jnp.dot(activation, fc_out, preferred_element_type=jnp.float32)
 
-    text_emb = chip_sum(lax.all_gather(core_sum(text_term), MP))
-    text_unit, text_inv = unit_rows(text_emb)
-    text_own = text_unit.astype(jnp.bfloat16)
+    sums = reduced(image_term, text_term, core)
+    image_emb = core_halves(images, core)[0].astype(jnp.float32) + sums[:half]
+    image_unit, image_inv = unit_rows(image_emb)
+    text_unit, text_inv = unit_rows(sums[half:])
+    image_own, text_own = core_gather(image_unit.astype(jnp.bfloat16), text_unit.astype(jnp.bfloat16))
+    scored = move(image_own, lambda role: -role)
     text_far = move(text_own, lambda role: NEAR)
-    image_emb = images.astype(jnp.float32) + chip_sum(lax.all_gather(core_sum(image_term), MP))
-    image_unit, image_inv = unit_rows(image_emb)
-    scored = move(image_unit.astype(jnp.bfloat16), lambda role: -role)
     visiting = jnp.concatenate([text_own, text_far], 0)
 
     logits = (
@@ -93,22 +115,21 @@
         pair_grad, scored, (((0,), (0,)), ((), ())), preferred_element_type=jnp.float32
     )
 
-    loss_high = loss_part.astype(jnp.bfloat16)
-    loss_low = (loss_part - loss_high.astype(jnp.float32)).astype(jnp.bfloat16)
-    lanes = lax.broadcasted_iota(jnp.int32, (rows, 128), 1)
-    loss_lanes = jnp.where(lanes == 0, loss_high, jnp.where(lanes == 1, loss_low, 0))
-    image_sent = jnp.concatenate([image_part.astype(jnp.bfloat16), loss_lanes], 1)
+    image_sent = jnp.concatenate([image_part.astype(jnp.bfloat16), split_loss(loss_part)], 1)
     image_back = move(image_sent, lambda role: role)
     text_back = move(text_part[rows:].astype(jnp.bfloat16), lambda role: -NEAR)
     text_total = text_part[:rows] + text_back.astype(jnp.float32)
 
-    image_half = core_sum(image_back.astype(jnp.float32))
-    text_half = core_sum(text_total)
-    image_sums, text_sums = lax.all_gather((image_half, text_half), MP)
-    image_all = chip_sum(image_sums)
-    loss_all = image_all[:, width] + image_all[:, width + 1]
-    image_emb_grad = tangent_rows(image_all[:, :width], image_unit, image_inv)
-    text_emb_grad = tangent_rows(chip_sum(text_sums), text_unit, text_inv)
+    sums = reduced(image_back, jnp.pad(text_total, ((0, 0), (0, 128))), core)
+    loss_half = sums[:half, width : width + 1] + sums[:half, width + 1 : width + 2]
+    image_half = tangent_rows(sums[:half, :width], image_unit, image_inv)
+    text_half = tangent_rows(sums[half:, :width], text_unit, text_inv)
+    image_emb_grad, text_emb_grad = core_gather(
+        jnp.concatenate([image_half, split_loss(loss_half)], 1),
+        jnp.pad(text_half, ((0, 0), (0, 128))),
+    )
+    loss_all = image_emb_grad[:, width : width + 2].astype(jnp.float32).sum(axis=1)
+    image_emb_grad, text_emb_grad = image_emb_grad[:, :width], text_emb_grad[:, :width]
 
     act_grad = lax.dot_general(
         image_emb_grad, fc_out, (((1,), (1,)), ((), ())), preferred_element_type=jnp.float32

time: 144 us -> 123 us (0.85); the launches traced: 142 us -> 123 us
  blocking collectives: 58 us -> 38.3 us
  waiting for transfers between devices: 11.8 us -> 22.2 us
  other arithmetic: 10.4 us -> 3.96 us
  starting transfers between devices: 44.7 us -> 40.8 us
  local copies, waits for them, and re-layouts: 1.76 us -> 5.58 us
  matrix products: 14.7 us -> 10.9 us
    all_to_all x2 -> x0, starting transfers between devices: 21.7 us -> none  [core_sum(): got = lax.all_to_all(halves, 'core', 0, 0).astype(jnp.float32)]
    ppermute x0 -> x2, starting transfers between devices: none -> 18 us  [reduced(): got = lax.ppermute(sent, 'core', [(0, 1), (1, 0)])]
    all_to_all x2 -> x0, blocking collectives: 13.3 us -> none  [core_sum(): got = lax.all_to_all(halves, 'core', 0, 0).astype(jnp.float32)]
    ppermute x4, waiting for transfers between devices: 11.8 us -> 20.4 us  [move(): return lax.ppermute(value, AXES, moves(shift))]
    all_gather x4, blocking collectives: 44.7 us -> 38.3 us  [the longest x2 32.7 us: reduced(): both = lax.all_gather(chip, 'y_hi').astype(jnp.float32)]
    convert_element_type x12 -> x7, other arithmetic: 5.01 us -> 1.54 us  [the longest x2 1.07 us: reduced(): (kept.astype(jnp.float32) + got.astype(jnp.float32)).astype(jnp.bfloat16)]
    unnamed x18 -> x22, local copies, waits for them, and re-layouts: 1.56 us -> 3.45 us
    ppermute x0 -> x2, waiting for transfers between devices: none -> 1.85 us  [reduced(): got = lax.ppermute(sent, 'core', [(0, 1), (1, 0)])]
  transfers between devices with their start and end apart: 6 -> 6, of which waited for: 1 -> 6; matrix products, arithmetic and copies ran while one was open for 11% -> 2% of each run, Pallas kernels for 0% -> 0%
where the time goes in v2:
time: 123 us
  starting transfers between devices  40.8 us (33%)
  blocking collectives  38.3 us (31%)
  waiting for transfers between devices  22.2 us (18%)
  matrix products  10.9 us (9%)
  local copies, waits for them, and re-layouts  5.58 us (5%)
  other arithmetic  3.96 us (3%)
    all_gather x2, blocking collectives, reduced(): both = lax.all_gather(chip, 'y_hi').astype(jnp.float32)  32.7 us
    ppermute x4, starting transfers between devices, move(): return lax.ppermute(value, AXES, moves(shift))  22.8 us
    ppermute x4, waiting for transfers between devices, move(): return lax.ppermute(value, AXES, moves(shift))  20.4 us
    ppermute x2, starting transfers between devices, reduced(): got = lax.ppermute(sent, 'core', [(0, 1), (1, 0)])  18 us
    all_gather x2, blocking collectives, core_gather(): both = lax.all_gather(jnp.concatenate([image_half, text_half], 0), 'core')  5.55 us
    unnamed x22, local copies, waits for them, and re-layouts  3.45 us
    dot_general x1, matrix products, local(): pre_act = jnp.dot(images, fc_in, preferred_element_type=jnp.float32)  2.83 us
  transfers between devices with their start and end apart: 6, of which 6 were waited for; matrix products, arithmetic and copies ran while one was open for 2% of the time, Pallas kernels for 0%

profile of v2, /device:TPU:1, one launch (start us, length us, event | category | flops | bytes accessed | tf_op | source)
XLA Modules:
  0.0 122.7 jit_solution(3455826707961845350)
XLA Ops:
  0.7 2.8 %fusion.47 = f32[128,1076]{0,1:T(8,128)S(1)} fusion(bf16[128,1152]{1,0:T(8,128)(2,1)} %param.6, bf16[1152,1076]{0,1:T(8,128)(2,1)} %param.8), kind=kOutput, calls=%fused_computation.94 | convolution fusion | flops 317325312 | bytes 3324928 | tf_op jit(solution)/shard_map/dot_general | solution.py:87
  7.2 16.0 %collective-permute-start = (bf16[128,1152]{1,0:T(8,128)(2,1)}, bf16[128,1152]{1,0:T(8,128)(2,1)S(1)}, u32[]{:S(2)}, u32[]{:S(2)}) collective-permute-start(bf16[128,1152]{1,0:T(8,128)(2,1)} %pad_maximum_fusion.5), channel_id=1, source_target_pairs={{0,1},{1,0},{2,3},{3,2},{4,5},{5,4},{6,7},{7,6},{8,9},{9,8},{10,11... | collective-permute-start | bytes 884744 | tf_op jit(solution)/shard_map/ppermute | solution.py:61
  23.2 1.1 constant_dynamic-slice_fusion.1
  25.3 1.0 fusion.6
  26.4 12.8 %all-gather = bf16[256,1152]{1,0:T(8,128)(2,1)S(1)} all-gather(bf16[128,1152]{1,0:T(8,128)(2,1)S(1)} %fusion.6), channel_id=2, replica_groups=mesh['z'=16,'y_lo'=4,'x'=4,'y_hi'=2,'core'=2] {'y_hi'}, dimensions={0}, use_global_device_ids=true | all-gather | bytes 884736 | tf_op jit(solution)/shard_map/all_gather | solution.py:63
  39.3 0.9 copy-done.1
  40.5 3.1 %all-gather.1 = bf16[256,1152]{1,0:T(8,128)(2,1)S(1)} all-gather(bf16[128,1152]{1,0:T(8,128)(2,1)S(1)} %pad_maximum_fusion.6), channel_id=3, replica_groups=mesh['z'=16,'y_lo'=4,'x'=4,'y_hi'=2,'core'=2] {'core'}, dimensions={0}, use_global_device_ids=true | all-gather | bytes 884736 | tf_op jit(solution)/shard_map/all_gather | solution.py:69
  44.5 16.8 %collective-permute-start.1 = (bf16[128,1152]{1,0:T(8,128)(2,1)}, bf16[128,1152]{1,0:T(8,128)(2,1)}, u32[]{:S(2)}, u32[]{:S(2)}) collective-permute-start(bf16[128,1152]{1,0:T(8,128)(2,1)} %bitcast.4), channel_id=1, source_target_pairs={{0,0},{1,1023},{2,1016},{3,1013},{4,4},{5,1},{6,1020},{7,1017},{8,... | collective-permute-start | bytes 884744 | tf_op jit(solution)/shard_map/ppermute | solution.py:35
  61.2 1.9 %collective-permute-start.2 = (bf16[128,1152]{1,0:T(8,128)(2,1)}, bf16[128,1152]{1,0:T(8,128)(2,1)}, u32[]{:S(2)}, u32[]{:S(2)}) collective-permute-start(bf16[128,1152]{1,0:T(8,128)(2,1)} %bitcast.5), channel_id=1, source_target_pairs={{0,16},{1,17},{2,18},{3,19},{4,20},{5,21},{6,22},{7,23},{8,24},{9,... | collective-permute-start | bytes 884744 | tf_op jit(solution)/shard_map/ppermute | solution.py:35
  63.2 2.0 %collective-permute-done.1 = bf16[128,1152]{1,0:T(8,128)(2,1)} collective-permute-done((bf16[128,1152]{1,0:T(8,128)(2,1)}, bf16[128,1152]{1,0:T(8,128)(2,1)}, u32[]{:S(2)}, u32[]{:S(2)}) %collective-permute-start.1) | collective-permute-done | bytes 294944 | tf_op jit(solution)/shard_map/ppermute | solution.py:35
  65.2 7.1 %collective-permute-done.2 = bf16[128,1152]{1,0:T(8,128)(2,1)} collective-permute-done((bf16[128,1152]{1,0:T(8,128)(2,1)}, bf16[128,1152]{1,0:T(8,128)(2,1)}, u32[]{:S(2)}, u32[]{:S(2)}) %collective-permute-start.2) | collective-permute-done | bytes 294944 | tf_op jit(solution)/shard_map/ppermute | solution.py:35
  72.3 1.6 %fusion.31 = (f32[128]{0:T(128)S(1)}, f32[128,256]{1,0:T(8,128)S(1)}) fusion(bf16[128,1152]{1,0:T(8,128)(2,1)} %collective-permute-done.1, bf16[128,1152]{1,0:T(8,128)(2,1)} %collective-permute-done.2, bf16[128,1152]{1,0:T(8,128)(2,1)} %bitcast.5, pred[]{:T(512)S(6)} %eq.37, s32[128]{0:T(128)S(1)} %copy-done.10), kind=kOutput, calls=%fused_computation.65 | convolution fusion | flops 77135744 | bytes 1016833 | tf_op jit(solution)/shard_map/dot_general | solution.py:102
  74.0 1.4 %convolution_multiply_fusion = f32[256,1152]{1,0:T(8,128)S(1)} fusion(bf16[128,1152]{1,0:T(8,128)(2,1)} %collective-permute-done.1, f32[128,256]{1,0:T(8,128)S(1)} %get-tuple-element.22, s32[128]{0:T(128)S(1)} %copy-done.10, pred[]{:T(512)S(6)} %eq.37), kind=kOutput, calls=%fused_computation | convolution fusion | flops 76087296 | bytes 1606145 | tf_op jit(solution)/shard_map/dot_general | solution.py:114
  75.4 2.2 %collective-permute-start.4 = (bf16[128,1152]{1,0:T(8,128)(2,1)S(1)}, bf16[128,1152]{1,0:T(8,128)(2,1)S(1)}, u32[]{:S(2)}, u32[]{:S(2)}) collective-permute-start(bf16[128,1152]{1,0:T(8,128)(2,1)S(1)} %slice.159), channel_id=1, source_target_pairs={{0,1010},{1,1011},{2,1008},{3,1009},{4,1014},{5,1015},{6,1012},{7,... | collective-permute-start | bytes 884744 | tf_op jit(solution)/shard_map/ppermute | solution.py:35
  77.7 1.4 %fusion = bf16[128,1152]{1,0:T(8,128)(2,1)S(1)} fusion(bf16[128,1152]{1,0:T(8,128)(2,1)} %collective-permute-done.2, bf16[128,1152]{1,0:T(8,128)(2,1)} %bitcast.5, f32[128,256]{1,0:T(8,128)S(1)} %get-tuple-element.22, s32[128]{0:T(128)S(1)} %copy-done.10, pred[]{:T(512)S(6)} %eq.37), kind=kOutput, calls=%fused_computation.2 | convolution fusion | flops 77266944 | bytes 1016321 | tf_op jit(solution)/shard_map/dot_general | solution.py:113
  79.2 1.9 %collective-permute-start.3 = (bf16[128,1280]{1,0:T(8,128)(2,1)S(1)}, bf16[128,1280]{1,0:T(8,128)(2,1)S(1)}, u32[]{:S(2)}, u32[]{:S(2)}) collective-permute-start(bf16[128,1280]{1,0:T(8,128)(2,1)S(1)} %pad_maximum_fusion.3), channel_id=1, source_target_pairs={{0,0},{1,5},{2,10},{3,15},{4,4},{5,9},{6,14},{7,19},{8,8},{9,13},{... | collective-permute-start | bytes 983048 | tf_op jit(solution)/shard_map/ppermute | solution.py:35
  81.1 2.5 %collective-permute-done.4 = bf16[128,1152]{1,0:T(8,128)(2,1)S(1)} collective-permute-done((bf16[128,1152]{1,0:T(8,128)(2,1)S(1)}, bf16[128,1152]{1,0:T(8,128)(2,1)S(1)}, u32[]{:S(2)}, u32[]{:S(2)}) %collective-permute-start.4) | collective-permute-done | bytes 294944 | tf_op jit(solution)/shard_map/ppermute | solution.py:35
  83.7 8.7 %collective-permute-done.3 = bf16[128,1280]{1,0:T(8,128)(2,1)S(1)} collective-permute-done((bf16[128,1280]{1,0:T(8,128)(2,1)S(1)}, bf16[128,1280]{1,0:T(8,128)(2,1)S(1)}, u32[]{:S(2)}, u32[]{:S(2)}) %collective-permute-start.3) | collective-permute-done | bytes 327712 | tf_op jit(solution)/shard_map/ppermute | solution.py:35
  92.5 1.9 %collective-permute-start.5 = (bf16[128,1280]{1,0:T(8,128)(2,1)S(1)}, bf16[128,1280]{1,0:T(8,128)(2,1)S(1)}, u32[]{:S(2)}, u32[]{:S(2)}) collective-permute-start(bf16[128,1280]{1,0:T(8,128)(2,1)S(1)} %pad_maximum_fusion.4), channel_id=1, source_target_pairs={{0,1},{1,0},{2,3},{3,2},{4,5},{5,4},{6,7},{7,6},{8,9},{9,8},{10,11... | collective-permute-start | bytes 983048 | tf_op jit(solution)/shard_map/ppermute | solution.py:61
  94.5 1.6 %collective-permute-done.5 = bf16[128,1280]{1,0:T(8,128)(2,1)S(1)} collective-permute-done((bf16[128,1280]{1,0:T(8,128)(2,1)S(1)}, bf16[128,1280]{1,0:T(8,128)(2,1)S(1)}, u32[]{:S(2)}, u32[]{:S(2)}) %collective-permute-start.5) | collective-permute-done | bytes 327712 | tf_op jit(solution)/shard_map/ppermute | solution.py:61
  96.1 19.9 %all-gather.2 = bf16[256,1280]{1,0:T(8,128)(2,1)S(1)} all-gather(bf16[128,1280]{1,0:T(8,128)(2,1)S(1)} %fusion.3), channel_id=4, replica_groups=mesh['z'=16,'y_lo'=4,'x'=4,'y_hi'=2,'core'=2] {'y_hi'}, dimensions={0}, use_global_device_ids=true | all-gather | bytes 983040 | tf_op jit(solution)/shard_map/all_gather | solution.py:63
  116.9 2.5 %all-gather.3 = bf16[256,1280]{1,0:T(8,128)(2,1)S(1)} all-gather(bf16[128,1280]{1,0:T(8,128)(2,1)S(1)} %fusion.15), channel_id=5, replica_groups=mesh['z'=16,'y_lo'=4,'x'=4,'y_hi'=2,'core'=2] {'core'}, dimensions={0}, use_global_device_ids=true | all-gather | bytes 983040 | tf_op jit(solution)/shard_map/all_gather | solution.py:69
  119.4 1.7 %fusion.13 = bf16[128,1076]{0,1:T(8,128)(2,1)} fusion(f32[128,1076]{0,1:T(8,128)S(1)} %copy-done.5, bf16[1076,1152]{1,0:T(8,128)(2,1)S(1)} %copy-done, bf16[128,1280]{1,0:T(8,128)(2,1)S(1)} %bitcast.44), kind=kOutput, calls=%fused_computation.29 | convolution fusion | flops 320079872 | bytes 3611648 | tf_op jit(solution)/shard_map/dot_general | solution.py:134
  121.8 1.0 convolution_convert_fusion
  (55 shorter events, 7.9 us)
Async XLA Ops:
  0.6 2.9 %copy-start = (bf16[1076,1152]{1,0:T(8,128)(2,1)S(1)}, bf16[1076,1152]{1,0:T(8,128)(2,1)}, u32[]{:S(2)}) copy-start(bf16[1076,1152]{1,0:T(8,128)(2,1)} %param.9) | copy-start | bytes 7437316
  3.5 0.8 copy-start.4
  3.5 1.3 %copy-start.2 = (bf16[288,1152]{1,0:T(8,128)(2,1)S(1)}, bf16[288,1152]{1,0:T(8,128)(2,1)}, u32[]{:S(2)}) copy-start(bf16[288,1152]{1,0:T(8,128)(2,1)} %param.10) | copy-start | bytes 1990660
  3.5 1.3 %copy-start.9 = (bf16[128,288]{0,1:T(8,128)(2,1)S(1)}, bf16[128,288]{0,1:T(8,128)(2,1)}, u32[]{:S(2)}) copy-start(bf16[128,288]{0,1:T(8,128)(2,1)} %param.7) | copy-start | bytes 221188
  4.8 0.8 copy-start.6
  5.6 0.8 copy-start.7
  7.2 17.4 %collective-permute-start = (bf16[128,1152]{1,0:T(8,128)(2,1)}, bf16[128,1152]{1,0:T(8,128)(2,1)S(1)}, u32[]{:S(2)}, u32[]{:S(2)}) collective-permute-start(bf16[128,1152]{1,0:T(8,128)(2,1)} %pad_maximum_fusion.5), channel_id=1, source_target_pairs={{0,1},{1,0},{2,3},{3,2},{4,5},{5,4},{6,7},{7,6},{8,9},{9,8},{10,11... | collective-permute-start | bytes 884744 | tf_op jit(solution)/shard_map/ppermute | solution.py:61
  24.6 0.7 copy-start.8
  39.2 1.0 copy-start.1
  40.5 31.8 %copy-start.10 = (s32[128]{0:T(128)S(1)}, s32[128]{0:T(128)}, u32[]{:S(2)}) copy-start(s32[128]{0:T(128)} %param.11) | copy-start | bytes 1540
  44.5 20.7 %collective-permute-start.1 = (bf16[128,1152]{1,0:T(8,128)(2,1)}, bf16[128,1152]{1,0:T(8,128)(2,1)}, u32[]{:S(2)}, u32[]{:S(2)}) collective-permute-start(bf16[128,1152]{1,0:T(8,128)(2,1)} %bitcast.4), channel_id=1, source_target_pairs={{0,0},{1,1023},{2,1016},{3,1013},{4,4},{5,1},{6,1020},{7,1017},{8,... | collective-permute-start | bytes 884744 | tf_op jit(solution)/shard_map/ppermute | solution.py:35
  61.2 11.1 %collective-permute-start.2 = (bf16[128,1152]{1,0:T(8,128)(2,1)}, bf16[128,1152]{1,0:T(8,128)(2,1)}, u32[]{:S(2)}, u32[]{:S(2)}) collective-permute-start(bf16[128,1152]{1,0:T(8,128)(2,1)} %bitcast.5), channel_id=1, source_target_pairs={{0,16},{1,17},{2,18},{3,19},{4,20},{5,21},{6,22},{7,23},{8,24},{9,... | collective-permute-start | bytes 884744 | tf_op jit(solution)/shard_map/ppermute | solution.py:35
  75.4 8.2 %collective-permute-start.4 = (bf16[128,1152]{1,0:T(8,128)(2,1)S(1)}, bf16[128,1152]{1,0:T(8,128)(2,1)S(1)}, u32[]{:S(2)}, u32[]{:S(2)}) collective-permute-start(bf16[128,1152]{1,0:T(8,128)(2,1)S(1)} %slice.159), channel_id=1, source_target_pairs={{0,1010},{1,1011},{2,1008},{3,1009},{4,1014},{5,1015},{6,1012},{7,... | collective-permute-start | bytes 884744 | tf_op jit(solution)/shard_map/ppermute | solution.py:35
  79.2 13.2 %collective-permute-start.3 = (bf16[128,1280]{1,0:T(8,128)(2,1)S(1)}, bf16[128,1280]{1,0:T(8,128)(2,1)S(1)}, u32[]{:S(2)}, u32[]{:S(2)}) collective-permute-start(bf16[128,1280]{1,0:T(8,128)(2,1)S(1)} %pad_maximum_fusion.3), channel_id=1, source_target_pairs={{0,0},{1,5},{2,10},{3,15},{4,4},{5,9},{6,14},{7,19},{8,8},{9,13},{... | collective-permute-start | bytes 983048 | tf_op jit(solution)/shard_map/ppermute | solution.py:35
  92.5 3.5 %collective-permute-start.5 = (bf16[128,1280]{1,0:T(8,128)(2,1)S(1)}, bf16[128,1280]{1,0:T(8,128)(2,1)S(1)}, u32[]{:S(2)}, u32[]{:S(2)}) collective-permute-start(bf16[128,1280]{1,0:T(8,128)(2,1)S(1)} %pad_maximum_fusion.4), channel_id=1, source_target_pairs={{0,1},{1,0},{2,3},{3,2},{4,5},{5,4},{6,7},{7,6},{8,9},{9,8},{10,11... | collective-permute-start | bytes 983048 | tf_op jit(solution)/shard_map/ppermute | solution.py:61
  116.8 2.6 %copy-start.5 = (f32[128,1076]{0,1:T(8,128)S(1)}, f32[128,1076]{0,1:T(8,128)}, u32[]{:S(2)}) copy-start(f32[128,1076]{0,1:T(8,128)} %copy-done.4) | copy-start | bytes 1652740
  119.4 2.3 %copy-start.3 = (bf16[288,1152]{1,0:T(8,128)(2,1)S(1)}, bf16[288,1152]{1,0:T(8,128)(2,1)}, u32[]{:S(2)}) copy-start(bf16[288,1152]{1,0:T(8,128)(2,1)} %param.10) | copy-start | bytes 1990660

commit v3 on v2

--- a/solution.py
+++ b/solution.py
@@ -15,6 +15,7 @@
 SIZES = (16, 4, 4, 2, 2)
 MP = ("y_hi", "core")
 NEAR = 4
+OFFSET = (0, 3, 1, 2)
 
 
 def place(block, role):
@@ -77,11 +78,26 @@
     return jnp.where(lanes == 0, high, jnp.where(lanes == 1, low, 0)).astype(jnp.bfloat16)
 
 
+def scored(own, others, positive):
+    logits = (
+        logit_scale
+        * lax.dot_general(
+            own, others, (((1,), (1,)), ((), ())), preferred_element_type=jnp.float32
+        )
+        + logit_bias
+    )
+    label_sign = jnp.where(positive, 1.0, -1.0).astype(jnp.float32)
+    flipped = -label_sign * logits
+    loss = jnp.sum(jax.nn.softplus(flipped), axis=1, keepdims=True)
+    pair_grad = (-loss_scale * label_sign * jax.nn.sigmoid(flipped)).astype(jnp.bfloat16)
+    return logit_scale * jnp.dot(pair_grad, others, preferred_element_type=jnp.float32), loss
+
+
 def local(images, texts, fc_in, fc_out, head, partner):
     rows, width = images.shape
     half = rows // 2
     core = lax.axis_index("core")
-    shift = 2 * (lax.axis_index("y_hi") ^ (lax.axis_index("z") & 1)) + core
+    role = 2 * (lax.axis_index("y_hi") ^ (lax.axis_index("z") & 1)) + core
 
     text_term = jnp.dot(texts, head, preferred_element_type=jnp.float32)
     pre_act = jnp.dot(images, fc_in, preferred_element_type=jnp.float32)
@@ -93,34 +109,26 @@
     image_unit, image_inv = unit_rows(image_emb)
     text_unit, text_inv = unit_rows(sums[half:])
     image_own, text_own = core_gather(image_unit.astype(jnp.bfloat16), text_unit.astype(jnp.bfloat16))
-    scored = move(image_own, lambda role: -role)
-    text_far = move(text_own, lambda role: NEAR)
-    visiting = jnp.concatenate([text_own, text_far], 0)
-
-    logits = (
-        logit_scale
-        * lax.dot_general(
-            scored, visiting, (((1,), (1,)), ((), ())), preferred_element_type=jnp.float32
-        )
-        + logit_bias
+    visits = (
+        move(text_own, lambda role: OFFSET[role] + NEAR),
+        move(image_own, lambda role: -OFFSET[role] - NEAR),
+        move(text_own, lambda role: OFFSET[role]),
+        move(image_own, lambda role: -OFFSET[role]),
     )
-    columns = lax.broadcasted_iota(jnp.int32, logits.shape, 1)
-    positive = (columns == partner[:, None]) & (shift == 0)
-    label_sign = jnp.where(positive, 1.0, -1.0).astype(jnp.float32)
-    flipped = -label_sign * logits
-    loss_part = jnp.sum(jax.nn.softplus(flipped), axis=1, keepdims=True)
-    pair_grad = (-loss_scale * label_sign * jax.nn.sigmoid(flipped)).astype(jnp.bfloat16)
-    image_part = logit_scale * jnp.dot(pair_grad, visiting, preferred_element_type=jnp.float32)
-    text_part = logit_scale * lax.dot_general(
-        pair_grad, scored, (((0,), (0,)), ((), ())), preferred_element_type=jnp.float32
+    paired = jnp.where(role == 0, partner, -1)
+    columns = lax.broadcasted_iota(jnp.int32, (rows, 2 * rows), 1)
+    on_row = lax.broadcasted_iota(jnp.int32, (rows, 2 * rows), 0)
+    image_part, loss_part = scored(
+        image_own, jnp.concatenate([visits[2], visits[0]], 0), columns == paired[:, None]
+    )
+    text_part, unused = scored(
+        text_own,
+        jnp.concatenate([visits[3], visits[1]], 0),
+        on_row == jnp.pad(paired, (0, rows), constant_values=-1)[None, :],
     )
 
-    image_sent = jnp.concatenate([image_part.astype(jnp.bfloat16), split_loss(loss_part)], 1)
-    image_back = move(image_sent, lambda role: role)
-    text_back = move(text_part[rows:].astype(jnp.bfloat16), lambda role: -NEAR)
-    text_total = text_part[:rows] + text_back.astype(jnp.float32)
-
-    sums = reduced(image_back, jnp.pad(text_total, ((0, 0), (0, 128))), core)
+    image_part = jnp.concatenate([image_part, split_loss(loss_part).astype(jnp.float32)], 1)
+    sums = reduced(image_part, jnp.pad(text_part, ((0, 0), (0, 128))), core)
     loss_half = sums[:half, width : width + 1] + sums[:half, width + 1 : width + 2]
     image_half = tangent_rows(sums[:half, :width], image_unit, image_inv)
     text_half = tangent_rows(sums[half:, :width], text_unit, text_inv)

time: 123 us -> 119 us (0.967)
  waiting for transfers between devices: 22.2 us -> 10.1 us
  blocking collectives: 38.3 us -> 42.1 us
  local copies, waits for them, and re-layouts: 5.58 us -> 7.79 us
  starting transfers between devices: 40.8 us -> 42.8 us
    ppermute x4, waiting for transfers between devices: 20.4 us -> 8.26 us  [move(): return lax.ppermute(value, AXES, moves(shift))]
    all_gather x2, blocking collectives: 32.7 us -> 36.3 us  [reduced(): both = lax.all_gather(chip, 'y_hi').astype(jnp.float32)]
    ppermute x4, starting transfers between devices: 22.8 us -> 24.8 us  [move(): return lax.ppermute(value, AXES, moves(shift))]
    concatenate x0 -> x2, local copies, waits for them, and re-layouts: none -> 1.79 us  [the longest x1 1.05 us: local(): jnp.concatenate([visits[2], visits[0]], 0)]
    unnamed x22 -> x24, local copies, waits for them, and re-layouts: 3.45 us -> 3.09 us
  transfers between devices with their start and end apart: 6 -> 6, of which waited for: 6 -> 4; matrix products, arithmetic and copies ran while one was open for 2% -> 6% of each run, Pallas kernels for 0% -> 0%
where the time goes in v3:
time: 119 us; the launch traced here: 118 us
  starting transfers between devices  42.8 us (36%)
  blocking collectives  42.1 us (35%)
  matrix products  11.1 us (9%)
  waiting for transfers between devices  10.1 us (8%)
  local copies, waits for them, and re-layouts  7.79 us (7%)
  other arithmetic  3.22 us (3%)
    all_gather x2, blocking collectives, reduced(): both = lax.all_gather(chip, 'y_hi').astype(jnp.float32)  36.3 us
    ppermute x4, starting transfers between devices, move(): return lax.ppermute(value, AXES, moves(shift))  24.8 us
    ppermute x2, starting transfers between devices, reduced(): got = lax.ppermute(sent, 'core', [(0, 1), (1, 0)])  18 us
    ppermute x4, waiting for transfers between devices, move(): return lax.ppermute(value, AXES, moves(shift))  8.26 us
    all_gather x2, blocking collectives, core_gather(): both = lax.all_gather(jnp.concatenate([image_half, text_half], 0), 'core')  5.84 us
    dot_general x2, matrix products, scored(): jnp.dot(pair_grad, others, preferred_element_type=jnp.float32)  3.15 us
    unnamed x24, local copies, waits for them, and re-layouts  3.09 us
    dot_general x1, matrix products, local(): pre_act = jnp.dot(images, fc_in, preferred_element_type=jnp.float32)  2.83 us
  transfers between devices with their start and end apart: 6, of which 4 were waited for; matrix products, arithmetic and copies ran while one was open for 6% of the time, Pallas kernels for 0%

profile of v3, /device:TPU:1, one launch (start us, length us, event | category | flops | bytes accessed | tf_op | source)
XLA Modules:
  0.0 118.1 jit_solution(2022569660074094317)
XLA Ops:
  0.7 2.8 %fusion.71 = f32[128,1076]{0,1:T(8,128)S(1)} fusion(bf16[128,1152]{1,0:T(8,128)(2,1)} %param.6, bf16[1152,1076]{0,1:T(8,128)(2,1)} %param.8), kind=kOutput, calls=%fused_computation.126 | convolution fusion | flops 317325312 | bytes 3324928 | tf_op jit(solution)/shard_map/dot_general | solution.py:103
  6.0 16.1 %collective-permute-start = (bf16[128,1152]{1,0:T(8,128)(2,1)S(1)}, bf16[128,1152]{1,0:T(8,128)(2,1)}, u32[]{:S(2)}, u32[]{:S(2)}) collective-permute-start(bf16[128,1152]{1,0:T(8,128)(2,1)S(1)} %pad_maximum_fusion.1), channel_id=1, source_target_pairs={{0,1},{1,0},{2,3},{3,2},{4,5},{5,4},{6,7},{7,6},{8,9},{9,8},{10,11... | collective-permute-start | bytes 884744 | tf_op jit(solution)/shard_map/ppermute | solution.py:62
  22.1 1.0 constant_dynamic-slice_fusion
  23.4 1.0 fusion.13
  24.4 12.9 %all-gather = bf16[256,1152]{1,0:T(8,128)(2,1)S(1)} all-gather(bf16[128,1152]{1,0:T(8,128)(2,1)S(1)} %fusion.13), channel_id=2, replica_groups=mesh['z'=16,'y_lo'=4,'x'=4,'y_hi'=2,'core'=2] {'y_hi'}, dimensions={0}, use_global_device_ids=true | all-gather | bytes 884736 | tf_op jit(solution)/shard_map/all_gather | solution.py:64
  37.9 3.1 %all-gather.1 = bf16[256,1152]{1,0:T(8,128)(2,1)S(1)} all-gather(bf16[128,1152]{1,0:T(8,128)(2,1)S(1)} %pad_maximum_fusion.2), channel_id=3, replica_groups=mesh['z'=16,'y_lo'=4,'x'=4,'y_hi'=2,'core'=2] {'core'}, dimensions={0}, use_global_device_ids=true | all-gather | bytes 884736 | tf_op jit(solution)/shard_map/all_gather | solution.py:70
  40.9 0.8 fusion.69
  41.7 15.5 %collective-permute-start.3 = (bf16[128,1152]{1,0:T(8,128)(2,1)S(1)}, bf16[128,1152]{1,0:T(8,128)(2,1)S(1)}, u32[]{:S(2)}, u32[]{:S(2)}) collective-permute-start(bf16[128,1152]{1,0:T(8,128)(2,1)S(1)} %bitcast.50), channel_id=1, source_target_pairs={{0,0},{1,1015},{2,1020},{3,1017},{4,4},{5,1019},{6,2},{7,1021},{8,... | collective-permute-start | bytes 884744 | tf_op jit(solution)/shard_map/ppermute | solution.py:36
  57.2 3.8 %collective-permute-start.4 = (bf16[128,1152]{1,0:T(8,128)(2,1)S(1)}, bf16[128,1152]{1,0:T(8,128)(2,1)S(1)}, u32[]{:S(2)}, u32[]{:S(2)}) collective-permute-start(bf16[128,1152]{1,0:T(8,128)(2,1)S(1)} %bitcast.51), channel_id=1, source_target_pairs={{0,1010},{1,999},{2,1004},{3,1001},{4,1014},{5,1003},{6,1008},{7,1... | collective-permute-start | bytes 884744 | tf_op jit(solution)/shard_map/ppermute | solution.py:36
  61.1 3.6 %collective-permute-start.2 = (bf16[128,1152]{1,0:T(8,128)(2,1)}, bf16[128,1152]{1,0:T(8,128)(2,1)}, u32[]{:S(2)}, u32[]{:S(2)}) collective-permute-start(bf16[128,1152]{1,0:T(8,128)(2,1)} %bitcast.5), channel_id=1, source_target_pairs={{0,16},{1,29},{2,22},{3,27},{4,20},{5,33},{6,26},{7,31},{8,24},{9,... | collective-permute-start | bytes 884744 | tf_op jit(solution)/shard_map/ppermute | solution.py:36
  64.7 1.9 %collective-permute-start.1 = (bf16[128,1152]{1,0:T(8,128)(2,1)}, bf16[128,1152]{1,0:T(8,128)(2,1)}, u32[]{:S(2)}, u32[]{:S(2)}) collective-permute-start(bf16[128,1152]{1,0:T(8,128)(2,1)} %bitcast.5), channel_id=1, source_target_pairs={{0,0},{1,13},{2,6},{3,11},{4,4},{5,17},{6,10},{7,15},{8,8},{9,21},... | collective-permute-start | bytes 884744 | tf_op jit(solution)/shard_map/ppermute | solution.py:36
  67.3 1.9 %collective-permute-done.4 = bf16[128,1152]{1,0:T(8,128)(2,1)S(1)} collective-permute-done((bf16[128,1152]{1,0:T(8,128)(2,1)S(1)}, bf16[128,1152]{1,0:T(8,128)(2,1)S(1)}, u32[]{:S(2)}, u32[]{:S(2)}) %collective-permute-start.4) | collective-permute-done | bytes 294944 | tf_op jit(solution)/shard_map/ppermute | solution.py:36
  70.0 2.9 %convolution_multiply_fusion = f32[128,1152]{1,0:T(8,128)} fusion(bf16[256,1152]{1,0:T(8,128)(2,1)} %constant_dynamic-update-slice_fusion.2, bf16[128,1152]{1,0:T(8,128)(2,1)} %bitcast.5, s32[256]{0:T(256)S(1)} %pad.12), kind=kOutput, calls=%fused_computation | convolution fusion | flops 151535616 | bytes 1475584 | tf_op jit(solution)/shard_map/dot_general | solution.py:93
  72.9 1.0 fusion.21
  73.9 6.3 %collective-permute-done.1 = bf16[128,1152]{1,0:T(8,128)(2,1)} collective-permute-done((bf16[128,1152]{1,0:T(8,128)(2,1)}, bf16[128,1152]{1,0:T(8,128)(2,1)}, u32[]{:S(2)}, u32[]{:S(2)}) %collective-permute-start.1) | collective-permute-done | bytes 294944 | tf_op jit(solution)/shard_map/ppermute | solution.py:36
  80.2 1.0 constant_dynamic-update-slice_fusion.1
  81.2 1.1 constant_dynamic-update-slice_fusion
  82.2 1.4 %fusion.41 = (f32[128]{0:T(128)S(1)}, f32[128,256]{1,0:T(8,128)S(1)}) fusion(bf16[128,1152]{1,0:T(8,128)(2,1)} %bitcast.52, bf16[256,1152]{1,0:T(8,128)(2,1)S(1)} %constant_dynamic-update-slice_fusion, s32[128]{0:T(128)S(1)} %broadcast_select_fusion), kind=kOutput, calls=%fused_computation.77 | convolution fusion | flops 75923328 | bytes 1016832 | tf_op jit(solution)/shard_map/dot_general | solution.py:84
  84.2 1.9 %collective-permute-start.5 = (bf16[128,1280]{1,0:T(8,128)(2,1)S(1)}, bf16[128,1280]{1,0:T(8,128)(2,1)S(1)}, u32[]{:S(2)}, u32[]{:S(2)}) collective-permute-start(bf16[128,1280]{1,0:T(8,128)(2,1)S(1)} %pad_maximum_fusion), channel_id=1, source_target_pairs={{0,1},{1,0},{2,3},{3,2},{4,5},{5,4},{6,7},{7,6},{8,9},{9,8},{10,11... | collective-permute-start | bytes 983048 | tf_op jit(solution)/shard_map/ppermute | solution.py:62
  86.2 1.5 %collective-permute-done.5 = bf16[128,1280]{1,0:T(8,128)(2,1)S(1)} collective-permute-done((bf16[128,1280]{1,0:T(8,128)(2,1)S(1)}, bf16[128,1280]{1,0:T(8,128)(2,1)S(1)}, u32[]{:S(2)}, u32[]{:S(2)}) %collective-permute-start.5) | collective-permute-done | bytes 327712 | tf_op jit(solution)/shard_map/ppermute | solution.py:62
  87.8 23.3 %all-gather.2 = bf16[256,1280]{1,0:T(8,128)(2,1)S(1)} all-gather(bf16[128,1280]{1,0:T(8,128)(2,1)S(1)} %fusion.10), channel_id=4, replica_groups=mesh['z'=16,'y_lo'=4,'x'=4,'y_hi'=2,'core'=2] {'y_hi'}, dimensions={0}, use_global_device_ids=true | all-gather | bytes 983040 | tf_op jit(solution)/shard_map/all_gather | solution.py:64
  112.0 2.8 %all-gather.3 = bf16[256,1280]{1,0:T(8,128)(2,1)S(1)} all-gather(bf16[128,1280]{1,0:T(8,128)(2,1)S(1)} %fusion.25), channel_id=5, replica_groups=mesh['z'=16,'y_lo'=4,'x'=4,'y_hi'=2,'core'=2] {'core'}, dimensions={0}, use_global_device_ids=true | all-gather | bytes 983040 | tf_op jit(solution)/shard_map/all_gather | solution.py:70
  114.8 1.7 %fusion.20 = bf16[128,1076]{0,1:T(8,128)(2,1)} fusion(f32[128,1076]{0,1:T(8,128)S(1)} %copy-done.6, bf16[1076,1152]{1,0:T(8,128)(2,1)S(1)} %copy-done, bf16[128,1280]{1,0:T(8,128)(2,1)S(1)} %bitcast.48), kind=kOutput, calls=%fused_computation.38 | convolution fusion | flops 320079872 | bytes 3611648 | tf_op jit(solution)/shard_map/dot_general | solution.py:142
  117.2 1.0 convolution_convert_fusion
  (59 shorter events, 6.8 us)
Async XLA Ops:
  0.6 2.9 %copy-start = (bf16[1076,1152]{1,0:T(8,128)(2,1)S(1)}, bf16[1076,1152]{1,0:T(8,128)(2,1)}, u32[]{:S(2)}) copy-start(bf16[1076,1152]{1,0:T(8,128)(2,1)} %param.9) | copy-start | bytes 7437316
  3.5 1.7 %copy-start.5 = (f32[128,1076]{0,1:T(8,128)}, f32[128,1076]{0,1:T(8,128)S(1)}, u32[]{:S(2)}) copy-start(f32[128,1076]{0,1:T(8,128)S(1)} %fusion.71) | copy-start | bytes 1652740
  3.5 1.3 %copy-start.2 = (bf16[288,1152]{1,0:T(8,128)(2,1)S(1)}, bf16[288,1152]{1,0:T(8,128)(2,1)}, u32[]{:S(2)}) copy-start(bf16[288,1152]{1,0:T(8,128)(2,1)} %param.10) | copy-start | bytes 1990660
  3.5 1.3 %copy-start.9 = (bf16[128,288]{0,1:T(8,128)(2,1)S(1)}, bf16[128,288]{0,1:T(8,128)(2,1)}, u32[]{:S(2)}) copy-start(bf16[128,288]{0,1:T(8,128)(2,1)} %param.7) | copy-start | bytes 221188
  5.2 0.8 copy-start.7
  6.0 17.4 %collective-permute-start = (bf16[128,1152]{1,0:T(8,128)(2,1)S(1)}, bf16[128,1152]{1,0:T(8,128)(2,1)}, u32[]{:S(2)}, u32[]{:S(2)}) collective-permute-start(bf16[128,1152]{1,0:T(8,128)(2,1)S(1)} %pad_maximum_fusion.1), channel_id=1, source_target_pairs={{0,1},{1,0},{2,3},{3,2},{4,5},{5,4},{6,7},{7,6},{8,9},{9,8},{10,11... | collective-permute-start | bytes 884744 | tf_op jit(solution)/shard_map/ppermute | solution.py:62
  24.4 13.1 %copy-start.1 = (bf16[128,1152]{1,0:T(8,128)(2,1)S(1)}, bf16[128,1152]{1,0:T(8,128)(2,1)}, u32[]{:S(2)}) copy-start(bf16[128,1152]{1,0:T(8,128)(2,1)} %param.6) | copy-start | bytes 884740
  37.5 19.7 %copy-start.10 = (s32[128]{0:T(128)S(1)}, s32[128]{0:T(128)}, u32[]{:S(2)}) copy-start(s32[128]{0:T(128)} %param.11) | copy-start | bytes 1540
  41.7 27.6 %copy-start.8 = (bf16[2,64,1152]{2,1,0:T(8,128)(2,1)}, bf16[2,64,1152]{2,1,0:T(8,128)(2,1)S(1)}, u32[]{:S(2)}) copy-start(bf16[2,64,1152]{2,1,0:T(8,128)(2,1)S(1)} %get-tuple-element.14) | copy-start | bytes 884740
  41.7 24.9 %collective-permute-start.3 = (bf16[128,1152]{1,0:T(8,128)(2,1)S(1)}, bf16[128,1152]{1,0:T(8,128)(2,1)S(1)}, u32[]{:S(2)}, u32[]{:S(2)}) collective-permute-start(bf16[128,1152]{1,0:T(8,128)(2,1)S(1)} %bitcast.50), channel_id=1, source_target_pairs={{0,0},{1,1015},{2,1020},{3,1017},{4,4},{5,1019},{6,2},{7,1021},{8,... | collective-permute-start | bytes 884744 | tf_op jit(solution)/shard_map/ppermute | solution.py:36
  57.2 12.0 %collective-permute-start.4 = (bf16[128,1152]{1,0:T(8,128)(2,1)S(1)}, bf16[128,1152]{1,0:T(8,128)(2,1)S(1)}, u32[]{:S(2)}, u32[]{:S(2)}) collective-permute-start(bf16[128,1152]{1,0:T(8,128)(2,1)S(1)} %bitcast.51), channel_id=1, source_target_pairs={{0,1010},{1,999},{2,1004},{3,1001},{4,1014},{5,1003},{6,1008},{7,1... | collective-permute-start | bytes 884744 | tf_op jit(solution)/shard_map/ppermute | solution.py:36
  61.1 20.1 %collective-permute-start.2 = (bf16[128,1152]{1,0:T(8,128)(2,1)}, bf16[128,1152]{1,0:T(8,128)(2,1)}, u32[]{:S(2)}, u32[]{:S(2)}) collective-permute-start(bf16[128,1152]{1,0:T(8,128)(2,1)} %bitcast.5), channel_id=1, source_target_pairs={{0,16},{1,29},{2,22},{3,27},{4,20},{5,33},{6,26},{7,31},{8,24},{9,... | collective-permute-start | bytes 884744 | tf_op jit(solution)/shard_map/ppermute | solution.py:36
  64.7 15.5 %collective-permute-start.1 = (bf16[128,1152]{1,0:T(8,128)(2,1)}, bf16[128,1152]{1,0:T(8,128)(2,1)}, u32[]{:S(2)}, u32[]{:S(2)}) collective-permute-start(bf16[128,1152]{1,0:T(8,128)(2,1)} %bitcast.5), channel_id=1, source_target_pairs={{0,0},{1,13},{2,6},{3,11},{4,4},{5,17},{6,10},{7,15},{8,8},{9,21},... | collective-permute-start | bytes 884744 | tf_op jit(solution)/shard_map/ppermute | solution.py:36
  81.2 4.9 %copy-start.4 = (f32[128,1152]{1,0:T(8,128)S(1)}, f32[128,1152]{1,0:T(8,128)}, u32[]{:S(2)}) copy-start(f32[128,1152]{1,0:T(8,128)} %convolution_multiply_fusion) | copy-start | bytes 1769476
  84.2 3.5 %collective-permute-start.5 = (bf16[128,1280]{1,0:T(8,128)(2,1)S(1)}, bf16[128,1280]{1,0:T(8,128)(2,1)S(1)}, u32[]{:S(2)}, u32[]{:S(2)}) collective-permute-start(bf16[128,1280]{1,0:T(8,128)(2,1)S(1)} %pad_maximum_fusion), channel_id=1, source_target_pairs={{0,1},{1,0},{2,3},{3,2},{4,5},{5,4},{6,7},{7,6},{8,9},{9,8},{10,11... | collective-permute-start | bytes 983048 | tf_op jit(solution)/shard_map/ppermute | solution.py:62
  111.5 3.3 %copy-start.6 = (f32[128,1076]{0,1:T(8,128)S(1)}, f32[128,1076]{0,1:T(8,128)}, u32[]{:S(2)}) copy-start(f32[128,1076]{0,1:T(8,128)} %copy-done.5) | copy-start | bytes 1652740
  114.8 2.3 %copy-start.3 = (bf16[288,1152]{1,0:T(8,128)(2,1)S(1)}, bf16[288,1152]{1,0:T(8,128)(2,1)}, u32[]{:S(2)}) copy-start(bf16[288,1152]{1,0:T(8,128)(2,1)} %param.10) | copy-start | bytes 1990660

commit v4 on v1

v4 whole, which is shorter than its diff:
```python
import jax
import jax.numpy as jnp
from jax import lax
from jax.experimental import pallas as pl
from jax.experimental.pallas import tpu as pltpu
from jax.sharding import Mesh, PartitionSpec as P

WINDOW = 8


logit_scale = 32.0
logit_bias = -2.0
loss_scale = 16.0
epsilon = 1e-06

AXES = ("z", "y_lo", "x", "y_hi", "core")
SIZES = (16, 4, 4, 2, 2)
MP = ("y_hi", "core")
NEAR = 4
OFFSET = (0, 3, 1, 2)
HALF = 64
LANES = 128
GELU_SCALE = 0.7978845608028654
GELU_CUBIC = 0.044715


def place(block, role):
    z = block // 16
    y_hi = (role // 2) ^ (z & 1)
    return block * 4 + y_hi * 2 + role % 2


def moves(shift):
    return [
        (place(block, role), place((block + shift(role)) % 256, role))
        for block in range(256)
        for role in range(4)
    ]


def move(value, shift):
    return lax.ppermute(value, AXES, moves(shift))


def dot(left, right, left_dim, right_dim):
    return lax.dot_general(
        left, right, (((left_dim,), (right_dim,)), ((), ())), preferred_element_type=jnp.float32
    )


def own_half(array, core):
    return array[pl.ds(pl.multiple_of(core * HALF, HALF), HALF), :]


def heads_kernel(
    core_ref, images_ref, texts_ref, fc_in_ref, fc_out_ref, head_ref,
    slope_ref, kept_ref, sent_ref, image_term, text_term,
):
    core = core_ref[0]
    text_term[...] = dot(texts_ref[...], head_ref[...], 0, 0)
    pre_act = dot(fc_in_ref[...], images_ref[...], 1, 1)
    square = pre_act * pre_act
    bent = jnp.tanh(GELU_SCALE * pre_act * (1.0 + GELU_CUBIC * square))
    activation = (0.5 * pre_act * (1.0 + bent)).astype(jnp.bfloat16)
    slope_ref[...] = 0.5 * (1.0 + bent) + (
        0.5 * GELU_SCALE * pre_act * (1.0 - bent * bent) * (1.0 + 3.0 * GELU_CUBIC * square)
    )
    image_term[...] = dot(activation, fc_out_ref[...], 0, 0)
    for first, term in ((0, image_term), (HALF, text_term)):
        kept_ref[first : first + HALF] = own_half(term, core)
        sent_ref[first : first + HALF] = own_half(term, 1 - core).astype(jnp.bfloat16)


def unit_kernel(core_ref, chips_ref, images_ref, unit_ref, inverse_ref, sent_ref):
    embed = chips_ref[0].astype(jnp.float32) + chips_ref[1].astype(jnp.float32)
    image_embed = own_half(images_ref, core_ref[0]).astype(jnp.float32) + embed[:HALF]
    for first, rows in ((0, image_embed), (HALF, embed[HALF:])):
        inverse = lax.rsqrt(jnp.sum(rows * rows, axis=1, keepdims=True) + epsilon)
        unit = rows * inverse
        unit_ref[first : first + HALF] = unit
        inverse_ref[first : first + HALF] = jnp.broadcast_to(inverse, (HALF, LANES))
        sent_ref[first : first + HALF] = unit.astype(jnp.bfloat16)


def split_loss(loss):
    high = loss.astype(jnp.bfloat16).astype(jnp.float32)
    lanes = lax.broadcasted_iota(jnp.int32, (loss.shape[0], LANES), 1)
    return jnp.where(lanes == 0, high, jnp.where(lanes == 1, loss - high, 0.0))


def pair_terms(own, others, positive):
    logits = logit_scale * dot(own, others, 1, 1) + logit_bias
    if positive is None:
        flipped = logits
    else:
        flipped = jnp.where(positive, -logits, logits)
    small = jnp.exp(-jnp.abs(flipped))
    loss = jnp.maximum(flipped, 0.0) + jnp.log1p(small)
    sigmoid = jnp.where(flipped >= 0.0, 1.0, small) / (1.0 + small)
    if positive is None:
        pair_grad = loss_scale * sigmoid
    else:
        pair_grad = jnp.where(positive, -loss_scale, loss_scale) * sigmoid
    return logit_scale * dot(pair_grad.astype(jnp.bfloat16), others, 1, 0), loss


def score_kernel(
    core_ref, image_ref, text_ref, near_text_ref, far_text_ref, near_image_ref, far_image_ref,
    column_ref, row_ref, kept_ref, sent_ref, image_part, text_part,
):
    core = core_ref[0]
    rows, width = image_ref.shape
    across = lax.broadcasted_iota(jnp.int32, (rows, rows), 1)
    down = lax.broadcasted_iota(jnp.int32, (rows, rows), 0)
    near, near_loss = pair_terms(image_ref[...], near_text_ref[...], across == column_ref[...])
    far, far_loss = pair_terms(image_ref[...], far_text_ref[...], None)
    image_part[:, :width] = near + far
    image_part[:, width:] = split_loss(jnp.sum(near_loss + far_loss, axis=1, keepdims=True))
    near, unused = pair_terms(text_ref[...], near_image_ref[...], down == row_ref[...])
    far, unused = pair_terms(text_ref[...], far_image_ref[...], None)
    text_part[:, :width] = near + far
    text_part[:, width:] = jnp.zeros((rows, LANES), jnp.float32)
    for first, part in ((0, image_part), (HALF, text_part)):
        kept_ref[first : first + HALF] = own_half(part, core)
        sent_ref[first : first + HALF] = own_half(part, 1 - core).astype(jnp.bfloat16)


def tangent_kernel(chips_ref, unit_ref, inverse_ref, sent_ref):
    width = unit_ref.shape[1]
    sums = chips_ref[0].astype(jnp.float32) + chips_ref[1].astype(jnp.float32)
    grad, unit = sums[:, :width], unit_ref[...]
    along = jnp.sum(unit * grad, axis=1, keepdims=True)
    tangent = (grad - unit * along) * inverse_ref[:, :1]
    sent_ref[:, :width] = tangent.astype(jnp.bfloat16)
    loss = sums[:, width : width + 1] + sums[:, width + 1 : width + 2]
    sent_ref[:, width:] = split_loss(loss).astype(jnp.bfloat16)


def backward_kernel(
    grads_ref, slope_ref, fc_out_ref, head_ref, hidden_ref, text_ref, loss_ref
):
    rows, width = 2 * HALF, fc_out_ref.shape[1]
    image_grad = grads_ref[:, :HALF].reshape(rows, width + LANES)
    text_grad = grads_ref[:, HALF:].reshape(rows, width + LANES)
    losses = jnp.sum(image_grad[:, width:].astype(jnp.float32), axis=1, keepdims=True)
    loss_ref[...] = jnp.broadcast_to(losses, (rows, LANES)).T / (WINDOW * rows)
    act_grad = dot(fc_out_ref[...], image_grad[:, :width], 1, 1)
    hidden_ref[...] = (slope_ref[...] * act_grad).astype(jnp.bfloat16)
    text_ref[...] = dot(head_ref[...], text_grad[:, :width], 1, 1).astype(jnp.bfloat16)


def kernel(body, outs, scratch=(), places=""):
    spaces = dict(s=pltpu.SMEM, v=pltpu.VMEM)
    return pl.pallas_call(
        body,
        out_shape=[jax.ShapeDtypeStruct(shape, dtype) for shape, dtype in outs],
        in_specs=[pl.BlockSpec(memory_space=spaces[place]) for place in places],
        out_specs=[pl.BlockSpec(memory_space=pltpu.VMEM) for unused in outs],
        scratch_shapes=list(scratch),
        compiler_params=pltpu.CompilerParams(vmem_limit_bytes=24 * 1024 * 1024),
    )


def chip_gather(kept, sent):
    got = lax.ppermute(sent, "core", [(0, 1), (1, 0)])
    return lax.all_gather((kept + got.astype(jnp.float32)).astype(jnp.bfloat16), "y_hi")


def local(images, texts, fc_in, fc_out, head, partner):
    rows, width = images.shape
    hidden, features = fc_out.shape[0], head.shape[0]
    f32, bf16 = jnp.float32, jnp.bfloat16
    core = lax.axis_index("core")
    role = 2 * (lax.axis_index("y_hi") ^ (lax.axis_index("z") & 1)) + core
    core = core.reshape(1)

    slope, kept, sent = kernel(
        heads_kernel,
        [((hidden, rows), f32), ((rows, width), f32), ((rows, width), bf16)],
        [
            pltpu.VMEM((rows, width), f32),
            pltpu.VMEM((rows, width), f32),
        ],
        "svvvvv",
    )(core, images, texts.T, fc_in.T, fc_out, head)

    unit, inverse, unit_sent = kernel(
        unit_kernel,
        [((rows, width), f32), ((rows, LANES), f32), ((rows, width), bf16)],
        places="svv",
    )(core, chip_gather(kept, sent), images)

    units = lax.all_gather(unit_sent, "core")
    image_own = units[:, :HALF].reshape(rows, width)
    text_own = units[:, HALF:].reshape(rows, width)
    far_text = move(text_own, lambda role: OFFSET[role] + NEAR)
    far_image = move(image_own, lambda role: -OFFSET[role] - NEAR)
    near_text = move(text_own, lambda role: OFFSET[role])
    near_image = move(image_own, lambda role: -OFFSET[role])

    paired = jnp.where(role == 0, partner, -1)
    columns = width + LANES
    kept, sent = kernel(
        score_kernel,
        [((rows, columns), f32), ((rows, columns), bf16)],
        [pltpu.VMEM((rows, columns), f32), pltpu.VMEM((rows, columns), f32)],
        "svvvvvvvv",
    )(
        core, image_own, text_own, near_text, far_text, near_image, far_image,
        paired.reshape(rows, 1), paired.reshape(1, rows),
    )

    (grads,) = kernel(tangent_kernel, [((rows, columns), bf16)], places="vvv")(
        chip_gather(kept, sent), unit, inverse
    )
    hidden_grad, text_grad, loss = kernel(
        backward_kernel,
        [((hidden, rows), bf16), ((features, rows), bf16), ((rows, rows), f32)],
        places="vvvv",
    )(lax.all_gather(grads, "core"), slope, fc_out, head)
    return (hidden_grad.T, text_grad.T, loss[0])


def solution(mesh):
    dp = ("z", "y_lo", "x")
    return jax.shard_map(
        local,
        mesh=Mesh(mesh.devices.reshape(SIZES), AXES),
        in_specs=(P(dp, None), P(dp, MP), P(None, MP), P(MP, None), P(MP, None), P(dp)),
        out_specs=(P(dp, MP), P(dp, MP), P(dp)),
        check_vma=False,
    )
```

time: 144 us -> 116 us (0.81); the launches traced: 142 us -> 116 us
  blocking collectives: 58 us -> 42.4 us
  matrix products: 14.7 us -> 0 us
  other arithmetic: 10.4 us -> 0.12 us
  Pallas kernels: 0 us -> 6.51 us
  local copies, waits for them, and re-layouts: 1.76 us -> 7.02 us
  waiting for transfers between devices: 11.8 us -> 15.9 us
  starting transfers between devices: 44.7 us -> 43.1 us
    all_to_all x2 -> x0, starting transfers between devices: 21.7 us -> none  [core_sum(): got = lax.all_to_all(halves, 'core', 0, 0).astype(jnp.float32)]
    ppermute x0 -> x2, starting transfers between devices: none -> 18.2 us  [chip_gather(): got = lax.ppermute(sent, 'core', [(0, 1), (1, 0)])]
    dot_general x8 -> x0, matrix products: 14.7 us -> none  [the longest x1 2.83 us: local(): pre_act = jnp.dot(images, fc_in, preferred_element_type=jnp.float32)]
    all_to_all x2 -> x0, blocking collectives: 13.3 us -> none  [core_sum(): got = lax.all_to_all(halves, 'core', 0, 0).astype(jnp.float32)]
    pallas_call x0 -> x5, Pallas kernels: none -> 6.51 us  [the longest x1 2.43 us: local(): kernel(heads_kernel, [((hidden, rows), f32), ((rows, width), f32), ((rows...]
    convert_element_type x13 -> x2, other arithmetic: 6.41 us -> 0.12 us  [chip_gather(): (kept + got.astype(jnp.float32)).astype(jnp.bfloat16)]
    unnamed x18 -> x16, local copies, waits for them, and re-layouts: 1.56 us -> 6.35 us
    ppermute x0 -> x2, waiting for transfers between devices: none -> 2.78 us  [chip_gather(): got = lax.ppermute(sent, 'core', [(0, 1), (1, 0)])]
  transfers between devices with their start and end apart: 6 -> 6, of which waited for: 1 -> 6; matrix products, arithmetic and copies ran while one was open for 11% -> 0% of each run, Pallas kernels for 0% -> 0%
where the time goes in v4:
time: 116 us
  starting transfers between devices  43.1 us (37%)
  blocking collectives  42.4 us (37%)
  waiting for transfers between devices  15.9 us (14%)
  local copies, waits for them, and re-layouts  7.02 us (6%)
  Pallas kernels  6.51 us (6%)
    all_gather x2, blocking collectives, chip_gather(): lax.all_gather((kept + got.astype(jnp.float32)).astype(jnp.bfloat16), 'y_...  36.6 us
    ppermute x4, starting transfers between devices, move(): return lax.ppermute(value, AXES, moves(shift))  24.8 us
    ppermute x2, starting transfers between devices, chip_gather(): got = lax.ppermute(sent, 'core', [(0, 1), (1, 0)])  18.2 us
    ppermute x4, waiting for transfers between devices, move(): return lax.ppermute(value, AXES, moves(shift))  13.1 us
    unnamed x16, local copies, waits for them, and re-layouts  6.35 us
    all_gather x1, blocking collectives, local(): units = lax.all_gather(unit_sent, 'core')  3.06 us
    all_gather x1, blocking collectives, local(): lax.all_gather(grads, 'core')  2.79 us
    ppermute x2, waiting for transfers between devices, chip_gather(): got = lax.ppermute(sent, 'core', [(0, 1), (1, 0)])  2.78 us
  transfers between devices with their start and end apart: 6, of which 6 were waited for; matrix products, arithmetic and copies ran while one was open for 0% of the time, Pallas kernels for 0%

profile of v4, /device:TPU:1, one launch (start us, length us, event | category | flops | bytes accessed | tf_op | source)
XLA Modules:
  0.0 115.8 jit_solution(18418685909529478109)
XLA Ops:
  0.6 1.7 %copy-done = bf16[1076,1152]{1,0:T(8,128)(2,1)S(1)} copy-done((bf16[1076,1152]{1,0:T(8,128)(2,1)S(1)}, bf16[1076,1152]{1,0:T(8,128)(2,1)}, u32[]{:S(2)}) %copy-start) | copy-done | bytes 2479128
  2.3 1.1 copy-done.2
  3.4 1.7 %copy-done.4 = bf16[1152,1076]{0,1:T(8,128)(2,1)S(1)} copy-done((bf16[1152,1076]{0,1:T(8,128)(2,1)S(1)}, bf16[1152,1076]{0,1:T(8,128)(2,1)}, u32[]{:S(2)}) %copy-start.4) | copy-done | bytes 2479128
  5.1 1.0 copy-done.5
  6.1 0.9 copy-done.6
  7.0 2.4 %shard_map.85 = (f32[1076,128]{1,0:T(8,128)S(1)}, f32[128,1152]{1,0:T(8,128)S(1)}, bf16[128,1152]{1,0:T(8,128)(2,1)S(1)}) custom-call(s32[1]{0:T(128)} %bitcast.core_ref, bf16[128,1152]{1,0:T(8,128)(2,1)S(1)} %copy-done.5, bf16[288,128]{1,0:T(8,128)(2,1)S(1)} %bitcast.27, bf16[1076,1152]{1,0:T(8,128)(2,1)S(1)} %bitcast.19, bf16[1076,1152]{1,0:T(8,128)(2,1)S(1)} %copy-done, ...), custom_call_target="tpu_custom_call" | custom-call | tf_op jit(solution)/shard_map/pallas_call | solution.py:177
  9.4 16.1 %collective-permute-start = (bf16[128,1152]{1,0:T(8,128)(2,1)S(1)}, bf16[128,1152]{1,0:T(8,128)(2,1)S(1)}, u32[]{:S(2)}, u32[]{:S(2)}) collective-permute-start(bf16[128,1152]{1,0:T(8,128)(2,1)S(1)} %get-tuple-element.15), channel_id=1, source_target_pairs={{0,1},{1,0},{2,3},{3,2},{4,5},{5,4},{6,7},{7,6},{8,9},{9,8},{10,11... | collective-permute-start | bytes 884744 | tf_op jit(solution)/shard_map/ppermute | solution.py:165
  25.5 1.2 %collective-permute-done = bf16[128,1152]{1,0:T(8,128)(2,1)S(1)} collective-permute-done((bf16[128,1152]{1,0:T(8,128)(2,1)S(1)}, bf16[128,1152]{1,0:T(8,128)(2,1)S(1)}, u32[]{:S(2)}, u32[]{:S(2)}) %collective-permute-start) | collective-permute-done | bytes 294944 | tf_op jit(solution)/shard_map/ppermute | solution.py:165
  26.7 12.8 %all-gather = bf16[256,1152]{1,0:T(8,128)(2,1)S(1)} all-gather(bf16[128,1152]{1,0:T(8,128)(2,1)S(1)} %add_convert_fusion.1), channel_id=2, replica_groups=mesh['z'=16,'y_lo'=4,'x'=4,'y_hi'=2,'core'=2] {'y_hi'}, dimensions={0}, use_global_device_ids=true | all-gather | bytes 884736 | tf_op jit(solution)/shard_map/all_gather | solution.py:166
  39.8 3.1 %all-gather.1 = bf16[256,1152]{1,0:T(8,128)(2,1)S(1)} all-gather(bf16[128,1152]{1,0:T(8,128)(2,1)S(1)} %get-tuple-element.16), channel_id=3, replica_groups=mesh['z'=16,'y_lo'=4,'x'=4,'y_hi'=2,'core'=2] {'core'}, dimensions={0}, use_global_device_ids=true | all-gather | bytes 884736 | tf_op jit(solution)/shard_map/all_gather | solution.py:193
  42.9 16.1 %collective-permute-start.4 = (bf16[128,1152]{1,0:T(8,128)(2,1)S(1)}, bf16[128,1152]{1,0:T(8,128)(2,1)S(1)}, u32[]{:S(2)}, u32[]{:S(2)}) collective-permute-start(bf16[128,1152]{1,0:T(8,128)(2,1)S(1)} %bitcast.24), channel_id=1, source_target_pairs={{0,1010},{1,999},{2,1004},{3,1001},{4,1014},{5,1003},{6,1008},{7,1... | collective-permute-start | bytes 884744 | tf_op jit(solution)/shard_map/ppermute | solution.py:42
  58.9 3.2 %collective-permute-start.3 = (bf16[128,1152]{1,0:T(8,128)(2,1)S(1)}, bf16[128,1152]{1,0:T(8,128)(2,1)S(1)}, u32[]{:S(2)}, u32[]{:S(2)}) collective-permute-start(bf16[128,1152]{1,0:T(8,128)(2,1)S(1)} %bitcast.25), channel_id=1, source_target_pairs={{0,0},{1,1015},{2,1020},{3,1017},{4,4},{5,1019},{6,2},{7,1021},{8,... | collective-permute-start | bytes 884744 | tf_op jit(solution)/shard_map/ppermute | solution.py:42
  62.1 3.6 %collective-permute-start.2 = (bf16[128,1152]{1,0:T(8,128)(2,1)S(1)}, bf16[128,1152]{1,0:T(8,128)(2,1)S(1)}, u32[]{:S(2)}, u32[]{:S(2)}) collective-permute-start(bf16[128,1152]{1,0:T(8,128)(2,1)S(1)} %bitcast.21), channel_id=1, source_target_pairs={{0,16},{1,29},{2,22},{3,27},{4,20},{5,33},{6,26},{7,31},{8,24},{9,... | collective-permute-start | bytes 884744 | tf_op jit(solution)/shard_map/ppermute | solution.py:42
  65.8 1.9 %collective-permute-start.1 = (bf16[128,1152]{1,0:T(8,128)(2,1)S(1)}, bf16[128,1152]{1,0:T(8,128)(2,1)S(1)}, u32[]{:S(2)}, u32[]{:S(2)}) collective-permute-start(bf16[128,1152]{1,0:T(8,128)(2,1)S(1)} %bitcast.22), channel_id=1, source_target_pairs={{0,0},{1,13},{2,6},{3,11},{4,4},{5,17},{6,10},{7,15},{8,8},{9,21},... | collective-permute-start | bytes 884744 | tf_op jit(solution)/shard_map/ppermute | solution.py:42
  68.0 3.4 %collective-permute-done.3.near_image_ref = bf16[128,1152]{1,0:T(8,128)(2,1)S(1)} collective-permute-done((bf16[128,1152]{1,0:T(8,128)(2,1)S(1)}, bf16[128,1152]{1,0:T(8,128)(2,1)S(1)}, u32[]{:S(2)}, u32[]{:S(2)}) %collective-permute-start.3) | collective-permute-done | bytes 294944 | tf_op jit(solution)/shard_map/ppermute | solution.py:42
  71.3 6.7 %collective-permute-done.2.far_text_ref = bf16[128,1152]{1,0:T(8,128)(2,1)S(1)} collective-permute-done((bf16[128,1152]{1,0:T(8,128)(2,1)S(1)}, bf16[128,1152]{1,0:T(8,128)(2,1)S(1)}, u32[]{:S(2)}, u32[]{:S(2)}) %collective-permute-start.2) | collective-permute-done | bytes 294944 | tf_op jit(solution)/shard_map/ppermute | solution.py:42
  78.1 2.9 %collective-permute-done.1.near_text_ref = bf16[128,1152]{1,0:T(8,128)(2,1)S(1)} collective-permute-done((bf16[128,1152]{1,0:T(8,128)(2,1)S(1)}, bf16[128,1152]{1,0:T(8,128)(2,1)S(1)}, u32[]{:S(2)}, u32[]{:S(2)}) %collective-permute-start.1) | collective-permute-done | bytes 294944 | tf_op jit(solution)/shard_map/ppermute | solution.py:42
  81.0 1.8 %shard_map.87 = (f32[128,1280]{1,0:T(8,128)S(1)}, bf16[128,1280]{1,0:T(8,128)(2,1)S(1)}) custom-call(s32[1]{0:T(128)} %bitcast.core_ref, bf16[128,1152]{1,0:T(8,128)(2,1)S(1)} %bitcast.26, bf16[128,1152]{1,0:T(8,128)(2,1)S(1)} %bitcast.23, bf16[128,1152]{1,0:T(8,128)(2,1)S(1)} %collective-permute-done.1.near_text_ref, ...), custom_call_target="tpu_custom_call" | custom-call | tf_op jit(solution)/shard_map/pallas_call | solution.py:203
  82.8 2.2 %collective-permute-start.5 = (bf16[128,1280]{1,0:T(8,128)(2,1)S(1)}, bf16[128,1280]{1,0:T(8,128)(2,1)S(1)}, u32[]{:S(2)}, u32[]{:S(2)}) collective-permute-start(bf16[128,1280]{1,0:T(8,128)(2,1)S(1)} %get-tuple-element.18), channel_id=1, source_target_pairs={{0,1},{1,0},{2,3},{3,2},{4,5},{5,4},{6,7},{7,6},{8,9},{9,8},{10,11... | collective-permute-start | bytes 983048 | tf_op jit(solution)/shard_map/ppermute | solution.py:165
  85.0 1.6 %collective-permute-done.5 = bf16[128,1280]{1,0:T(8,128)(2,1)S(1)} collective-permute-done((bf16[128,1280]{1,0:T(8,128)(2,1)S(1)}, bf16[128,1280]{1,0:T(8,128)(2,1)S(1)}, u32[]{:S(2)}, u32[]{:S(2)}) %collective-permute-start.5) | collective-permute-done | bytes 327712 | tf_op jit(solution)/shard_map/ppermute | solution.py:165
  86.7 23.8 %all-gather.2 = bf16[256,1280]{1,0:T(8,128)(2,1)S(1)} all-gather(bf16[128,1280]{1,0:T(8,128)(2,1)S(1)} %add_convert_fusion), channel_id=4, replica_groups=mesh['z'=16,'y_lo'=4,'x'=4,'y_hi'=2,'core'=2] {'y_hi'}, dimensions={0}, use_global_device_ids=true | all-gather | bytes 983040 | tf_op jit(solution)/shard_map/all_gather | solution.py:166
  110.8 2.8 %all-gather.3 = bf16[256,1280]{1,0:T(8,128)(2,1)S(1)} all-gather(bf16[128,1280]{1,0:T(8,128)(2,1)S(1)} %shard_map.88), channel_id=5, replica_groups=mesh['z'=16,'y_lo'=4,'x'=4,'y_hi'=2,'core'=2] {'core'}, dimensions={0}, use_global_device_ids=true | all-gather | bytes 983040 | tf_op jit(solution)/shard_map/all_gather | solution.py:220
  113.6 1.7 %shard_map.89 = (bf16[1076,128]{1,0:T(8,128)(2,1)}, bf16[288,128]{1,0:T(8,128)(2,1)}, f32[128,128]{1,0:T(8,128)S(1)}) custom-call(bf16[2,128,1280]{2,1,0:T(8,128)(2,1)S(1)} %bitcast.18, f32[1076,128]{1,0:T(8,128)S(1)} %get-tuple-element.21.slope_ref, bf16[1076,1152]{1,0:T(8,128)(2,1)S(1)} %copy-done.1, bf16[288,1152]{1,0:T(8,128)(2,1)S(1)} %copy-done.3), custom_call_target="tpu_custom_call" | custom-call | tf_op jit(solution)/shard_map/pallas_call | solution.py:216
  115.3 0.5 slice_bitcast_fusion
  (19 shorter events, 1.0 us)
Async XLA Ops:
  0.6 1.7 %copy-start = (bf16[1076,1152]{1,0:T(8,128)(2,1)S(1)}, bf16[1076,1152]{1,0:T(8,128)(2,1)}, u32[]{:S(2)}) copy-start(bf16[1076,1152]{1,0:T(8,128)(2,1)} %fc_out_ref.3) | copy-start | bytes 7437316
  2.3 1.1 copy-start.2
  3.4 1.7 %copy-start.4 = (bf16[1152,1076]{0,1:T(8,128)(2,1)S(1)}, bf16[1152,1076]{0,1:T(8,128)(2,1)}, u32[]{:S(2)}) copy-start(bf16[1152,1076]{0,1:T(8,128)(2,1)} %param.8) | copy-start | bytes 7437316
  5.1 1.0 copy-start.5
  6.1 0.9 copy-start.6
  9.4 17.3 %collective-permute-start = (bf16[128,1152]{1,0:T(8,128)(2,1)S(1)}, bf16[128,1152]{1,0:T(8,128)(2,1)S(1)}, u32[]{:S(2)}, u32[]{:S(2)}) collective-permute-start(bf16[128,1152]{1,0:T(8,128)(2,1)S(1)} %get-tuple-element.15), channel_id=1, source_target_pairs={{0,1},{1,0},{2,3},{3,2},{4,5},{5,4},{6,7},{7,6},{8,9},{9,8},{10,11... | collective-permute-start | bytes 884744 | tf_op jit(solution)/shard_map/ppermute | solution.py:165
  26.7 41.0 %copy-start.7 = (s32[128]{0:T(128)S(1)}, s32[128]{0:T(128)}, u32[]{:S(2)}) copy-start(s32[128]{0:T(128)} %param.11) | copy-start | bytes 1540
  42.9 25.1 %collective-permute-start.4 = (bf16[128,1152]{1,0:T(8,128)(2,1)S(1)}, bf16[128,1152]{1,0:T(8,128)(2,1)S(1)}, u32[]{:S(2)}, u32[]{:S(2)}) collective-permute-start(bf16[128,1152]{1,0:T(8,128)(2,1)S(1)} %bitcast.24), channel_id=1, source_target_pairs={{0,1010},{1,999},{2,1004},{3,1001},{4,1014},{5,1003},{6,1008},{7,1... | collective-permute-start | bytes 884744 | tf_op jit(solution)/shard_map/ppermute | solution.py:42
  58.9 12.4 %collective-permute-start.3 = (bf16[128,1152]{1,0:T(8,128)(2,1)S(1)}, bf16[128,1152]{1,0:T(8,128)(2,1)S(1)}, u32[]{:S(2)}, u32[]{:S(2)}) collective-permute-start(bf16[128,1152]{1,0:T(8,128)(2,1)S(1)} %bitcast.25), channel_id=1, source_target_pairs={{0,0},{1,1015},{2,1020},{3,1017},{4,4},{5,1019},{6,2},{7,1021},{8,... | collective-permute-start | bytes 884744 | tf_op jit(solution)/shard_map/ppermute | solution.py:42
  62.1 15.9 %collective-permute-start.2 = (bf16[128,1152]{1,0:T(8,128)(2,1)S(1)}, bf16[128,1152]{1,0:T(8,128)(2,1)S(1)}, u32[]{:S(2)}, u32[]{:S(2)}) collective-permute-start(bf16[128,1152]{1,0:T(8,128)(2,1)S(1)} %bitcast.21), channel_id=1, source_target_pairs={{0,16},{1,29},{2,22},{3,27},{4,20},{5,33},{6,26},{7,31},{8,24},{9,... | collective-permute-start | bytes 884744 | tf_op jit(solution)/shard_map/ppermute | solution.py:42
  65.8 15.2 %collective-permute-start.1 = (bf16[128,1152]{1,0:T(8,128)(2,1)S(1)}, bf16[128,1152]{1,0:T(8,128)(2,1)S(1)}, u32[]{:S(2)}, u32[]{:S(2)}) collective-permute-start(bf16[128,1152]{1,0:T(8,128)(2,1)S(1)} %bitcast.22), channel_id=1, source_target_pairs={{0,0},{1,13},{2,6},{3,11},{4,4},{5,17},{6,10},{7,15},{8,8},{9,21},... | collective-permute-start | bytes 884744 | tf_op jit(solution)/shard_map/ppermute | solution.py:42
  82.8 30.8 %copy-start.1 = (bf16[1076,1152]{1,0:T(8,128)(2,1)S(1)}, bf16[1076,1152]{1,0:T(8,128)(2,1)}, u32[]{:S(2)}) copy-start(bf16[1076,1152]{1,0:T(8,128)(2,1)} %fc_out_ref.3) | copy-start | bytes 7437316
  82.8 30.8 %copy-start.3 = (bf16[288,1152]{1,0:T(8,128)(2,1)S(1)}, bf16[288,1152]{1,0:T(8,128)(2,1)}, u32[]{:S(2)}) copy-start(bf16[288,1152]{1,0:T(8,128)(2,1)} %head_ref.3) | copy-start | bytes 1990660
  82.8 3.8 %collective-permute-start.5 = (bf16[128,1280]{1,0:T(8,128)(2,1)S(1)}, bf16[128,1280]{1,0:T(8,128)(2,1)S(1)}, u32[]{:S(2)}, u32[]{:S(2)}) collective-permute-start(bf16[128,1280]{1,0:T(8,128)(2,1)S(1)} %get-tuple-element.18), channel_id=1, source_target_pairs={{0,1},{1,0},{2,3},{3,2},{4,5},{5,4},{6,7},{7,6},{8,9},{9,8},{10,11... | collective-permute-start | bytes 983048 | tf_op jit(solution)/shard_map/ppermute | solution.py:165

commit v5 on v4

--- a/solution.py
+++ b/solution.py
@@ -17,9 +17,11 @@
 SIZES = (16, 4, 4, 2, 2)
 MP = ("y_hi", "core")
 NEAR = 4
-OFFSET = (0, 3, 1, 2)
+OFFSET = (0, 2, 1, 3)
 HALF = 64
 LANES = 128
+HEADS_VMEM = 56
+CUTS = 3
 GELU_SCALE = 0.7978845608028654
 GELU_CUBIC = 0.044715
 
@@ -53,19 +55,40 @@
 
 
 def heads_kernel(
-    core_ref, images_ref, texts_ref, fc_in_ref, fc_out_ref, head_ref,
-    slope_ref, kept_ref, sent_ref, image_term, text_term,
+    core_ref, texts_hbm, head_hbm, images_hbm, fc_in_hbm, fc_out_hbm,
+    slope_ref, kept_ref, sent_ref,
+    texts_ref, head_ref, images_ref, fc_in_ref, fc_out_ref, image_term, text_term, sems,
 ):
     core = core_ref[0]
+    width = images_ref.shape[1]
+    cuts = [pl.ds(first, width // CUTS) for first in range(0, width, width // CUTS)]
+    pairs = [(texts_hbm, texts_ref), (head_hbm, head_ref), (images_hbm, images_ref)]
+    for source, target in ((fc_in_hbm, fc_in_ref), (fc_out_hbm, fc_out_ref)):
+        pairs += [(source.at[:, cut], target.at[:, cut]) for cut in cuts]
+    copies = [
+        pltpu.make_async_copy(source, target, sems.at[index])
+        for index, (source, target) in enumerate(pairs)
+    ]
+    for copy in copies:
+        copy.start()
+    for copy in copies[:2]:
+        copy.wait()
     text_term[...] = dot(texts_ref[...], head_ref[...], 0, 0)
-    pre_act = dot(fc_in_ref[...], images_ref[...], 1, 1)
+    copies[2].wait()
+    pre_act = None
+    for cut, copy in zip(cuts, copies[3 : 3 + CUTS]):
+        copy.wait()
+        part = dot(fc_in_ref[:, cut], images_ref[:, cut], 1, 1)
+        pre_act = part if pre_act is None else pre_act + part
     square = pre_act * pre_act
     bent = jnp.tanh(GELU_SCALE * pre_act * (1.0 + GELU_CUBIC * square))
     activation = (0.5 * pre_act * (1.0 + bent)).astype(jnp.bfloat16)
     slope_ref[...] = 0.5 * (1.0 + bent) + (
         0.5 * GELU_SCALE * pre_act * (1.0 - bent * bent) * (1.0 + 3.0 * GELU_CUBIC * square)
     )
-    image_term[...] = dot(activation, fc_out_ref[...], 0, 0)
+    for cut, copy in zip(cuts, copies[3 + CUTS :]):
+        copy.wait()
+        image_term[:, cut] = dot(activation, fc_out_ref[:, cut], 0, 0)
     for first, term in ((0, image_term), (HALF, text_term)):
         kept_ref[first : first + HALF] = own_half(term, core)
         sent_ref[first : first + HALF] = own_half(term, 1 - core).astype(jnp.bfloat16)
@@ -143,26 +166,26 @@
     image_grad = grads_ref[:, :HALF].reshape(rows, width + LANES)
     text_grad = grads_ref[:, HALF:].reshape(rows, width + LANES)
     losses = jnp.sum(image_grad[:, width:].astype(jnp.float32), axis=1, keepdims=True)
-    loss_ref[...] = jnp.broadcast_to(losses, (rows, LANES)).T / (WINDOW * rows)
+    loss_ref[...] = jnp.broadcast_to(losses, (rows, LANES)).T[:1] / (WINDOW * rows)
     act_grad = dot(fc_out_ref[...], image_grad[:, :width], 1, 1)
     hidden_ref[...] = (slope_ref[...] * act_grad).astype(jnp.bfloat16)
     text_ref[...] = dot(head_ref[...], text_grad[:, :width], 1, 1).astype(jnp.bfloat16)
 
 
-def kernel(body, outs, scratch=(), places=""):
-    spaces = dict(s=pltpu.SMEM, v=pltpu.VMEM)
+def kernel(body, outs, scratch=(), places="", vmem=24):
+    spaces = dict(s=pltpu.SMEM, v=pltpu.VMEM, h=pltpu.HBM)
     return pl.pallas_call(
         body,
         out_shape=[jax.ShapeDtypeStruct(shape, dtype) for shape, dtype in outs],
         in_specs=[pl.BlockSpec(memory_space=spaces[place]) for place in places],
         out_specs=[pl.BlockSpec(memory_space=pltpu.VMEM) for unused in outs],
         scratch_shapes=list(scratch),
-        compiler_params=pltpu.CompilerParams(vmem_limit_bytes=24 * 1024 * 1024),
-    )
-
-
-def chip_gather(kept, sent):
-    got = lax.ppermute(sent, "core", [(0, 1), (1, 0)])
+        compiler_params=pltpu.CompilerParams(vmem_limit_bytes=vmem * 1024 * 1024),
+    )
+
+
+def chip_gather(kept, sent, core):
+    got = lax.dynamic_index_in_dim(lax.all_gather(sent, "core"), 1 - core[0], 0, False)
     return lax.all_gather((kept + got.astype(jnp.float32)).astype(jnp.bfloat16), "y_hi")
 
 
@@ -178,25 +201,32 @@
         heads_kernel,
         [((hidden, rows), f32), ((rows, width), f32), ((rows, width), bf16)],
         [
+            pltpu.VMEM((features, rows), bf16),
+            pltpu.VMEM((features, width), bf16),
+            pltpu.VMEM((rows, width), bf16),
+            pltpu.VMEM((hidden, width), bf16),
+            pltpu.VMEM((hidden, width), bf16),
             pltpu.VMEM((rows, width), f32),
             pltpu.VMEM((rows, width), f32),
+            pltpu.SemaphoreType.DMA((3 + 2 * CUTS,)),
         ],
-        "svvvvv",
-    )(core, images, texts.T, fc_in.T, fc_out, head)
+        "shhhhh",
+        vmem=HEADS_VMEM,
+    )(core, texts.T, head, images, fc_in.T, fc_out)
 
     unit, inverse, unit_sent = kernel(
         unit_kernel,
         [((rows, width), f32), ((rows, LANES), f32), ((rows, width), bf16)],
         places="svv",
-    )(core, chip_gather(kept, sent), images)
+    )(core, chip_gather(kept, sent, core), images)
 
     units = lax.all_gather(unit_sent, "core")
     image_own = units[:, :HALF].reshape(rows, width)
     text_own = units[:, HALF:].reshape(rows, width)
-    far_text = move(text_own, lambda role: OFFSET[role] + NEAR)
-    far_image = move(image_own, lambda role: -OFFSET[role] - NEAR)
     near_text = move(text_own, lambda role: OFFSET[role])
     near_image = move(image_own, lambda role: -OFFSET[role])
+    far_text = move(near_text, lambda role: NEAR)
+    far_image = move(near_image, lambda role: -NEAR)
 
     paired = jnp.where(role == 0, partner, -1)
     columns = width + LANES
@@ -211,14 +241,14 @@
     )
 
     (grads,) = kernel(tangent_kernel, [((rows, columns), bf16)], places="vvv")(
-        chip_gather(kept, sent), unit, inverse
+        chip_gather(kept, sent, core), unit, inverse
     )
     hidden_grad, text_grad, loss = kernel(
         backward_kernel,
-        [((hidden, rows), bf16), ((features, rows), bf16), ((rows, rows), f32)],
+        [((hidden, rows), bf16), ((features, rows), bf16), ((1, rows), f32)],
         places="vvvv",
     )(lax.all_gather(grads, "core"), slope, fc_out, head)
-    return (hidden_grad.T, text_grad.T, loss[0])
+    return (hidden_grad.T, text_grad.T, loss.reshape(rows))
 
 
 def solution(mesh):

time: 116 us -> 109 us (0.940)
  the two profiles are of different devices: /device:TPU:1 before, /device:TPU:3 now
where the time goes in v5:
time: 109 us
  blocking collectives  39.7 us (36%)
  starting transfers between devices  33.4 us (31%)
  waiting for transfers between devices  24.7 us (23%)
  Pallas kernels  9.02 us (8%)
  other arithmetic  1.2 us (1%)
    ppermute x4, starting transfers between devices, move(): return lax.ppermute(value, AXES, moves(shift))  33.4 us
    all_gather x2, blocking collectives, chip_gather(): lax.all_gather((kept + got.astype(jnp.float32)).astype(jnp.bfloat16), 'y_...  28.7 us
    ppermute x4, waiting for transfers between devices, move(): return lax.ppermute(value, AXES, moves(shift))  24.7 us
    all_gather x2, blocking collectives, chip_gather(): lax.all_gather(sent, 'core')  5.16 us
    pallas_call x1, Pallas kernels, local(): kernel(heads_kernel, [((hidden, rows), f32), ((rows, width), f32), ((rows...  4.96 us
    all_gather x1, blocking collectives, local(): units = lax.all_gather(unit_sent, 'core')  2.99 us
    all_gather x1, blocking collectives, local(): lax.all_gather(grads, 'core')  2.86 us
  transfers between devices with their start and end apart: 4, of which 3 were waited for; matrix products, arithmetic and copies ran while one was open for 0% of the time, Pallas kernels for 0%

profile of v5, /device:TPU:3, one launch (start us, length us, event | category | flops | bytes accessed | tf_op | source)
XLA Modules:
  0.0 109.0 jit_solution(7807225464622513992)
XLA Ops:
  0.6 5.0 %shard_map.85 = (f32[1076,128]{1,0:T(8,128)}, f32[128,1152]{1,0:T(8,128)}, bf16[128,1152]{1,0:T(8,128)(2,1)}) custom-call(s32[1]{0:T(128)} %bitcast.core_ref, bf16[288,128]{1,0:T(8,128)(2,1)} %bitcast.35, bf16[288,1152]{1,0:T(8,128)(2,1)} %head_ref.1, bf16[128,1152]{1,0:T(8,128)(2,1)} %images_ref.1, bf16[1076,1152]{1,0:T(8,128)(2,1)} %bitcast.31, ...), custom_call_target="tpu_custom_call" | custom-call | tf_op jit(solution)/shard_map/pallas_call | solution.py:200
  5.6 0.0 copy-start.2
  5.6 2.9 %all-gather = bf16[256,1152]{1,0:T(8,128)(2,1)S(1)} all-gather(bf16[128,1152]{1,0:T(8,128)(2,1)} %get-tuple-element.15), channel_id=2, replica_groups=mesh['z'=16,'y_lo'=4,'x'=4,'y_hi'=2,'core'=2] {'core'}, dimensions={0}, use_global_device_ids=true | all-gather | bytes 884736 | tf_op jit(solution)/shard_map/all_gather | solution.py:188
  8.5 1.1 %fusion.1 = bf16[128,1152]{1,0:T(8,128)(2,1)S(1)} fusion(f32[128,1152]{1,0:T(8,128)} %get-tuple-element.14, bf16[2,128,1152]{2,1,0:T(8,128)(2,1)S(1)} %bitcast.34, s32[]{:T(128)S(6)} %select_n.14), kind=kLoop, calls=%fused_computation.3 | loop fusion | flops 442368 | bytes 1179652 | tf_op jit(solution)/shard_map/convert_element_type | solution.py:189
  9.6 14.9 %all-gather.1 = bf16[256,1152]{1,0:T(8,128)(2,1)S(1)} all-gather(bf16[128,1152]{1,0:T(8,128)(2,1)S(1)} %fusion.1), channel_id=3, replica_groups=mesh['z'=16,'y_lo'=4,'x'=4,'y_hi'=2,'core'=2] {'y_hi'}, dimensions={0}, use_global_device_ids=true | all-gather | bytes 884736 | tf_op jit(solution)/shard_map/all_gather | solution.py:189
  24.5 0.2 shard_map.86
  24.7 3.0 %all-gather.2 = bf16[256,1152]{1,0:T(8,128)(2,1)S(1)} all-gather(bf16[128,1152]{1,0:T(8,128)(2,1)S(1)} %get-tuple-element.16), channel_id=4, replica_groups=mesh['z'=16,'y_lo'=4,'x'=4,'y_hi'=2,'core'=2] {'core'}, dimensions={0}, use_global_device_ids=true | all-gather | bytes 884736 | tf_op jit(solution)/shard_map/all_gather | solution.py:223
  27.7 26.8 %collective-permute-start.2 = (bf16[128,1152]{1,0:T(8,128)(2,1)S(1)}, bf16[128,1152]{1,0:T(8,128)(2,1)S(1)}, u32[]{:S(2)}, u32[]{:S(2)}) collective-permute-start(bf16[128,1152]{1,0:T(8,128)(2,1)S(1)} %bitcast.29), channel_id=1, source_target_pairs={{0,0},{1,1019},{2,1020},{3,1013},{4,4},{5,1023},{6,2},{7,1017},{8,... | collective-permute-start | bytes 884744 | tf_op jit(solution)/shard_map/ppermute | solution.py:44
  54.5 1.9 %collective-permute-start = (bf16[128,1152]{1,0:T(8,128)(2,1)S(1)}, bf16[128,1152]{1,0:T(8,128)(2,1)S(1)}, u32[]{:S(2)}, u32[]{:S(2)}) collective-permute-start(bf16[128,1152]{1,0:T(8,128)(2,1)S(1)} %bitcast.27), channel_id=1, source_target_pairs={{0,0},{1,9},{2,6},{3,15},{4,4},{5,13},{6,10},{7,19},{8,8},{9,17},{... | collective-permute-start | bytes 884744 | tf_op jit(solution)/shard_map/ppermute | solution.py:44
  56.5 4.3 %collective-permute-done.2.near_image_ref = bf16[128,1152]{1,0:T(8,128)(2,1)S(1)} collective-permute-done((bf16[128,1152]{1,0:T(8,128)(2,1)S(1)}, bf16[128,1152]{1,0:T(8,128)(2,1)S(1)}, u32[]{:S(2)}, u32[]{:S(2)}) %collective-permute-start.2) | collective-permute-done | bytes 294944 | tf_op jit(solution)/shard_map/ppermute | solution.py:44
  60.7 2.7 %collective-permute-start.3 = (bf16[128,1152]{1,0:T(8,128)(2,1)S(1)}, bf16[128,1152]{1,0:T(8,128)(2,1)S(1)}, u32[]{:S(2)}, u32[]{:S(2)}) collective-permute-start(bf16[128,1152]{1,0:T(8,128)(2,1)S(1)} %collective-permute-done.2.near_image_ref), channel_id=1, source_target_pairs={{0,1010},{1,1011},{2,1008},{3,1009},{4,1014},{5,1015},{6,1012},{7,... | collective-permute-start | bytes 884744 | tf_op jit(solution)/shard_map/ppermute | solution.py:44
  63.5 9.4 %collective-permute-done.near_text_ref = bf16[128,1152]{1,0:T(8,128)(2,1)S(1)} collective-permute-done((bf16[128,1152]{1,0:T(8,128)(2,1)S(1)}, bf16[128,1152]{1,0:T(8,128)(2,1)S(1)}, u32[]{:S(2)}, u32[]{:S(2)}) %collective-permute-start) | collective-permute-done | bytes 294944 | tf_op jit(solution)/shard_map/ppermute | solution.py:44
  72.9 1.9 %collective-permute-start.1 = (bf16[128,1152]{1,0:T(8,128)(2,1)S(1)}, bf16[128,1152]{1,0:T(8,128)(2,1)S(1)}, u32[]{:S(2)}, u32[]{:S(2)}) collective-permute-start(bf16[128,1152]{1,0:T(8,128)(2,1)S(1)} %collective-permute-done.near_text_ref), channel_id=1, source_target_pairs={{0,16},{1,17},{2,18},{3,19},{4,20},{5,21},{6,22},{7,23},{8,24},{9,... | collective-permute-start | bytes 884744 | tf_op jit(solution)/shard_map/ppermute | solution.py:44
  74.9 0.1 copy.9.column_ref
  75.0 0.0 collective-permute-done.3.far_image_ref
  75.0 11.1 %collective-permute-done.1.far_text_ref = bf16[128,1152]{1,0:T(8,128)(2,1)S(1)} collective-permute-done((bf16[128,1152]{1,0:T(8,128)(2,1)S(1)}, bf16[128,1152]{1,0:T(8,128)(2,1)S(1)}, u32[]{:S(2)}, u32[]{:S(2)}) %collective-permute-start.1) | collective-permute-done | bytes 294944 | tf_op jit(solution)/shard_map/ppermute | solution.py:44
  86.0 1.8 %shard_map.87 = (f32[128,1280]{1,0:T(8,128)S(1)}, bf16[128,1280]{1,0:T(8,128)(2,1)S(1)}) custom-call(s32[1]{0:T(128)} %bitcast.core_ref, bf16[128,1152]{1,0:T(8,128)(2,1)S(1)} %bitcast.30, bf16[128,1152]{1,0:T(8,128)(2,1)S(1)} %bitcast.28, bf16[128,1152]{1,0:T(8,128)(2,1)S(1)} %collective-permute-done.near_text_ref, ...), custom_call_target="tpu_custom_call" | custom-call | tf_op jit(solution)/shard_map/pallas_call | solution.py:233
  87.8 2.3 %all-gather.3 = bf16[256,1280]{1,0:T(8,128)(2,1)S(1)} all-gather(bf16[128,1280]{1,0:T(8,128)(2,1)S(1)} %get-tuple-element.18), channel_id=5, replica_groups=mesh['z'=16,'y_lo'=4,'x'=4,'y_hi'=2,'core'=2] {'core'}, dimensions={0}, use_global_device_ids=true | all-gather | bytes 983040 | tf_op jit(solution)/shard_map/all_gather | solution.py:188
  90.1 0.1 fusion
  90.2 13.9 %all-gather.4 = bf16[256,1280]{1,0:T(8,128)(2,1)S(1)} all-gather(bf16[128,1280]{1,0:T(8,128)(2,1)S(1)} %fusion), channel_id=6, replica_groups=mesh['z'=16,'y_lo'=4,'x'=4,'y_hi'=2,'core'=2] {'y_hi'}, dimensions={0}, use_global_device_ids=true | all-gather | bytes 983040 | tf_op jit(solution)/shard_map/all_gather | solution.py:189
  104.1 0.3 shard_map.88
  104.4 2.9 %all-gather.5 = bf16[256,1280]{1,0:T(8,128)(2,1)S(1)} all-gather(bf16[128,1280]{1,0:T(8,128)(2,1)S(1)} %shard_map.88), channel_id=7, replica_groups=mesh['z'=16,'y_lo'=4,'x'=4,'y_hi'=2,'core'=2] {'core'}, dimensions={0}, use_global_device_ids=true | all-gather | bytes 983040 | tf_op jit(solution)/shard_map/all_gather | solution.py:250
  107.3 0.0 copy-done
  107.3 1.7 %shard_map.89 = (bf16[1076,128]{1,0:T(8,128)(2,1)}, bf16[288,128]{1,0:T(8,128)(2,1)}, f32[1,128]{1,0:T(1,128)}) custom-call(bf16[2,128,1280]{2,1,0:T(8,128)(2,1)S(1)} %bitcast.25, f32[1076,128]{1,0:T(8,128)S(1)} %copy-done.3, bf16[1076,1152]{1,0:T(8,128)(2,1)S(1)} %copy-done, bf16[288,1152]{1,0:T(8,128)(2,1)S(1)} %copy-done.1), custom_call_target="tpu_custom_call" | custom-call | tf_op jit(solution)/shard_map/pallas_call | solution.py:246
  (10 shorter events, 0.1 us)
Async XLA Ops:
  5.6 18.9 %copy-start.2 = (bf16[128,1152]{1,0:T(8,128)(2,1)S(1)}, bf16[128,1152]{1,0:T(8,128)(2,1)}, u32[]{:S(2)}) copy-start(bf16[128,1152]{1,0:T(8,128)(2,1)} %images_ref.1) | copy-start | bytes 884740
  8.5 66.3 %copy-start.4 = (s32[128]{0:T(128)S(1)}, s32[128]{0:T(128)}, u32[]{:S(2)}) copy-start(s32[128]{0:T(128)} %param.11) | copy-start | bytes 1540
  27.7 33.0 %collective-permute-start.2 = (bf16[128,1152]{1,0:T(8,128)(2,1)S(1)}, bf16[128,1152]{1,0:T(8,128)(2,1)S(1)}, u32[]{:S(2)}, u32[]{:S(2)}) collective-permute-start(bf16[128,1152]{1,0:T(8,128)(2,1)S(1)} %bitcast.29), channel_id=1, source_target_pairs={{0,0},{1,1019},{2,1020},{3,1013},{4,4},{5,1023},{6,2},{7,1017},{8,... | collective-permute-start | bytes 884744 | tf_op jit(solution)/shard_map/ppermute | solution.py:44
  54.5 18.4 %collective-permute-start = (bf16[128,1152]{1,0:T(8,128)(2,1)S(1)}, bf16[128,1152]{1,0:T(8,128)(2,1)S(1)}, u32[]{:S(2)}, u32[]{:S(2)}) collective-permute-start(bf16[128,1152]{1,0:T(8,128)(2,1)S(1)} %bitcast.27), channel_id=1, source_target_pairs={{0,0},{1,9},{2,6},{3,15},{4,4},{5,13},{6,10},{7,19},{8,8},{9,17},{... | collective-permute-start | bytes 884744 | tf_op jit(solution)/shard_map/ppermute | solution.py:44
  60.7 14.2 %collective-permute-start.3 = (bf16[128,1152]{1,0:T(8,128)(2,1)S(1)}, bf16[128,1152]{1,0:T(8,128)(2,1)S(1)}, u32[]{:S(2)}, u32[]{:S(2)}) collective-permute-start(bf16[128,1152]{1,0:T(8,128)(2,1)S(1)} %collective-permute-done.2.near_image_ref), channel_id=1, source_target_pairs={{0,1010},{1,1011},{2,1008},{3,1009},{4,1014},{5,1015},{6,1012},{7,... | collective-permute-start | bytes 884744 | tf_op jit(solution)/shard_map/ppermute | solution.py:44
  72.9 13.1 %collective-permute-start.1 = (bf16[128,1152]{1,0:T(8,128)(2,1)S(1)}, bf16[128,1152]{1,0:T(8,128)(2,1)S(1)}, u32[]{:S(2)}, u32[]{:S(2)}) collective-permute-start(bf16[128,1152]{1,0:T(8,128)(2,1)S(1)} %collective-permute-done.near_text_ref), channel_id=1, source_target_pairs={{0,16},{1,17},{2,18},{3,19},{4,20},{5,21},{6,22},{7,23},{8,24},{9,... | collective-permute-start | bytes 884744 | tf_op jit(solution)/shard_map/ppermute | solution.py:44
  90.1 17.2 %copy-start = (bf16[1076,1152]{1,0:T(8,128)(2,1)S(1)}, bf16[1076,1152]{1,0:T(8,128)(2,1)}, u32[]{:S(2)}) copy-start(bf16[1076,1152]{1,0:T(8,128)(2,1)} %fc_out_ref.1) | copy-start | bytes 7437316
  90.1 17.2 %copy-start.1 = (bf16[288,1152]{1,0:T(8,128)(2,1)S(1)}, bf16[288,1152]{1,0:T(8,128)(2,1)}, u32[]{:S(2)}) copy-start(bf16[288,1152]{1,0:T(8,128)(2,1)} %head_ref.1) | copy-start | bytes 1990660
  90.1 17.2 %copy-start.3 = (f32[1076,128]{1,0:T(8,128)S(1)}, f32[1076,128]{1,0:T(8,128)}, u32[]{:S(2)}) copy-start(f32[1076,128]{1,0:T(8,128)} %get-tuple-element.21.slope_ref) | copy-start | bytes 1652740

commit v6 on v5

--- a/solution.py
+++ b/solution.py
@@ -94,7 +94,9 @@
         sent_ref[first : first + HALF] = own_half(term, 1 - core).astype(jnp.bfloat16)
 
 
-def unit_kernel(core_ref, chips_ref, images_ref, unit_ref, inverse_ref, sent_ref):
+def unit_kernel(
+    core_ref, chips_ref, images_ref, unit_ref, inverse_ref, image_sent_ref, text_sent_ref
+):
     embed = chips_ref[0].astype(jnp.float32) + chips_ref[1].astype(jnp.float32)
     image_embed = own_half(images_ref, core_ref[0]).astype(jnp.float32) + embed[:HALF]
     for first, rows in ((0, image_embed), (HALF, embed[HALF:])):
@@ -102,7 +104,8 @@
         unit = rows * inverse
         unit_ref[first : first + HALF] = unit
         inverse_ref[first : first + HALF] = jnp.broadcast_to(inverse, (HALF, LANES))
-        sent_ref[first : first + HALF] = unit.astype(jnp.bfloat16)
+        sent = text_sent_ref if first else image_sent_ref
+        sent[...] = unit.astype(jnp.bfloat16)
 
 
 def split_loss(loss):
@@ -127,25 +130,35 @@
     return logit_scale * dot(pair_grad.astype(jnp.bfloat16), others, 1, 0), loss
 
 
-def score_kernel(
-    core_ref, image_ref, text_ref, near_text_ref, far_text_ref, near_image_ref, far_image_ref,
-    column_ref, row_ref, kept_ref, sent_ref, image_part, text_part,
+def image_kernel(
+    core_ref, own_ref, near_ref, far_ref, column_ref, kept_ref, sent_ref, part_ref
 ):
     core = core_ref[0]
-    rows, width = image_ref.shape
+    rows, width = own_ref.shape
     across = lax.broadcasted_iota(jnp.int32, (rows, rows), 1)
+    near, near_loss = pair_terms(own_ref[...], near_ref[...], across == column_ref[...])
+    far, far_loss = pair_terms(own_ref[...], far_ref[...], None)
+    part_ref[:, :width] = near + far
+    part_ref[:, width:] = split_loss(jnp.sum(near_loss + far_loss, axis=1, keepdims=True))
+    kept_ref[...] = own_half(part_ref, core)
+    sent_ref[...] = own_half(part_ref, 1 - core).astype(jnp.bfloat16)
+
+
+def text_kernel(
+    core_ref, own_ref, near_ref, far_ref, row_ref, image_kept_ref, image_sent_ref,
+    kept_ref, sent_ref, part_ref,
+):
+    core = core_ref[0]
+    rows, width = own_ref.shape
     down = lax.broadcasted_iota(jnp.int32, (rows, rows), 0)
-    near, near_loss = pair_terms(image_ref[...], near_text_ref[...], across == column_ref[...])
-    far, far_loss = pair_terms(image_ref[...], far_text_ref[...], None)
-    image_part[:, :width] = near + far
-    image_part[:, width:] = split_loss(jnp.sum(near_loss + far_loss, axis=1, keepdims=True))
-    near, unused = pair_terms(text_ref[...], near_image_ref[...], down == row_ref[...])
-    far, unused = pair_terms(text_ref[...], far_image_ref[...], None)
-    text_part[:, :width] = near + far
-    text_part[:, width:] = jnp.zeros((rows, LANES), jnp.float32)
-    for first, part in ((0, image_part), (HALF, text_part)):
-        kept_ref[first : first + HALF] = own_half(part, core)
-        sent_ref[first : first + HALF] = own_half(part, 1 - core).astype(jnp.bfloat16)
+    near, unused = pair_terms(own_ref[...], near_ref[...], down == row_ref[...])
+    far, unused = pair_terms(own_ref[...], far_ref[...], None)
+    part_ref[:, :width] = near + far
+    part_ref[:, width:] = jnp.zeros((rows, LANES), jnp.float32)
+    kept_ref[:HALF] = image_kept_ref[...]
+    sent_ref[:HALF] = image_sent_ref[...]
+    kept_ref[HALF:] = own_half(part_ref, core)
+    sent_ref[HALF:] = own_half(part_ref, 1 - core).astype(jnp.bfloat16)
 
 
 def tangent_kernel(chips_ref, unit_ref, inverse_ref, sent_ref):
@@ -214,31 +227,29 @@
         vmem=HEADS_VMEM,
     )(core, texts.T, head, images, fc_in.T, fc_out)
 
-    unit, inverse, unit_sent = kernel(
+    unit, inverse, *unit_sent = kernel(
         unit_kernel,
-        [((rows, width), f32), ((rows, LANES), f32), ((rows, width), bf16)],
+        [((rows, width), f32), ((rows, LANES), f32)] + [((HALF, width), bf16)] * 2,
         places="svv",
     )(core, chip_gather(kept, sent, core), images)
 
-    units = lax.all_gather(unit_sent, "core")
-    image_own = units[:, :HALF].reshape(rows, width)
-    text_own = units[:, HALF:].reshape(rows, width)
+    text_own = lax.all_gather(unit_sent[1], "core", tiled=True)
+    text_own, image_sent = lax.optimization_barrier((text_own, unit_sent[0]))
     near_text = move(text_own, lambda role: OFFSET[role])
+    image_own = lax.all_gather(image_sent, "core", tiled=True)
     near_image = move(image_own, lambda role: -OFFSET[role])
     far_text = move(near_text, lambda role: NEAR)
     far_image = move(near_image, lambda role: -NEAR)
 
     paired = jnp.where(role == 0, partner, -1)
     columns = width + LANES
+    part = [pltpu.VMEM((rows, columns), f32)]
+    image_parts = kernel(
+        image_kernel, [((HALF, columns), f32), ((HALF, columns), bf16)], part, "svvvv"
+    )(core, image_own, near_text, far_text, paired.reshape(rows, 1))
     kept, sent = kernel(
-        score_kernel,
-        [((rows, columns), f32), ((rows, columns), bf16)],
-        [pltpu.VMEM((rows, columns), f32), pltpu.VMEM((rows, columns), f32)],
-        "svvvvvvvv",
-    )(
-        core, image_own, text_own, near_text, far_text, near_image, far_image,
-        paired.reshape(rows, 1), paired.reshape(1, rows),
-    )
+        text_kernel, [((rows, columns), f32), ((rows, columns), bf16)], part, "svvvvvv"
+    )(core, text_own, near_image, far_image, paired.reshape(1, rows), *image_parts)
 
     (grads,) = kernel(tangent_kernel, [((rows, columns), bf16)], places="vvv")(
         chip_gather(kept, sent, core), unit, inverse

time: 109 us -> 102 us (0.936)
  the two profiles are of different devices: /device:TPU:3 before, /device:TPU:1 now
where the time goes in v6:
time: 102 us
  blocking collectives  59.4 us (58%)
  starting transfers between devices  26.4 us (26%)
  Pallas kernels  9.23 us (9%)
  waiting for transfers between devices  4.78 us (5%)
  other arithmetic  1.19 us (1%)
    all_gather x2, blocking collectives, chip_gather(): lax.all_gather((kept + got.astype(jnp.float32)).astype(jnp.bfloat16), 'y_...  33.1 us
    ppermute x4, starting transfers between devices, move(): return lax.ppermute(value, AXES, moves(shift))  26.4 us
    all_gather x2, blocking collectives, chip_gather(): lax.all_gather(sent, 'core')  18.6 us
    pallas_call x1, Pallas kernels, local(): kernel(heads_kernel, [((hidden, rows), f32), ((rows, width), f32), ((rows...  4.97 us
    ppermute x4, waiting for transfers between devices, move(): return lax.ppermute(value, AXES, moves(shift))  4.78 us
    all_gather x1, blocking collectives, local(): text_own = lax.all_gather(unit_sent[1], 'core', tiled=True)  2.85 us
    all_gather x1, blocking collectives, local(): lax.all_gather(grads, 'core')  2.79 us
  transfers between devices with their start and end apart: 4, of which 3 were waited for; matrix products, arithmetic and copies ran while one was open for 0% of the time, Pallas kernels for 1%

profile of v6, /device:TPU:1, one launch (start us, length us, event | category | flops | bytes accessed | tf_op | source)
XLA Modules:
  0.0 101.9 jit_solution(16591705490726124483)
XLA Ops:
  0.6 5.0 %shard_map.85 = (f32[1076,128]{1,0:T(8,128)}, f32[128,1152]{1,0:T(8,128)}, bf16[128,1152]{1,0:T(8,128)(2,1)}) custom-call(s32[1]{0:T(128)} %bitcast.core_ref, bf16[288,128]{1,0:T(8,128)(2,1)} %bitcast.27, bf16[288,1152]{1,0:T(8,128)(2,1)} %head_ref.1, bf16[128,1152]{1,0:T(8,128)(2,1)} %images_ref.1, bf16[1076,1152]{1,0:T(8,128)(2,1)} %bitcast.24, ...), custom_call_target="tpu_custom_call" | custom-call | tf_op jit(solution)/shard_map/pallas_call | solution.py:213
  5.6 0.0 copy-start.2
  5.6 16.4 %all-gather = bf16[256,1152]{1,0:T(8,128)(2,1)S(1)} all-gather(bf16[128,1152]{1,0:T(8,128)(2,1)} %get-tuple-element.20), channel_id=2, replica_groups=mesh['z'=16,'y_lo'=4,'x'=4,'y_hi'=2,'core'=2] {'core'}, dimensions={0}, use_global_device_ids=true | all-gather | bytes 884736 | tf_op jit(solution)/shard_map/all_gather | solution.py:201
  22.0 1.1 %fusion.1 = bf16[128,1152]{1,0:T(8,128)(2,1)S(1)} fusion(f32[128,1152]{1,0:T(8,128)} %get-tuple-element.19, bf16[2,128,1152]{2,1,0:T(8,128)(2,1)S(1)} %bitcast.26, s32[]{:T(128)S(6)} %select_n.14), kind=kLoop, calls=%fused_computation.3 | loop fusion | flops 442368 | bytes 1179652 | tf_op jit(solution)/shard_map/convert_element_type | solution.py:202
  23.1 12.8 %all-gather.1 = bf16[256,1152]{1,0:T(8,128)(2,1)S(1)} all-gather(bf16[128,1152]{1,0:T(8,128)(2,1)S(1)} %fusion.1), channel_id=3, replica_groups=mesh['z'=16,'y_lo'=4,'x'=4,'y_hi'=2,'core'=2] {'y_hi'}, dimensions={0}, use_global_device_ids=true | all-gather | bytes 884736 | tf_op jit(solution)/shard_map/all_gather | solution.py:202
  35.9 0.2 shard_map.86
  36.1 2.9 %all_gather.40.own_ref = bf16[128,1152]{1,0:T(8,128)(2,1)S(1)} all-gather(bf16[64,1152]{1,0:T(8,128)(2,1)S(1)} %get-tuple-element.21), channel_id=1, replica_groups=mesh['z'=16,'y_lo'=4,'x'=4,'y_hi'=2,'core'=2] {'core'}, dimensions={0}, use_global_device_ids=true | all-gather | bytes 442368 | tf_op jit(solution)/shard_map/all_gather | solution.py:236
  39.0 1.9 %collective-permute-start.2 = (bf16[128,1152]{1,0:T(8,128)(2,1)S(1)}, bf16[128,1152]{1,0:T(8,128)(2,1)S(1)}, u32[]{:S(2)}, u32[]{:S(2)}) collective-permute-start(bf16[128,1152]{1,0:T(8,128)(2,1)S(1)} %all_gather.40.own_ref), channel_id=1, source_target_pairs={{0,0},{1,9},{2,6},{3,15},{4,4},{5,13},{6,10},{7,19},{8,8},{9,17},{... | collective-permute-start | bytes 884744 | tf_op jit(solution)/shard_map/ppermute | solution.py:44
  40.9 2.0 %all_gather.41.own_ref = bf16[128,1152]{1,0:T(8,128)(2,1)S(1)} all-gather(bf16[64,1152]{1,0:T(8,128)(2,1)S(1)} %get-tuple-element.24), channel_id=1, replica_groups=mesh['z'=16,'y_lo'=4,'x'=4,'y_hi'=2,'core'=2] {'core'}, dimensions={0}, use_global_device_ids=true | all-gather | bytes 442368 | tf_op jit(solution)/shard_map/all_gather | solution.py:239
  42.9 17.0 %collective-permute-start = (bf16[128,1152]{1,0:T(8,128)(2,1)S(1)}, bf16[128,1152]{1,0:T(8,128)(2,1)S(1)}, u32[]{:S(2)}, u32[]{:S(2)}) collective-permute-start(bf16[128,1152]{1,0:T(8,128)(2,1)S(1)} %all_gather.41.own_ref), channel_id=1, source_target_pairs={{0,0},{1,1019},{2,1020},{3,1013},{4,4},{5,1023},{6,2},{7,1017},{8,... | collective-permute-start | bytes 884744 | tf_op jit(solution)/shard_map/ppermute | solution.py:44
  59.9 0.2 collective-permute-done.2.near_ref
  60.1 1.9 %collective-permute-start.3 = (bf16[128,1152]{1,0:T(8,128)(2,1)S(1)}, bf16[128,1152]{1,0:T(8,128)(2,1)S(1)}, u32[]{:S(2)}, u32[]{:S(2)}) collective-permute-start(bf16[128,1152]{1,0:T(8,128)(2,1)S(1)} %collective-permute-done.2.near_ref), channel_id=1, source_target_pairs={{0,16},{1,17},{2,18},{3,19},{4,20},{5,21},{6,22},{7,23},{8,24},{9,... | collective-permute-start | bytes 884744 | tf_op jit(solution)/shard_map/ppermute | solution.py:44
  62.0 1.6 %collective-permute-done.near_ref = bf16[128,1152]{1,0:T(8,128)(2,1)S(1)} collective-permute-done((bf16[128,1152]{1,0:T(8,128)(2,1)S(1)}, bf16[128,1152]{1,0:T(8,128)(2,1)S(1)}, u32[]{:S(2)}, u32[]{:S(2)}) %collective-permute-start) | collective-permute-done | bytes 294944 | tf_op jit(solution)/shard_map/ppermute | solution.py:44
  63.6 5.6 %collective-permute-start.1 = (bf16[128,1152]{1,0:T(8,128)(2,1)S(1)}, bf16[128,1152]{1,0:T(8,128)(2,1)S(1)}, u32[]{:S(2)}, u32[]{:S(2)}) collective-permute-start(bf16[128,1152]{1,0:T(8,128)(2,1)S(1)} %collective-permute-done.near_ref), channel_id=1, source_target_pairs={{0,1010},{1,1011},{2,1008},{3,1009},{4,1014},{5,1015},{6,1012},{7,... | collective-permute-start | bytes 884744 | tf_op jit(solution)/shard_map/ppermute | solution.py:44
  69.2 0.1 copy.9.column_ref
  69.3 3.1 %collective-permute-done.3.far_ref = bf16[128,1152]{1,0:T(8,128)(2,1)S(1)} collective-permute-done((bf16[128,1152]{1,0:T(8,128)(2,1)S(1)}, bf16[128,1152]{1,0:T(8,128)(2,1)S(1)}, u32[]{:S(2)}, u32[]{:S(2)}) %collective-permute-start.3) | collective-permute-done | bytes 294944 | tf_op jit(solution)/shard_map/ppermute | solution.py:44
  72.4 1.0 shard_map.87
  73.4 1.0 shard_map.88
  74.4 2.3 %all-gather.2 = bf16[256,1280]{1,0:T(8,128)(2,1)S(1)} all-gather(bf16[128,1280]{1,0:T(8,128)(2,1)S(1)} %get-tuple-element.28), channel_id=4, replica_groups=mesh['z'=16,'y_lo'=4,'x'=4,'y_hi'=2,'core'=2] {'core'}, dimensions={0}, use_global_device_ids=true | all-gather | bytes 983040 | tf_op jit(solution)/shard_map/all_gather | solution.py:201
  76.7 0.1 fusion
  76.7 20.3 %all-gather.3 = bf16[256,1280]{1,0:T(8,128)(2,1)S(1)} all-gather(bf16[128,1280]{1,0:T(8,128)(2,1)S(1)} %fusion), channel_id=5, replica_groups=mesh['z'=16,'y_lo'=4,'x'=4,'y_hi'=2,'core'=2] {'y_hi'}, dimensions={0}, use_global_device_ids=true | all-gather | bytes 983040 | tf_op jit(solution)/shard_map/all_gather | solution.py:202
  97.0 0.3 shard_map.89
  97.4 2.8 %all-gather.4 = bf16[256,1280]{1,0:T(8,128)(2,1)S(1)} all-gather(bf16[128,1280]{1,0:T(8,128)(2,1)S(1)} %shard_map.89), channel_id=6, replica_groups=mesh['z'=16,'y_lo'=4,'x'=4,'y_hi'=2,'core'=2] {'core'}, dimensions={0}, use_global_device_ids=true | all-gather | bytes 983040 | tf_op jit(solution)/shard_map/all_gather | solution.py:261
  100.2 1.7 %shard_map.90 = (bf16[1076,128]{1,0:T(8,128)(2,1)}, bf16[288,128]{1,0:T(8,128)(2,1)}, f32[1,128]{1,0:T(1,128)}) custom-call(bf16[2,128,1280]{2,1,0:T(8,128)(2,1)S(1)} %bitcast.22, f32[1076,128]{1,0:T(8,128)S(1)} %copy-done.3, bf16[1076,1152]{1,0:T(8,128)(2,1)S(1)} %copy-done, bf16[288,1152]{1,0:T(8,128)(2,1)S(1)} %copy-done.1), custom_call_target="tpu_custom_call" | custom-call | tf_op jit(solution)/shard_map/pallas_call | solution.py:257
  (11 shorter events, 0.0 us)
Async XLA Ops:
  5.6 30.3 %copy-start.2 = (bf16[128,1152]{1,0:T(8,128)(2,1)S(1)}, bf16[128,1152]{1,0:T(8,128)(2,1)}, u32[]{:S(2)}) copy-start(bf16[128,1152]{1,0:T(8,128)(2,1)} %images_ref.1) | copy-start | bytes 884740
  5.6 63.6 %copy-start.4 = (s32[128]{0:T(128)S(1)}, s32[128]{0:T(128)}, u32[]{:S(2)}) copy-start(s32[128]{0:T(128)} %param.11) | copy-start | bytes 1540
  39.0 21.1 %collective-permute-start.2 = (bf16[128,1152]{1,0:T(8,128)(2,1)S(1)}, bf16[128,1152]{1,0:T(8,128)(2,1)S(1)}, u32[]{:S(2)}, u32[]{:S(2)}) collective-permute-start(bf16[128,1152]{1,0:T(8,128)(2,1)S(1)} %all_gather.40.own_ref), channel_id=1, source_target_pairs={{0,0},{1,9},{2,6},{3,15},{4,4},{5,13},{6,10},{7,19},{8,8},{9,17},{... | collective-permute-start | bytes 884744 | tf_op jit(solution)/shard_map/ppermute | solution.py:44
  42.9 20.7 %collective-permute-start = (bf16[128,1152]{1,0:T(8,128)(2,1)S(1)}, bf16[128,1152]{1,0:T(8,128)(2,1)S(1)}, u32[]{:S(2)}, u32[]{:S(2)}) collective-permute-start(bf16[128,1152]{1,0:T(8,128)(2,1)S(1)} %all_gather.41.own_ref), channel_id=1, source_target_pairs={{0,0},{1,1019},{2,1020},{3,1013},{4,4},{5,1023},{6,2},{7,1017},{8,... | collective-permute-start | bytes 884744 | tf_op jit(solution)/shard_map/ppermute | solution.py:44
  60.1 12.3 %collective-permute-start.3 = (bf16[128,1152]{1,0:T(8,128)(2,1)S(1)}, bf16[128,1152]{1,0:T(8,128)(2,1)S(1)}, u32[]{:S(2)}, u32[]{:S(2)}) collective-permute-start(bf16[128,1152]{1,0:T(8,128)(2,1)S(1)} %collective-permute-done.2.near_ref), channel_id=1, source_target_pairs={{0,16},{1,17},{2,18},{3,19},{4,20},{5,21},{6,22},{7,23},{8,24},{9,... | collective-permute-start | bytes 884744 | tf_op jit(solution)/shard_map/ppermute | solution.py:44
  63.6 9.8 %collective-permute-start.1 = (bf16[128,1152]{1,0:T(8,128)(2,1)S(1)}, bf16[128,1152]{1,0:T(8,128)(2,1)S(1)}, u32[]{:S(2)}, u32[]{:S(2)}) collective-permute-start(bf16[128,1152]{1,0:T(8,128)(2,1)S(1)} %collective-permute-done.near_ref), channel_id=1, source_target_pairs={{0,1010},{1,1011},{2,1008},{3,1009},{4,1014},{5,1015},{6,1012},{7,... | collective-permute-start | bytes 884744 | tf_op jit(solution)/shard_map/ppermute | solution.py:44
  76.7 23.5 %copy-start = (bf16[1076,1152]{1,0:T(8,128)(2,1)S(1)}, bf16[1076,1152]{1,0:T(8,128)(2,1)}, u32[]{:S(2)}) copy-start(bf16[1076,1152]{1,0:T(8,128)(2,1)} %fc_out_ref.1) | copy-start | bytes 7437316
  76.7 23.5 %copy-start.1 = (bf16[288,1152]{1,0:T(8,128)(2,1)S(1)}, bf16[288,1152]{1,0:T(8,128)(2,1)}, u32[]{:S(2)}) copy-start(bf16[288,1152]{1,0:T(8,128)(2,1)} %head_ref.1) | copy-start | bytes 1990660
  76.7 23.5 %copy-start.3 = (f32[1076,128]{1,0:T(8,128)S(1)}, f32[1076,128]{1,0:T(8,128)}, u32[]{:S(2)}) copy-start(f32[1076,128]{1,0:T(8,128)} %get-tuple-element.31.slope_ref) | copy-start | bytes 1652740

commit v7 on v6

v7 whole, which is shorter than its diff:
```python
import jax
import jax.numpy as jnp
from jax import lax
from jax.experimental import pallas as pl
from jax.experimental.pallas import tpu as pltpu
from jax.sharding import Mesh, PartitionSpec as P

WINDOW = 8


logit_scale = 32.0
logit_bias = -2.0
loss_scale = 16.0
epsilon = 1e-06

AXES = ("z", "y_lo", "x", "y_hi", "core")
SIZES = (16, 4, 4, 2, 2)
MP = ("y_hi", "core")
FIRST = (1, 2)
SECOND = (4, 3)
RELAY = 4
HALF = 64
LANES = 128
HEADS_VMEM = 56
CUTS = 3
GELU_SCALE = 0.7978845608028654
GELU_CUBIC = 0.044715


def place(block, role):
    z = block // 16
    y_hi = (role // 2) ^ (z & 1)
    return block * 4 + y_hi * 2 + role % 2


def move(value, steps):
    pairs = [
        (place(block, role), place((block + (1 - role // 2 * 2) * steps[role % 2]) % 256, role))
        for block in range(256)
        for role in range(4)
        if steps[role % 2]
    ]
    return lax.ppermute(value, AXES, pairs)


def dot(left, right, left_dim, right_dim):
    return lax.dot_general(
        left, right, (((left_dim,), (right_dim,)), ((), ())), preferred_element_type=jnp.float32
    )


def own_half(array, core):
    return array[pl.ds(pl.multiple_of(core * HALF, HALF), HALF), :]


def heads_kernel(
    place_ref, texts_hbm, head_hbm, images_hbm, fc_in_hbm, fc_out_hbm,
    slope_ref, kept_ref, sent_ref,
    texts_ref, head_ref, images_ref, fc_in_ref, fc_out_ref, image_term, text_term, sems,
):
    core = place_ref[0]
    width = images_ref.shape[1]
    cuts = [pl.ds(first, width // CUTS) for first in range(0, width, width // CUTS)]
    pairs = [(texts_hbm, texts_ref), (head_hbm, head_ref), (images_hbm, images_ref)]
    for source, target in ((fc_in_hbm, fc_in_ref), (fc_out_hbm, fc_out_ref)):
        pairs += [(source.at[:, cut], target.at[:, cut]) for cut in cuts]
    copies = [
        pltpu.make_async_copy(source, target, sems.at[index])
        for index, (source, target) in enumerate(pairs)
    ]
    for copy in copies:
        copy.start()
    for copy in copies[:2]:
        copy.wait()
    text_term[...] = dot(texts_ref[...], head_ref[...], 0, 0)
    copies[2].wait()
    pre_act = None
    for cut, copy in zip(cuts, copies[3 : 3 + CUTS]):
        copy.wait()
        part = dot(fc_in_ref[:, cut], images_ref[:, cut], 1, 1)
        pre_act = part if pre_act is None else pre_act + part
    square = pre_act * pre_act
    bent = jnp.tanh(GELU_SCALE * pre_act * (1.0 + GELU_CUBIC * square))
    activation = (0.5 * pre_act * (1.0 + bent)).astype(jnp.bfloat16)
    slope_ref[...] = 0.5 * (1.0 + bent) + (
        0.5 * GELU_SCALE * pre_act * (1.0 - bent * bent) * (1.0 + 3.0 * GELU_CUBIC * square)
    )
    for cut, copy in zip(cuts, copies[3 + CUTS :]):
        copy.wait()
        image_term[:, cut] = dot(activation, fc_out_ref[:, cut], 0, 0)
    for first, term in ((0, image_term), (HALF, text_term)):
        kept_ref[first : first + HALF] = own_half(term, core)
        sent_ref[first : first + HALF] = own_half(term, 1 - core).astype(jnp.bfloat16)


def unit_kernel(
    place_ref, chips_ref, images_ref, unit_ref, inverse_ref, own_sent_ref, moved_sent_ref
):
    embed = chips_ref[0].astype(jnp.float32) + chips_ref[1].astype(jnp.float32)
    image_embed = own_half(images_ref, place_ref[0]).astype(jnp.float32) + embed[:HALF]
    units = []
    for first, rows in ((0, image_embed), (HALF, embed[HALF:])):
        inverse = lax.rsqrt(jnp.sum(rows * rows, axis=1, keepdims=True) + epsilon)
        units.append(rows * inverse)
        unit_ref[first : first + HALF] = units[-1]
        inverse_ref[first : first + HALF] = jnp.broadcast_to(inverse, (HALF, LANES))
    image_side = place_ref[1] == 0
    own_sent_ref[...] = jnp.where(image_side, units[0], units[1]).astype(jnp.bfloat16)
    moved_sent_ref[...] = jnp.where(image_side, units[1], units[0]).astype(jnp.bfloat16)


def split_loss(loss):
    high = loss.astype(jnp.bfloat16).astype(jnp.float32)
    lanes = lax.broadcasted_iota(jnp.int32, (loss.shape[0], LANES), 1)
    return jnp.where(lanes == 0, high, jnp.where(lanes == 1, loss - high, 0.0))


def pair_terms(own, others, positive):
    logits = logit_scale * dot(own, others, 1, 1) + logit_bias
    if positive is None:
        flipped = logits
    else:
        flipped = jnp.where(positive, -logits, logits)
    small = jnp.exp(-jnp.abs(flipped))
    loss = jnp.maximum(flipped, 0.0) + jnp.log1p(small)
    sigmoid = jnp.where(flipped >= 0.0, 1.0, small) / (1.0 + small)
    if positive is None:
        pair_grad = loss_scale * sigmoid
    else:
        pair_grad = jnp.where(positive, -loss_scale, loss_scale) * sigmoid
    return logit_scale * dot(pair_grad.astype(jnp.bfloat16), others, 1, 0), loss


def early_kernel(own_ref, first_ref, second_ref, part_ref):
    rows, width = own_ref.shape
    own = own_ref[...]
    first, first_loss = pair_terms(own, first_ref[...], None)
    second, second_loss = pair_terms(own, second_ref[...], None)
    part_ref[:, :width] = first + second
    loss = jnp.sum(first_loss + second_loss, axis=1, keepdims=True)
    part_ref[:, width:] = jnp.broadcast_to(loss, (rows, LANES))


def late_kernel(
    place_ref, own_ref, here_ref, third_ref, fourth_ref, column_ref, row_ref, early_ref,
    kept_ref, sent_ref, part_ref,
):
    core = place_ref[0]
    rows, width = own_ref.shape
    own = own_ref[...]
    across = lax.broadcasted_iota(jnp.int32, (rows, rows), 1) == column_ref[...]
    down = lax.broadcasted_iota(jnp.int32, (rows, rows), 0) == row_ref[...]
    paired = jnp.where(place_ref[1] == 0, across.astype(jnp.int32), down.astype(jnp.int32))
    third, third_loss = pair_terms(own, third_ref[...], None)
    last = jnp.where(core == 0, here_ref[...], fourth_ref[...])
    last, last_loss = pair_terms(own, last, paired == 1)
    part_ref[:, :width] = early_ref[:, :width] + third + last
    loss = jnp.sum(third_loss + last_loss, axis=1, keepdims=True)
    part_ref[:, width:] = split_loss(early_ref[:, width : width + 1] + loss)
    kept_ref[...] = own_half(part_ref, core)
    sent_ref[...] = own_half(part_ref, 1 - core).astype(jnp.bfloat16)


def tangent_kernel(place_ref, kept_ref, swapped_ref, unit_ref, inverse_ref, sent_ref):
    width = unit_ref.shape[1]
    sums = kept_ref[...] + swapped_ref[1 - place_ref[0]].astype(jnp.float32)
    side = pl.ds(pl.multiple_of(place_ref[1] * HALF, HALF), HALF)
    grad, unit = sums[:, :width], unit_ref[side, :]
    along = jnp.sum(unit * grad, axis=1, keepdims=True)
    tangent = (grad - unit * along) * inverse_ref[side, :][:, :1]
    sent_ref[:, :width] = tangent.astype(jnp.bfloat16)
    loss = sums[:, width : width + 1] + sums[:, width + 1 : width + 2]
    sent_ref[:, width:] = split_loss(loss).astype(jnp.bfloat16)


def backward_kernel(
    place_ref, grads_ref, slope_ref, fc_out_ref, head_ref, hidden_ref, text_ref, loss_ref
):
    rows, width = 2 * HALF, fc_out_ref.shape[1]
    image_chip = place_ref[2] * 2
    image_grad = grads_ref[pl.ds(image_chip, 2)].reshape(rows, width + LANES)
    text_grad = grads_ref[pl.ds(2 - image_chip, 2)].reshape(rows, width + LANES)
    losses = jnp.sum(image_grad[:, width:].astype(jnp.float32), axis=1, keepdims=True)
    loss_ref[...] = jnp.broadcast_to(losses, (rows, LANES)).T[:1] / (WINDOW * rows)
    act_grad = dot(fc_out_ref[...], image_grad[:, :width], 1, 1)
    hidden_ref[...] = (slope_ref[...] * act_grad).astype(jnp.bfloat16)
    text_ref[...] = dot(head_ref[...], text_grad[:, :width], 1, 1).astype(jnp.bfloat16)


def kernel(body, outs, scratch=(), places="", vmem=24):
    spaces = dict(s=pltpu.SMEM, v=pltpu.VMEM, h=pltpu.HBM)
    return pl.pallas_call(
        body,
        out_shape=[jax.ShapeDtypeStruct(shape, dtype) for shape, dtype in outs],
        in_specs=[pl.BlockSpec(memory_space=spaces[place]) for place in places],
        out_specs=[pl.BlockSpec(memory_space=pltpu.VMEM) for unused in outs],
        scratch_shapes=list(scratch),
        compiler_params=pltpu.CompilerParams(vmem_limit_bytes=vmem * 1024 * 1024),
    )


def local(images, texts, fc_in, fc_out, head, partner):
    rows, width = images.shape
    hidden, features = fc_out.shape[0], head.shape[0]
    f32, bf16 = jnp.float32, jnp.bfloat16
    core, flip = lax.axis_index("core"), lax.axis_index("z") & 1
    here = jnp.stack([core, lax.axis_index("y_hi") ^ flip, flip])

    slope, kept, sent = kernel(
        heads_kernel,
        [((hidden, rows), f32), ((rows, width), f32), ((rows, width), bf16)],
        [
            pltpu.VMEM((features, rows), bf16),
            pltpu.VMEM((features, width), bf16),
            pltpu.VMEM((rows, width), bf16),
            pltpu.VMEM((hidden, width), bf16),
            pltpu.VMEM((hidden, width), bf16),
            pltpu.VMEM((rows, width), f32),
            pltpu.VMEM((rows, width), f32),
            pltpu.SemaphoreType.DMA((3 + 2 * CUTS,)),
        ],
        "shhhhh",
        vmem=HEADS_VMEM,
    )(here, texts.T, head, images, fc_in.T, fc_out)
    got = lax.dynamic_index_in_dim(lax.all_gather(sent, "core"), 1 - core, 0, False)
    chips = lax.all_gather((kept + got.astype(f32)).astype(bf16), "y_hi")

    unit, inverse, own_sent, moved_sent = kernel(
        unit_kernel,
        [((rows, width), f32), ((rows, LANES), f32)] + [((HALF, width), bf16)] * 2,
        places="svv",
    )(here, chips, images)

    moved = lax.all_gather(moved_sent, "core", tiled=True)
    moved, own_sent = lax.optimization_barrier((moved, own_sent))
    first = move(moved, FIRST)
    second = move(moved, SECOND)
    own = lax.all_gather(own_sent, "core", tiled=True)
    third = move(first, (RELAY, RELAY))
    fourth = move(second, (0, RELAY))

    paired = jnp.where(core == 0, partner, -1)
    columns = width + LANES
    part = [((rows, columns), f32)]
    (early,) = kernel(early_kernel, part, places="vvv")(own, first, second)
    kept, sent = kernel(
        late_kernel,
        [((HALF, columns), f32), ((HALF, columns), bf16)],
        [pltpu.VMEM(*part[0])],
        "svvvvvvv",
    )(here, own, moved, third, fourth, paired.reshape(rows, 1), paired.reshape(1, rows), early)

    (grads,) = kernel(tangent_kernel, [((HALF, columns), bf16)], places="svvvv")(
        here, kept, lax.all_gather(sent, "core"), unit, inverse
    )
    hidden_grad, text_grad, loss = kernel(
        backward_kernel,
        [((hidden, rows), bf16), ((features, rows), bf16), ((1, rows), f32)],
        places="svvvv",
    )(here, lax.all_gather(grads, MP), slope, fc_out, head)
    return (hidden_grad.T, text_grad.T, loss.reshape(rows))


def solution(mesh):
    dp = ("z", "y_lo", "x")
    return jax.shard_map(
        local,
        mesh=Mesh(mesh.devices.reshape(SIZES), AXES),
        in_specs=(P(dp, None), P(dp, MP), P(None, MP), P(MP, None), P(MP, None), P(dp)),
        out_specs=(P(dp, MP), P(dp, MP), P(dp)),
        check_vma=False,
    )
```

time: 102 us -> 101 us (level)
  waiting for transfers between devices: 4.78 us -> 30.4 us
  starting transfers between devices: 26.4 us -> 7.65 us
  blocking collectives: 59.4 us -> 48 us
  Pallas kernels: 9.23 us -> 11.9 us
    ppermute x4, waiting for transfers between devices: 4.78 us -> 30.4 us  [move(): return lax.ppermute(value, AXES, pairs)]
    ppermute x4, starting transfers between devices: 26.4 us -> 7.65 us  [move(): return lax.ppermute(value, AXES, pairs)]
    all_gather x7 -> x6, blocking collectives: 59.4 us -> 48 us  [the longest x2 18.4 us: local(): lax.all_gather(sent, 'core')]
  transfers between devices with their start and end apart: 4 -> 4, of which waited for: 3 -> 4; matrix products, arithmetic and copies ran while one was open for 0% -> 0% of each run, Pallas kernels for 1% -> 1%
where the time goes in v7:
time: 101 us
  blocking collectives  48 us (48%)
  waiting for transfers between devices  30.4 us (30%)
  Pallas kernels  11.9 us (12%)
  starting transfers between devices  7.65 us (8%)
  other arithmetic  1.78 us (2%)
    ppermute x4, waiting for transfers between devices, move(): return lax.ppermute(value, AXES, pairs)  30.4 us
    all_gather x2, blocking collectives, local(): lax.all_gather(sent, 'core')  18.4 us
    all_gather x1, blocking collectives, local(): chips = lax.all_gather((kept + got.astype(f32)).astype(bf16), 'y_hi')  12.8 us
    all_gather x1, blocking collectives, local(): lax.all_gather(grads, MP)  11.9 us
    ppermute x4, starting transfers between devices, move(): return lax.ppermute(value, AXES, pairs)  7.65 us
    pallas_call x1, Pallas kernels, local(): kernel(heads_kernel, [((hidden, rows), f32), ((rows, width), f32), ((rows...  5.63 us
    all_gather x1, blocking collectives, local(): moved = lax.all_gather(moved_sent, 'core', tiled=True)  2.85 us
    pallas_call x1, Pallas kernels, local(): kernel(backward_kernel, [((hidden, rows), bf16), ((features, rows), bf16)...  2.3 us
  transfers between devices with their start and end apart: 4, of which 4 were waited for; matrix products, arithmetic and copies ran while one was open for 0% of the time, Pallas kernels for 1%

profile of v7, /device:TPU:1, one launch (start us, length us, event | category | flops | bytes accessed | tf_op | source)
XLA Modules:
  0.0 100.6 jit_solution(8659609296007642637)
XLA Ops:
  0.6 0.7 pad_add_fusion.place_ref
  1.3 5.6 %shard_map.85 = (f32[1076,128]{1,0:T(8,128)}, f32[128,1152]{1,0:T(8,128)}, bf16[128,1152]{1,0:T(8,128)(2,1)}) custom-call(s32[3]{0:T(128)} %pad_add_fusion.place_ref, bf16[288,128]{1,0:T(8,128)(2,1)} %bitcast.24, bf16[288,1152]{1,0:T(8,128)(2,1)} %head_ref.1, bf16[128,1152]{1,0:T(8,128)(2,1)} %images_ref.1, bf16[1076,1152]{1,0:T(8,128)(2,1)} %bitcast.22, ...), custom_call_target="tpu_custom_call" | custom-call | tf_op jit(solution)/shard_map/pallas_call | solution.py:209
  7.0 16.3 %all-gather = bf16[256,1152]{1,0:T(8,128)(2,1)S(1)} all-gather(bf16[128,1152]{1,0:T(8,128)(2,1)} %get-tuple-element.18), channel_id=2, replica_groups=mesh['z'=16,'y_lo'=4,'x'=4,'y_hi'=2,'core'=2] {'core'}, dimensions={0}, use_global_device_ids=true | all-gather | bytes 884736 | tf_op jit(solution)/shard_map/all_gather | solution.py:225
  23.3 1.1 %fusion = bf16[128,1152]{1,0:T(8,128)(2,1)S(1)} fusion(f32[128,1152]{1,0:T(8,128)} %get-tuple-element.17, bf16[2,128,1152]{2,1,0:T(8,128)(2,1)S(1)} %bitcast.23, s32[]{:T(128)S(6)} %select_n.12), kind=kLoop, calls=%fused_computation.1 | loop fusion | flops 442368 | bytes 1179652 | tf_op jit(solution)/shard_map/convert_element_type | solution.py:226
  24.4 12.8 %all-gather.1 = bf16[256,1152]{1,0:T(8,128)(2,1)S(1)} all-gather(bf16[128,1152]{1,0:T(8,128)(2,1)S(1)} %fusion), channel_id=3, replica_groups=mesh['z'=16,'y_lo'=4,'x'=4,'y_hi'=2,'core'=2] {'y_hi'}, dimensions={0}, use_global_device_ids=true | all-gather | bytes 884736 | tf_op jit(solution)/shard_map/all_gather | solution.py:226
  37.2 0.7 shard_map.86
  38.0 2.9 %all_gather.34.here_ref = bf16[128,1152]{1,0:T(8,128)(2,1)S(1)} all-gather(bf16[64,1152]{1,0:T(8,128)(2,1)S(1)} %get-tuple-element.19), channel_id=1, replica_groups=mesh['z'=16,'y_lo'=4,'x'=4,'y_hi'=2,'core'=2] {'core'}, dimensions={0}, use_global_device_ids=true | all-gather | bytes 442368 | tf_op jit(solution)/shard_map/all_gather | solution.py:234
  40.9 1.9 %collective-permute-start = (bf16[128,1152]{1,0:T(8,128)(2,1)S(1)}, bf16[128,1152]{1,0:T(8,128)(2,1)S(1)}, u32[]{:S(2)}, u32[]{:S(2)}) collective-permute-start(bf16[128,1152]{1,0:T(8,128)(2,1)S(1)} %all_gather.34.here_ref), channel_id=1, source_target_pairs={{0,4},{1,9},{2,1020},{3,1017},{4,8},{5,13},{6,2},{7,1021},{8,12},{... | collective-permute-start | bytes 884744 | tf_op jit(solution)/shard_map/ppermute | solution.py:43
  42.8 1.9 %collective-permute-start.2 = (bf16[128,1152]{1,0:T(8,128)(2,1)S(1)}, bf16[128,1152]{1,0:T(8,128)(2,1)S(1)}, u32[]{:S(2)}, u32[]{:S(2)}) collective-permute-start(bf16[128,1152]{1,0:T(8,128)(2,1)S(1)} %all_gather.34.here_ref), channel_id=1, source_target_pairs={{0,16},{1,13},{2,1008},{3,1013},{4,20},{5,17},{6,1012},{7,1017},{8... | collective-permute-start | bytes 884744 | tf_op jit(solution)/shard_map/ppermute | solution.py:43
  44.7 19.0 %collective-permute-done.first_ref = bf16[128,1152]{1,0:T(8,128)(2,1)S(1)} collective-permute-done((bf16[128,1152]{1,0:T(8,128)(2,1)S(1)}, bf16[128,1152]{1,0:T(8,128)(2,1)S(1)}, u32[]{:S(2)}, u32[]{:S(2)}) %collective-permute-start) | collective-permute-done | bytes 294944 | tf_op jit(solution)/shard_map/ppermute | solution.py:43
  63.7 1.9 %collective-permute-start.1 = (bf16[128,1152]{1,0:T(8,128)(2,1)S(1)}, bf16[128,1152]{1,0:T(8,128)(2,1)S(1)}, u32[]{:S(2)}, u32[]{:S(2)}) collective-permute-start(bf16[128,1152]{1,0:T(8,128)(2,1)S(1)} %collective-permute-done.first_ref), channel_id=1, source_target_pairs={{0,16},{1,17},{2,1008},{3,1009},{4,20},{5,21},{6,1012},{7,1013},{8... | collective-permute-start | bytes 884744 | tf_op jit(solution)/shard_map/ppermute | solution.py:43
  65.6 1.5 %collective-permute-done.2.second_ref = bf16[128,1152]{1,0:T(8,128)(2,1)S(1)} collective-permute-done((bf16[128,1152]{1,0:T(8,128)(2,1)S(1)}, bf16[128,1152]{1,0:T(8,128)(2,1)S(1)}, u32[]{:S(2)}, u32[]{:S(2)}) %collective-permute-start.2) | collective-permute-done | bytes 294944 | tf_op jit(solution)/shard_map/ppermute | solution.py:43
  67.2 1.9 %collective-permute-start.3 = (bf16[128,1152]{1,0:T(8,128)(2,1)S(1)}, bf16[128,1152]{1,0:T(8,128)(2,1)S(1)}, u32[]{:S(2)}, u32[]{:S(2)}) collective-permute-start(bf16[128,1152]{1,0:T(8,128)(2,1)S(1)} %collective-permute-done.2.second_ref), channel_id=1, source_target_pairs={{1,17},{3,1009},{5,21},{7,1013},{9,25},{11,1017},{13,29},{15,1021}... | collective-permute-start | bytes 884744 | tf_op jit(solution)/shard_map/ppermute | solution.py:43
  69.1 0.1 copy.9.column_ref
  69.2 2.0 %all_gather.35.own_ref = bf16[128,1152]{1,0:T(8,128)(2,1)S(1)} all-gather(bf16[64,1152]{1,0:T(8,128)(2,1)S(1)} %get-tuple-element.21), channel_id=1, replica_groups=mesh['z'=16,'y_lo'=4,'x'=4,'y_hi'=2,'core'=2] {'core'}, dimensions={0}, use_global_device_ids=true | all-gather | bytes 442368 | tf_op jit(solution)/shard_map/all_gather | solution.py:238
  71.2 1.0 shard_map.87.early_ref
  72.2 0.0 copy-start
  72.2 2.9 %collective-permute-done.1.third_ref = bf16[128,1152]{1,0:T(8,128)(2,1)S(1)} collective-permute-done((bf16[128,1152]{1,0:T(8,128)(2,1)S(1)}, bf16[128,1152]{1,0:T(8,128)(2,1)S(1)}, u32[]{:S(2)}, u32[]{:S(2)}) %collective-permute-start.1) | collective-permute-done | bytes 294944 | tf_op jit(solution)/shard_map/ppermute | solution.py:43
  75.1 7.0 %collective-permute-done.3.fourth_ref = bf16[128,1152]{1,0:T(8,128)(2,1)S(1)} collective-permute-done((bf16[128,1152]{1,0:T(8,128)(2,1)S(1)}, bf16[128,1152]{1,0:T(8,128)(2,1)S(1)}, u32[]{:S(2)}, u32[]{:S(2)}) %collective-permute-start.3) | collective-permute-done | bytes 294944 | tf_op jit(solution)/shard_map/ppermute | solution.py:43
  82.0 1.5 %shard_map.88 = (f32[64,1280]{1,0:T(8,128)S(1)}, bf16[64,1280]{1,0:T(8,128)(2,1)S(1)}) custom-call(s32[3]{0:T(128)S(1)} %copy-done.4, bf16[128,1152]{1,0:T(8,128)(2,1)S(1)} %all_gather.35.own_ref, bf16[128,1152]{1,0:T(8,128)(2,1)S(1)} %all_gather.34.here_ref, bf16[128,1152]{1,0:T(8,128)(2,1)S(1)} %collective-permute-done.1.third_ref, ...), custom_call_target="tpu_custom_call" | custom-call | tf_op jit(solution)/shard_map/pallas_call | solution.py:246
  83.6 2.0 %all-gather.2 = bf16[128,1280]{1,0:T(8,128)(2,1)S(1)} all-gather(bf16[64,1280]{1,0:T(8,128)(2,1)S(1)} %get-tuple-element.24), channel_id=4, replica_groups=mesh['z'=16,'y_lo'=4,'x'=4,'y_hi'=2,'core'=2] {'core'}, dimensions={0}, use_global_device_ids=true | all-gather | bytes 491520 | tf_op jit(solution)/shard_map/all_gather | solution.py:254
  85.6 0.7 shard_map.89
  86.3 11.9 %all-gather.3 = bf16[256,1280]{1,0:T(8,128)(2,1)S(1)} all-gather(bf16[64,1280]{1,0:T(8,128)(2,1)S(1)} %shard_map.89), channel_id=5, replica_groups=mesh['z'=16,'y_lo'=4,'x'=4,'y_hi'=2,'core'=2] {'y_hi','core'}, dimensions={0}, use_global_device_ids=true | all-gather | bytes 819200 | tf_op jit(solution)/shard_map/all_gather | solution.py:260
  98.3 2.3 %shard_map.90 = (bf16[1076,128]{1,0:T(8,128)(2,1)}, bf16[288,128]{1,0:T(8,128)(2,1)}, f32[1,128]{1,0:T(1,128)}) custom-call(s32[3]{0:T(128)S(1)} %copy-done.4, bf16[4,64,1280]{2,1,0:T(8,128)(2,1)S(1)} %bitcast.19, f32[1076,128]{1,0:T(8,128)S(1)} %copy-done.3, bf16[1076,1152]{1,0:T(8,128)(2,1)S(1)} %copy-done, bf16[288,1152]{1,0:T(8,128)(2,1)S(1)} %copy-done.1), custom_call_target="tpu_custom_call" | custom-call | tf_op jit(solution)/shard_map/pallas_call | solution.py:256
  (12 shorter events, 0.0 us)
Async XLA Ops:
  6.9 30.3 %copy-start.2 = (bf16[128,1152]{1,0:T(8,128)(2,1)S(1)}, bf16[128,1152]{1,0:T(8,128)(2,1)}, u32[]{:S(2)}) copy-start(bf16[128,1152]{1,0:T(8,128)(2,1)} %images_ref.1) | copy-start | bytes 884740
  6.9 30.3 %copy-start.4 = (s32[3]{0:T(128)S(1)}, s32[3]{0:T(128)}, u32[]{:S(2)}) copy-start(s32[3]{0:T(128)} %pad_add_fusion.place_ref) | copy-start | bytes 40
  7.0 62.1 %copy-start.5 = (s32[128]{0:T(128)S(1)}, s32[128]{0:T(128)}, u32[]{:S(2)}) copy-start(s32[128]{0:T(128)} %param.11) | copy-start | bytes 1540
  40.9 22.9 %collective-permute-start = (bf16[128,1152]{1,0:T(8,128)(2,1)S(1)}, bf16[128,1152]{1,0:T(8,128)(2,1)S(1)}, u32[]{:S(2)}, u32[]{:S(2)}) collective-permute-start(bf16[128,1152]{1,0:T(8,128)(2,1)S(1)} %all_gather.34.here_ref), channel_id=1, source_target_pairs={{0,4},{1,9},{2,1020},{3,1017},{4,8},{5,13},{6,2},{7,1021},{8,12},{... | collective-permute-start | bytes 884744 | tf_op jit(solution)/shard_map/ppermute | solution.py:43
  42.8 24.4 %collective-permute-start.2 = (bf16[128,1152]{1,0:T(8,128)(2,1)S(1)}, bf16[128,1152]{1,0:T(8,128)(2,1)S(1)}, u32[]{:S(2)}, u32[]{:S(2)}) collective-permute-start(bf16[128,1152]{1,0:T(8,128)(2,1)S(1)} %all_gather.34.here_ref), channel_id=1, source_target_pairs={{0,16},{1,13},{2,1008},{3,1013},{4,20},{5,17},{6,1012},{7,1017},{8... | collective-permute-start | bytes 884744 | tf_op jit(solution)/shard_map/ppermute | solution.py:43
  63.7 11.4 %collective-permute-start.1 = (bf16[128,1152]{1,0:T(8,128)(2,1)S(1)}, bf16[128,1152]{1,0:T(8,128)(2,1)S(1)}, u32[]{:S(2)}, u32[]{:S(2)}) collective-permute-start(bf16[128,1152]{1,0:T(8,128)(2,1)S(1)} %collective-permute-done.first_ref), channel_id=1, source_target_pairs={{0,16},{1,17},{2,1008},{3,1009},{4,20},{5,21},{6,1012},{7,1013},{8... | collective-permute-start | bytes 884744 | tf_op jit(solution)/shard_map/ppermute | solution.py:43
  67.2 14.9 %collective-permute-start.3 = (bf16[128,1152]{1,0:T(8,128)(2,1)S(1)}, bf16[128,1152]{1,0:T(8,128)(2,1)S(1)}, u32[]{:S(2)}, u32[]{:S(2)}) collective-permute-start(bf16[128,1152]{1,0:T(8,128)(2,1)S(1)} %collective-permute-done.2.second_ref), channel_id=1, source_target_pairs={{1,17},{3,1009},{5,21},{7,1013},{9,25},{11,1017},{13,29},{15,1021}... | collective-permute-start | bytes 884744 | tf_op jit(solution)/shard_map/ppermute | solution.py:43
  72.2 26.1 %copy-start = (bf16[1076,1152]{1,0:T(8,128)(2,1)S(1)}, bf16[1076,1152]{1,0:T(8,128)(2,1)}, u32[]{:S(2)}) copy-start(bf16[1076,1152]{1,0:T(8,128)(2,1)} %fc_out_ref.1) | copy-start | bytes 7437316
  72.2 26.1 %copy-start.1 = (bf16[288,1152]{1,0:T(8,128)(2,1)S(1)}, bf16[288,1152]{1,0:T(8,128)(2,1)}, u32[]{:S(2)}) copy-start(bf16[288,1152]{1,0:T(8,128)(2,1)} %head_ref.1) | copy-start | bytes 1990660
  72.2 26.1 %copy-start.3 = (f32[1076,128]{1,0:T(8,128)S(1)}, f32[1076,128]{1,0:T(8,128)}, u32[]{:S(2)}) copy-start(f32[1076,128]{1,0:T(8,128)} %get-tuple-element.27.slope_ref) | copy-start | bytes 1652740

commit v8 on v7

--- a/solution.py
+++ b/solution.py
@@ -16,8 +16,8 @@
 AXES = ("z", "y_lo", "x", "y_hi", "core")
 SIZES = (16, 4, 4, 2, 2)
 MP = ("y_hi", "core")
-FIRST = (1, 2)
-SECOND = (4, 3)
+FIRST = (1, 3)
+SECOND = (4, 2)
 RELAY = 4
 HALF = 64
 LANES = 128
@@ -49,16 +49,21 @@
     )
 
 
+def here():
+    flip = lax.axis_index("z") & 1
+    return lax.axis_index("core"), lax.axis_index("y_hi") ^ flip, flip
+
+
 def own_half(array, core):
     return array[pl.ds(pl.multiple_of(core * HALF, HALF), HALF), :]
 
 
 def heads_kernel(
-    place_ref, texts_hbm, head_hbm, images_hbm, fc_in_hbm, fc_out_hbm,
-    slope_ref, kept_ref, sent_ref,
-    texts_ref, head_ref, images_ref, fc_in_ref, fc_out_ref, image_term, text_term, sems,
-):
-    core = place_ref[0]
+    texts_hbm, head_hbm, images_hbm, fc_in_hbm, fc_out_hbm,
+    slope_hbm, kept_ref, sent_ref,
+    slope_ref, texts_ref, head_ref, images_ref, fc_in_ref, fc_out_ref, image_term, text_term, sems,
+):
+    core, unused, unused = here()
     width = images_ref.shape[1]
     cuts = [pl.ds(first, width // CUTS) for first in range(0, width, width // CUTS)]
     pairs = [(texts_hbm, texts_ref), (head_hbm, head_ref), (images_hbm, images_ref)]
@@ -85,28 +90,37 @@
     slope_ref[...] = 0.5 * (1.0 + bent) + (
         0.5 * GELU_SCALE * pre_act * (1.0 - bent * bent) * (1.0 + 3.0 * GELU_CUBIC * square)
     )
+    slope_copy = pltpu.make_async_copy(slope_ref, slope_hbm, sems.at[len(copies)])
+    slope_copy.start()
     for cut, copy in zip(cuts, copies[3 + CUTS :]):
         copy.wait()
         image_term[:, cut] = dot(activation, fc_out_ref[:, cut], 0, 0)
     for first, term in ((0, image_term), (HALF, text_term)):
-        kept_ref[first : first + HALF] = own_half(term, core)
+        kept_ref[first : first + HALF] = own_half(term, core).astype(jnp.bfloat16)
         sent_ref[first : first + HALF] = own_half(term, 1 - core).astype(jnp.bfloat16)
+    slope_copy.wait()
+
+
+def core_sum_kernel(kept_ref, swapped_ref, sum_ref):
+    core, unused, unused = here()
+    got = swapped_ref[1 - core].astype(jnp.float32)
+    sum_ref[...] = (kept_ref[...].astype(jnp.float32) + got).astype(jnp.bfloat16)
 
 
 def unit_kernel(
-    place_ref, chips_ref, images_ref, unit_ref, inverse_ref, own_sent_ref, moved_sent_ref
-):
+    chips_ref, images_ref, unit_ref, inverse_ref, own_sent_ref, moved_sent_ref
+):
+    core, side, unused = here()
     embed = chips_ref[0].astype(jnp.float32) + chips_ref[1].astype(jnp.float32)
-    image_embed = own_half(images_ref, place_ref[0]).astype(jnp.float32) + embed[:HALF]
+    image_embed = own_half(images_ref, core).astype(jnp.float32) + embed[:HALF]
     units = []
     for first, rows in ((0, image_embed), (HALF, embed[HALF:])):
         inverse = lax.rsqrt(jnp.sum(rows * rows, axis=1, keepdims=True) + epsilon)
         units.append(rows * inverse)
         unit_ref[first : first + HALF] = units[-1]
         inverse_ref[first : first + HALF] = jnp.broadcast_to(inverse, (HALF, LANES))
-    image_side = place_ref[1] == 0
-    own_sent_ref[...] = jnp.where(image_side, units[0], units[1]).astype(jnp.bfloat16)
-    moved_sent_ref[...] = jnp.where(image_side, units[1], units[0]).astype(jnp.bfloat16)
+    own_sent_ref[...] = jnp.where(side == 0, units[0], units[1]).astype(jnp.bfloat16)
+    moved_sent_ref[...] = jnp.where(side == 0, units[1], units[0]).astype(jnp.bfloat16)
 
 
 def split_loss(loss):
@@ -142,17 +156,17 @@
 
 
 def late_kernel(
-    place_ref, own_ref, here_ref, third_ref, fourth_ref, column_ref, row_ref, early_ref,
+    own_ref, moved_ref, third_ref, fourth_ref, column_ref, row_ref, early_ref,
     kept_ref, sent_ref, part_ref,
 ):
-    core = place_ref[0]
+    core, side, unused = here()
     rows, width = own_ref.shape
     own = own_ref[...]
     across = lax.broadcasted_iota(jnp.int32, (rows, rows), 1) == column_ref[...]
     down = lax.broadcasted_iota(jnp.int32, (rows, rows), 0) == row_ref[...]
-    paired = jnp.where(place_ref[1] == 0, across.astype(jnp.int32), down.astype(jnp.int32))
+    paired = jnp.where(side == 0, across.astype(jnp.int32), down.astype(jnp.int32))
     third, third_loss = pair_terms(own, third_ref[...], None)
-    last = jnp.where(core == 0, here_ref[...], fourth_ref[...])
+    last = jnp.where(core == 0, moved_ref[...], fourth_ref[...])
     last, last_loss = pair_terms(own, last, paired == 1)
     part_ref[:, :width] = early_ref[:, :width] + third + last
     loss = jnp.sum(third_loss + last_loss, axis=1, keepdims=True)
@@ -161,10 +175,11 @@
     sent_ref[...] = own_half(part_ref, 1 - core).astype(jnp.bfloat16)
 
 
-def tangent_kernel(place_ref, kept_ref, swapped_ref, unit_ref, inverse_ref, sent_ref):
+def tangent_kernel(kept_ref, swapped_ref, unit_ref, inverse_ref, sent_ref):
     width = unit_ref.shape[1]
-    sums = kept_ref[...] + swapped_ref[1 - place_ref[0]].astype(jnp.float32)
-    side = pl.ds(pl.multiple_of(place_ref[1] * HALF, HALF), HALF)
+    core, side, unused = here()
+    sums = kept_ref[...] + swapped_ref[1 - core].astype(jnp.float32)
+    side = pl.ds(pl.multiple_of(side * HALF, HALF), HALF)
     grad, unit = sums[:, :width], unit_ref[side, :]
     along = jnp.sum(unit * grad, axis=1, keepdims=True)
     tangent = (grad - unit * along) * inverse_ref[side, :][:, :1]
@@ -174,10 +189,11 @@
 
 
 def backward_kernel(
-    place_ref, grads_ref, slope_ref, fc_out_ref, head_ref, hidden_ref, text_ref, loss_ref
+    grads_ref, slope_ref, fc_out_ref, head_ref, hidden_ref, text_ref, loss_ref
 ):
     rows, width = 2 * HALF, fc_out_ref.shape[1]
-    image_chip = place_ref[2] * 2
+    unused, unused, flip = here()
+    image_chip = flip * 2
     image_grad = grads_ref[pl.ds(image_chip, 2)].reshape(rows, width + LANES)
     text_grad = grads_ref[pl.ds(2 - image_chip, 2)].reshape(rows, width + LANES)
     losses = jnp.sum(image_grad[:, width:].astype(jnp.float32), axis=1, keepdims=True)
@@ -187,13 +203,15 @@
     text_ref[...] = dot(head_ref[...], text_grad[:, :width], 1, 1).astype(jnp.bfloat16)
 
 
-def kernel(body, outs, scratch=(), places="", vmem=24):
-    spaces = dict(s=pltpu.SMEM, v=pltpu.VMEM, h=pltpu.HBM)
+def kernel(body, outs, scratch=(), places="", vmem=24, out_places=None):
+    spaces = dict(v=pltpu.VMEM, h=pltpu.HBM)
     return pl.pallas_call(
         body,
         out_shape=[jax.ShapeDtypeStruct(shape, dtype) for shape, dtype in outs],
         in_specs=[pl.BlockSpec(memory_space=spaces[place]) for place in places],
-        out_specs=[pl.BlockSpec(memory_space=pltpu.VMEM) for unused in outs],
+        out_specs=[
+            pl.BlockSpec(memory_space=spaces[place]) for place in out_places or "v" * len(outs)
+        ],
         scratch_shapes=list(scratch),
         compiler_params=pltpu.CompilerParams(vmem_limit_bytes=vmem * 1024 * 1024),
     )
@@ -203,13 +221,11 @@
     rows, width = images.shape
     hidden, features = fc_out.shape[0], head.shape[0]
     f32, bf16 = jnp.float32, jnp.bfloat16
-    core, flip = lax.axis_index("core"), lax.axis_index("z") & 1
-    here = jnp.stack([core, lax.axis_index("y_hi") ^ flip, flip])
-
     slope, kept, sent = kernel(
         heads_kernel,
-        [((hidden, rows), f32), ((rows, width), f32), ((rows, width), bf16)],
+        [((hidden, rows), f32), ((rows, width), bf16), ((rows, width), bf16)],
         [
+            pltpu.VMEM((hidden, rows), f32),
             pltpu.VMEM((features, rows), bf16),
             pltpu.VMEM((features, width), bf16),
             pltpu.VMEM((rows, width), bf16),
@@ -217,19 +233,22 @@
             pltpu.VMEM((hidden, width), bf16),
             pltpu.VMEM((rows, width), f32),
             pltpu.VMEM((rows, width), f32),
-            pltpu.SemaphoreType.DMA((3 + 2 * CUTS,)),
+            pltpu.SemaphoreType.DMA((4 + 2 * CUTS,)),
         ],
-        "shhhhh",
+        "hhhhh",
         vmem=HEADS_VMEM,
-    )(here, texts.T, head, images, fc_in.T, fc_out)
-    got = lax.dynamic_index_in_dim(lax.all_gather(sent, "core"), 1 - core, 0, False)
-    chips = lax.all_gather((kept + got.astype(f32)).astype(bf16), "y_hi")
+        out_places="hvv",
+    )(texts.T, head, images, fc_in.T, fc_out)
+    (core_sum,) = kernel(core_sum_kernel, [((rows, width), bf16)], places="vv")(
+        kept, lax.all_gather(sent, "core")
+    )
+    chips = lax.all_gather(core_sum, "y_hi")
 
     unit, inverse, own_sent, moved_sent = kernel(
         unit_kernel,
         [((rows, width), f32), ((rows, LANES), f32)] + [((HALF, width), bf16)] * 2,
-        places="svv",
-    )(here, chips, images)
+        places="vv",
+    )(chips, images)
 
     moved = lax.all_gather(moved_sent, "core", tiled=True)
     moved, own_sent = lax.optimization_barrier((moved, own_sent))
@@ -239,7 +258,7 @@
     third = move(first, (RELAY, RELAY))
     fourth = move(second, (0, RELAY))
 
-    paired = jnp.where(core == 0, partner, -1)
+    paired = jnp.where(lax.axis_index("core") == 0, partner, -1)
     columns = width + LANES
     part = [((rows, columns), f32)]
     (early,) = kernel(early_kernel, part, places="vvv")(own, first, second)
@@ -247,17 +266,17 @@
         late_kernel,
         [((HALF, columns), f32), ((HALF, columns), bf16)],
         [pltpu.VMEM(*part[0])],
-        "svvvvvvv",
-    )(here, own, moved, third, fourth, paired.reshape(rows, 1), paired.reshape(1, rows), early)
-
-    (grads,) = kernel(tangent_kernel, [((HALF, columns), bf16)], places="svvvv")(
-        here, kept, lax.all_gather(sent, "core"), unit, inverse
+        "vvvvvvv",
+    )(own, moved, third, fourth, paired.reshape(rows, 1), paired.reshape(1, rows), early)
+
+    (grads,) = kernel(tangent_kernel, [((HALF, columns), bf16)], places="vvvv")(
+        kept, lax.all_gather(sent, "core"), unit, inverse
     )
     hidden_grad, text_grad, loss = kernel(
         backward_kernel,
         [((hidden, rows), bf16), ((features, rows), bf16), ((1, rows), f32)],
-        places="svvvv",
-    )(here, lax.all_gather(grads, MP), slope, fc_out, head)
+        places="vvvv",
+    )(lax.all_gather(grads, MP), slope, fc_out, head)
     return (hidden_grad.T, text_grad.T, loss.reshape(rows))
 
 

time: 101 us -> 97.2 us (0.962)
  Pallas kernels: 11.9 us -> 9.07 us
  other arithmetic: 1.78 us -> 0.01 us
    pallas_call x2 -> x3, Pallas kernels: 6.34 us -> 5.11 us  [the longest x1 4.88 us: local(): kernel(heads_kernel, [((hidden, rows), f32), ((rows, width), bf16), ((row...]
    convert_element_type x1 -> x0, other arithmetic: 1.12 us -> none  [local(): chips = lax.all_gather((kept + got.astype(f32)).astype(bf16), 'y_hi')]
  transfers between devices with their start and end apart: 4 -> 4, of which waited for: 4 -> 3; matrix products, arithmetic and copies ran while one was open for 0% -> 0% of each run, Pallas kernels for 1% -> 1%
where the time goes in v8:
time: 97.2 us; the launch traced here: 96.9 us
  blocking collectives  48 us (49%)
  waiting for transfers between devices  30.3 us (31%)
  Pallas kernels  9.07 us (9%)
  starting transfers between devices  7.65 us (8%)
  local copies, waits for them, and re-layouts  1.1 us (1%)
    ppermute x4, waiting for transfers between devices, move(): return lax.ppermute(value, AXES, pairs)  30.3 us
    all_gather x2, blocking collectives, local(): lax.all_gather(sent, 'core')  18.4 us
    all_gather x1, blocking collectives, local(): chips = lax.all_gather(core_sum, 'y_hi')  12.8 us
    all_gather x1, blocking collectives, local(): lax.all_gather(grads, MP)  11.9 us
    ppermute x4, starting transfers between devices, move(): return lax.ppermute(value, AXES, pairs)  7.65 us
    pallas_call x1, Pallas kernels, local(): kernel(heads_kernel, [((hidden, rows), f32), ((rows, width), bf16), ((row...  4.88 us
    all_gather x1, blocking collectives, local(): moved = lax.all_gather(moved_sent, 'core', tiled=True)  2.85 us
    all_gather x1, blocking collectives, local(): own = lax.all_gather(own_sent, 'core', tiled=True)  2.01 us
  transfers between devices with their start and end apart: 4, of which 3 were waited for; matrix products, arithmetic and copies ran while one was open for 0% of the time, Pallas kernels for 1%

profile of v8, /device:TPU:1, one launch (start us, length us, event | category | flops | bytes accessed | tf_op | source)
XLA Modules:
  0.0 96.9 jit_solution(11821074374592128536)
XLA Ops:
  0.6 4.9 %shard_map.85 = (f32[1076,128]{1,0:T(8,128)}, bf16[128,1152]{1,0:T(8,128)(2,1)}, bf16[128,1152]{1,0:T(8,128)(2,1)}) custom-call(bf16[288,128]{1,0:T(8,128)(2,1)} %bitcast.18, bf16[288,1152]{1,0:T(8,128)(2,1)} %head_ref.1, bf16[128,1152]{1,0:T(8,128)(2,1)} %images_ref.1, bf16[1076,1152]{1,0:T(8,128)(2,1)} %bitcast.17, bf16[1076,1152]{1,0:T(8,128)(2,1)} %fc_out_ref.1), custom_call_target="tpu_custom_call" | custom-call | tf_op jit(solution)/shard_map/pallas_call | solution.py:224
  5.5 0.0 copy-start.2
  5.5 0.0 copy-start.5
  5.5 16.4 %all-gather = bf16[256,1152]{1,0:T(8,128)(2,1)S(1)} all-gather(bf16[128,1152]{1,0:T(8,128)(2,1)} %get-tuple-element.18), channel_id=2, replica_groups=mesh['z'=16,'y_lo'=4,'x'=4,'y_hi'=2,'core'=2] {'core'}, dimensions={0}, use_global_device_ids=true | all-gather | bytes 884736 | tf_op jit(solution)/shard_map/all_gather | solution.py:243
  21.9 1.0 copy-done.4
  22.9 0.1 shard_map.86
  22.9 12.8 %all-gather.1 = bf16[256,1152]{1,0:T(8,128)(2,1)S(1)} all-gather(bf16[128,1152]{1,0:T(8,128)(2,1)S(1)} %shard_map.86), channel_id=3, replica_groups=mesh['z'=16,'y_lo'=4,'x'=4,'y_hi'=2,'core'=2] {'y_hi'}, dimensions={0}, use_global_device_ids=true | all-gather | bytes 884736 | tf_op jit(solution)/shard_map/all_gather | solution.py:245
  35.7 0.2 shard_map.87
  36.0 2.9 %all_gather.34.moved_ref = bf16[128,1152]{1,0:T(8,128)(2,1)S(1)} all-gather(bf16[64,1152]{1,0:T(8,128)(2,1)S(1)} %get-tuple-element.19), channel_id=1, replica_groups=mesh['z'=16,'y_lo'=4,'x'=4,'y_hi'=2,'core'=2] {'core'}, dimensions={0}, use_global_device_ids=true | all-gather | bytes 442368 | tf_op jit(solution)/shard_map/all_gather | solution.py:253
  38.8 1.9 %collective-permute-start = (bf16[128,1152]{1,0:T(8,128)(2,1)S(1)}, bf16[128,1152]{1,0:T(8,128)(2,1)S(1)}, u32[]{:S(2)}, u32[]{:S(2)}) collective-permute-start(bf16[128,1152]{1,0:T(8,128)(2,1)S(1)} %all_gather.34.moved_ref), channel_id=1, source_target_pairs={{0,4},{1,13},{2,1020},{3,1013},{4,8},{5,17},{6,2},{7,1017},{8,12},... | collective-permute-start | bytes 884744 | tf_op jit(solution)/shard_map/ppermute | solution.py:43
  40.7 1.9 %collective-permute-start.2 = (bf16[128,1152]{1,0:T(8,128)(2,1)S(1)}, bf16[128,1152]{1,0:T(8,128)(2,1)S(1)}, u32[]{:S(2)}, u32[]{:S(2)}) collective-permute-start(bf16[128,1152]{1,0:T(8,128)(2,1)S(1)} %all_gather.34.moved_ref), channel_id=1, source_target_pairs={{0,16},{1,9},{2,1008},{3,1017},{4,20},{5,13},{6,1012},{7,1021},{8,... | collective-permute-start | bytes 884744 | tf_op jit(solution)/shard_map/ppermute | solution.py:43
  42.7 16.0 %collective-permute-done.first_ref = bf16[128,1152]{1,0:T(8,128)(2,1)S(1)} collective-permute-done((bf16[128,1152]{1,0:T(8,128)(2,1)S(1)}, bf16[128,1152]{1,0:T(8,128)(2,1)S(1)}, u32[]{:S(2)}, u32[]{:S(2)}) %collective-permute-start) | collective-permute-done | bytes 294944 | tf_op jit(solution)/shard_map/ppermute | solution.py:43
  58.7 1.9 %collective-permute-start.1 = (bf16[128,1152]{1,0:T(8,128)(2,1)S(1)}, bf16[128,1152]{1,0:T(8,128)(2,1)S(1)}, u32[]{:S(2)}, u32[]{:S(2)}) collective-permute-start(bf16[128,1152]{1,0:T(8,128)(2,1)S(1)} %collective-permute-done.first_ref), channel_id=1, source_target_pairs={{0,16},{1,17},{2,1008},{3,1009},{4,20},{5,21},{6,1012},{7,1013},{8... | collective-permute-start | bytes 884744 | tf_op jit(solution)/shard_map/ppermute | solution.py:43
  60.6 5.1 %collective-permute-done.2.second_ref = bf16[128,1152]{1,0:T(8,128)(2,1)S(1)} collective-permute-done((bf16[128,1152]{1,0:T(8,128)(2,1)S(1)}, bf16[128,1152]{1,0:T(8,128)(2,1)S(1)}, u32[]{:S(2)}, u32[]{:S(2)}) %collective-permute-start.2) | collective-permute-done | bytes 294944 | tf_op jit(solution)/shard_map/ppermute | solution.py:43
  65.7 1.9 %collective-permute-start.3 = (bf16[128,1152]{1,0:T(8,128)(2,1)S(1)}, bf16[128,1152]{1,0:T(8,128)(2,1)S(1)}, u32[]{:S(2)}, u32[]{:S(2)}) collective-permute-start(bf16[128,1152]{1,0:T(8,128)(2,1)S(1)} %collective-permute-done.2.second_ref), channel_id=1, source_target_pairs={{1,17},{3,1009},{5,21},{7,1013},{9,25},{11,1017},{13,29},{15,1021}... | collective-permute-start | bytes 884744 | tf_op jit(solution)/shard_map/ppermute | solution.py:43
  67.6 0.1 copy.9.column_ref
  67.7 2.0 %all_gather.35.own_ref = bf16[128,1152]{1,0:T(8,128)(2,1)S(1)} all-gather(bf16[64,1152]{1,0:T(8,128)(2,1)S(1)} %get-tuple-element.21), channel_id=1, replica_groups=mesh['z'=16,'y_lo'=4,'x'=4,'y_hi'=2,'core'=2] {'core'}, dimensions={0}, use_global_device_ids=true | all-gather | bytes 442368 | tf_op jit(solution)/shard_map/all_gather | solution.py:257
  69.7 0.9 shard_map.88.early_ref
  70.7 9.2 %collective-permute-done.3.fourth_ref = bf16[128,1152]{1,0:T(8,128)(2,1)S(1)} collective-permute-done((bf16[128,1152]{1,0:T(8,128)(2,1)S(1)}, bf16[128,1152]{1,0:T(8,128)(2,1)S(1)}, u32[]{:S(2)}, u32[]{:S(2)}) %collective-permute-start.3) | collective-permute-done | bytes 294944 | tf_op jit(solution)/shard_map/ppermute | solution.py:43
  80.0 1.1 %shard_map.89 = (f32[64,1280]{1,0:T(8,128)S(1)}, bf16[64,1280]{1,0:T(8,128)(2,1)S(1)}) custom-call(bf16[128,1152]{1,0:T(8,128)(2,1)S(1)} %all_gather.35.own_ref, bf16[128,1152]{1,0:T(8,128)(2,1)S(1)} %all_gather.34.moved_ref, bf16[128,1152]{1,0:T(8,128)(2,1)S(1)} %collective-permute-done.1.third_ref, ...), custom_call_target="tpu_custom_call" | custom-call | tf_op jit(solution)/shard_map/pallas_call | solution.py:265
  81.0 2.0 %all-gather.2 = bf16[128,1280]{1,0:T(8,128)(2,1)S(1)} all-gather(bf16[64,1280]{1,0:T(8,128)(2,1)S(1)} %get-tuple-element.24), channel_id=4, replica_groups=mesh['z'=16,'y_lo'=4,'x'=4,'y_hi'=2,'core'=2] {'core'}, dimensions={0}, use_global_device_ids=true | all-gather | bytes 491520 | tf_op jit(solution)/shard_map/all_gather | solution.py:273
  83.0 0.2 shard_map.90
  83.2 11.9 %all-gather.3 = bf16[256,1280]{1,0:T(8,128)(2,1)S(1)} all-gather(bf16[64,1280]{1,0:T(8,128)(2,1)S(1)} %shard_map.90), channel_id=5, replica_groups=mesh['z'=16,'y_lo'=4,'x'=4,'y_hi'=2,'core'=2] {'y_hi','core'}, dimensions={0}, use_global_device_ids=true | all-gather | bytes 819200 | tf_op jit(solution)/shard_map/all_gather | solution.py:279
  95.1 1.8 %shard_map.91 = (bf16[1076,128]{1,0:T(8,128)(2,1)}, bf16[288,128]{1,0:T(8,128)(2,1)}, f32[1,128]{1,0:T(1,128)}) custom-call(bf16[4,64,1280]{2,1,0:T(8,128)(2,1)S(1)} %bitcast.13, f32[1076,128]{1,0:T(8,128)S(1)} %copy-done.3, bf16[1076,1152]{1,0:T(8,128)(2,1)S(1)} %copy-done, bf16[288,1152]{1,0:T(8,128)(2,1)S(1)} %copy-done.1), custom_call_target="tpu_custom_call" | custom-call | tf_op jit(solution)/shard_map/pallas_call | solution.py:275
  (11 shorter events, 0.0 us)
Async XLA Ops:
  5.5 30.2 %copy-start.2 = (bf16[128,1152]{1,0:T(8,128)(2,1)S(1)}, bf16[128,1152]{1,0:T(8,128)(2,1)}, u32[]{:S(2)}) copy-start(bf16[128,1152]{1,0:T(8,128)(2,1)} %images_ref.1) | copy-start | bytes 884740
  5.5 62.1 %copy-start.5 = (s32[128]{0:T(128)S(1)}, s32[128]{0:T(128)}, u32[]{:S(2)}) copy-start(s32[128]{0:T(128)} %param.11) | copy-start | bytes 1540
  21.9 1.0 copy-start.4
  38.8 19.9 %collective-permute-start = (bf16[128,1152]{1,0:T(8,128)(2,1)S(1)}, bf16[128,1152]{1,0:T(8,128)(2,1)S(1)}, u32[]{:S(2)}, u32[]{:S(2)}) collective-permute-start(bf16[128,1152]{1,0:T(8,128)(2,1)S(1)} %all_gather.34.moved_ref), channel_id=1, source_target_pairs={{0,4},{1,13},{2,1020},{3,1013},{4,8},{5,17},{6,2},{7,1017},{8,12},... | collective-permute-start | bytes 884744 | tf_op jit(solution)/shard_map/ppermute | solution.py:43
  40.7 25.0 %collective-permute-start.2 = (bf16[128,1152]{1,0:T(8,128)(2,1)S(1)}, bf16[128,1152]{1,0:T(8,128)(2,1)S(1)}, u32[]{:S(2)}, u32[]{:S(2)}) collective-permute-start(bf16[128,1152]{1,0:T(8,128)(2,1)S(1)} %all_gather.34.moved_ref), channel_id=1, source_target_pairs={{0,16},{1,9},{2,1008},{3,1017},{4,20},{5,13},{6,1012},{7,1021},{8,... | collective-permute-start | bytes 884744 | tf_op jit(solution)/shard_map/ppermute | solution.py:43
  58.7 12.0 %collective-permute-start.1 = (bf16[128,1152]{1,0:T(8,128)(2,1)S(1)}, bf16[128,1152]{1,0:T(8,128)(2,1)S(1)}, u32[]{:S(2)}, u32[]{:S(2)}) collective-permute-start(bf16[128,1152]{1,0:T(8,128)(2,1)S(1)} %collective-permute-done.first_ref), channel_id=1, source_target_pairs={{0,16},{1,17},{2,1008},{3,1009},{4,20},{5,21},{6,1012},{7,1013},{8... | collective-permute-start | bytes 884744 | tf_op jit(solution)/shard_map/ppermute | solution.py:43
  65.7 14.3 %collective-permute-start.3 = (bf16[128,1152]{1,0:T(8,128)(2,1)S(1)}, bf16[128,1152]{1,0:T(8,128)(2,1)S(1)}, u32[]{:S(2)}, u32[]{:S(2)}) collective-permute-start(bf16[128,1152]{1,0:T(8,128)(2,1)S(1)} %collective-permute-done.2.second_ref), channel_id=1, source_target_pairs={{1,17},{3,1009},{5,21},{7,1013},{9,25},{11,1017},{13,29},{15,1021}... | collective-permute-start | bytes 884744 | tf_op jit(solution)/shard_map/ppermute | solution.py:43
  70.7 24.4 %copy-start = (bf16[1076,1152]{1,0:T(8,128)(2,1)S(1)}, bf16[1076,1152]{1,0:T(8,128)(2,1)}, u32[]{:S(2)}) copy-start(bf16[1076,1152]{1,0:T(8,128)(2,1)} %fc_out_ref.1) | copy-start | bytes 7437316
  70.7 24.4 %copy-start.1 = (bf16[288,1152]{1,0:T(8,128)(2,1)S(1)}, bf16[288,1152]{1,0:T(8,128)(2,1)}, u32[]{:S(2)}) copy-start(bf16[288,1152]{1,0:T(8,128)(2,1)} %head_ref.1) | copy-start | bytes 1990660
  70.7 24.4 %copy-start.3 = (f32[1076,128]{1,0:T(8,128)S(1)}, f32[1076,128]{1,0:T(8,128)}, u32[]{:S(2)}) copy-start(f32[1076,128]{1,0:T(8,128)} %get-tuple-element.27.slope_ref) | copy-start | bytes 1652740

commit v9 on v8

--- a/solution.py
+++ b/solution.py
@@ -16,9 +16,10 @@
 AXES = ("z", "y_lo", "x", "y_hi", "core")
 SIZES = (16, 4, 4, 2, 2)
 MP = ("y_hi", "core")
-FIRST = (1, 3)
-SECOND = (4, 2)
-RELAY = 4
+FIRST = (4, 3)
+SECOND = (1, 2)
+THIRD = (1, 4)
+FOURTH = (0, 4)
 HALF = 64
 LANES = 128
 HEADS_VMEM = 56
@@ -255,8 +256,8 @@
     first = move(moved, FIRST)
     second = move(moved, SECOND)
     own = lax.all_gather(own_sent, "core", tiled=True)
-    third = move(first, (RELAY, RELAY))
-    fourth = move(second, (0, RELAY))
+    third = move(first, THIRD)
+    fourth = move(second, FOURTH)
 
     paired = jnp.where(lax.axis_index("core") == 0, partner, -1)
     columns = width + LANES

time: 97.2 us -> 97.6 us (level)
  waiting for transfers between devices: 30.3 us -> 29.3 us
    ppermute x4, waiting for transfers between devices: 30.3 us -> 29.3 us  [move(): return lax.ppermute(value, AXES, pairs)]
where the time goes in v9:
time: 97.6 us; the launch traced here: 96.8 us
  blocking collectives  48.9 us (50%)
  waiting for transfers between devices  29.3 us (30%)
  Pallas kernels  9.07 us (9%)
  starting transfers between devices  7.65 us (8%)
  local copies, waits for them, and re-layouts  1.1 us (1%)
    ppermute x4, waiting for transfers between devices, move(): return lax.ppermute(value, AXES, pairs)  29.3 us
    all_gather x2, blocking collectives, local(): lax.all_gather(sent, 'core')  18.4 us
    all_gather x1, blocking collectives, local(): chips = lax.all_gather(core_sum, 'y_hi')  12.8 us
    all_gather x1, blocking collectives, local(): lax.all_gather(grads, MP)  11.9 us
    ppermute x4, starting transfers between devices, move(): return lax.ppermute(value, AXES, pairs)  7.65 us
    pallas_call x1, Pallas kernels, local(): kernel(heads_kernel, [((hidden, rows), f32), ((rows, width), bf16), ((row...  4.88 us
    all_gather x1, blocking collectives, local(): own = lax.all_gather(own_sent, 'core', tiled=True)  2.91 us
    all_gather x1, blocking collectives, local(): moved = lax.all_gather(moved_sent, 'core', tiled=True)  2.85 us
  transfers between devices with their start and end apart: 4, of which 3 were waited for; matrix products, arithmetic and copies ran while one was open for 0% of the time, Pallas kernels for 1%

profile of v9, /device:TPU:1, one launch (start us, length us, event | category | flops | bytes accessed | tf_op | source)
XLA Modules:
  0.0 96.8 jit_solution(7608374365590777509)
XLA Ops:
  0.6 4.9 %shard_map.85 = (f32[1076,128]{1,0:T(8,128)}, bf16[128,1152]{1,0:T(8,128)(2,1)}, bf16[128,1152]{1,0:T(8,128)(2,1)}) custom-call(bf16[288,128]{1,0:T(8,128)(2,1)} %bitcast.18, bf16[288,1152]{1,0:T(8,128)(2,1)} %head_ref.1, bf16[128,1152]{1,0:T(8,128)(2,1)} %images_ref.1, bf16[1076,1152]{1,0:T(8,128)(2,1)} %bitcast.17, bf16[1076,1152]{1,0:T(8,128)(2,1)} %fc_out_ref.1), custom_call_target="tpu_custom_call" | custom-call | tf_op jit(solution)/shard_map/pallas_call | solution.py:225
  5.5 0.0 copy-start.2
  5.5 0.0 copy-start.5
  5.5 16.4 %all-gather = bf16[256,1152]{1,0:T(8,128)(2,1)S(1)} all-gather(bf16[128,1152]{1,0:T(8,128)(2,1)} %get-tuple-element.18), channel_id=2, replica_groups=mesh['z'=16,'y_lo'=4,'x'=4,'y_hi'=2,'core'=2] {'core'}, dimensions={0}, use_global_device_ids=true | all-gather | bytes 884736 | tf_op jit(solution)/shard_map/all_gather | solution.py:244
  21.9 1.0 copy-done.4
  22.9 0.1 shard_map.86
  22.9 12.8 %all-gather.1 = bf16[256,1152]{1,0:T(8,128)(2,1)S(1)} all-gather(bf16[128,1152]{1,0:T(8,128)(2,1)S(1)} %shard_map.86), channel_id=3, replica_groups=mesh['z'=16,'y_lo'=4,'x'=4,'y_hi'=2,'core'=2] {'y_hi'}, dimensions={0}, use_global_device_ids=true | all-gather | bytes 884736 | tf_op jit(solution)/shard_map/all_gather | solution.py:246
  35.7 0.2 shard_map.87
  36.0 2.9 %all_gather.34.moved_ref = bf16[128,1152]{1,0:T(8,128)(2,1)S(1)} all-gather(bf16[64,1152]{1,0:T(8,128)(2,1)S(1)} %get-tuple-element.19), channel_id=1, replica_groups=mesh['z'=16,'y_lo'=4,'x'=4,'y_hi'=2,'core'=2] {'core'}, dimensions={0}, use_global_device_ids=true | all-gather | bytes 442368 | tf_op jit(solution)/shard_map/all_gather | solution.py:254
  38.8 1.9 %collective-permute-start = (bf16[128,1152]{1,0:T(8,128)(2,1)S(1)}, bf16[128,1152]{1,0:T(8,128)(2,1)S(1)}, u32[]{:S(2)}, u32[]{:S(2)}) collective-permute-start(bf16[128,1152]{1,0:T(8,128)(2,1)S(1)} %all_gather.34.moved_ref), channel_id=1, source_target_pairs={{0,16},{1,13},{2,1008},{3,1013},{4,20},{5,17},{6,1012},{7,1017},{8... | collective-permute-start | bytes 884744 | tf_op jit(solution)/shard_map/ppermute | solution.py:44
  40.7 1.9 %collective-permute-start.2 = (bf16[128,1152]{1,0:T(8,128)(2,1)S(1)}, bf16[128,1152]{1,0:T(8,128)(2,1)S(1)}, u32[]{:S(2)}, u32[]{:S(2)}) collective-permute-start(bf16[128,1152]{1,0:T(8,128)(2,1)S(1)} %all_gather.34.moved_ref), channel_id=1, source_target_pairs={{0,4},{1,9},{2,1020},{3,1017},{4,8},{5,13},{6,2},{7,1021},{8,12},{... | collective-permute-start | bytes 884744 | tf_op jit(solution)/shard_map/ppermute | solution.py:44
  42.7 18.4 %collective-permute-done.first_ref = bf16[128,1152]{1,0:T(8,128)(2,1)S(1)} collective-permute-done((bf16[128,1152]{1,0:T(8,128)(2,1)S(1)}, bf16[128,1152]{1,0:T(8,128)(2,1)S(1)}, u32[]{:S(2)}, u32[]{:S(2)}) %collective-permute-start) | collective-permute-done | bytes 294944 | tf_op jit(solution)/shard_map/ppermute | solution.py:44
  61.1 1.9 %collective-permute-start.1 = (bf16[128,1152]{1,0:T(8,128)(2,1)S(1)}, bf16[128,1152]{1,0:T(8,128)(2,1)S(1)}, u32[]{:S(2)}, u32[]{:S(2)}) collective-permute-start(bf16[128,1152]{1,0:T(8,128)(2,1)S(1)} %collective-permute-done.first_ref), channel_id=1, source_target_pairs={{0,4},{1,17},{2,1020},{3,1009},{4,8},{5,21},{6,2},{7,1013},{8,12},... | collective-permute-start | bytes 884744 | tf_op jit(solution)/shard_map/ppermute | solution.py:44
  63.0 4.8 %collective-permute-done.2.second_ref = bf16[128,1152]{1,0:T(8,128)(2,1)S(1)} collective-permute-done((bf16[128,1152]{1,0:T(8,128)(2,1)S(1)}, bf16[128,1152]{1,0:T(8,128)(2,1)S(1)}, u32[]{:S(2)}, u32[]{:S(2)}) %collective-permute-start.2) | collective-permute-done | bytes 294944 | tf_op jit(solution)/shard_map/ppermute | solution.py:44
  67.8 1.9 %collective-permute-start.3 = (bf16[128,1152]{1,0:T(8,128)(2,1)S(1)}, bf16[128,1152]{1,0:T(8,128)(2,1)S(1)}, u32[]{:S(2)}, u32[]{:S(2)}) collective-permute-start(bf16[128,1152]{1,0:T(8,128)(2,1)S(1)} %collective-permute-done.2.second_ref), channel_id=1, source_target_pairs={{1,17},{3,1009},{5,21},{7,1013},{9,25},{11,1017},{13,29},{15,1021}... | collective-permute-start | bytes 884744 | tf_op jit(solution)/shard_map/ppermute | solution.py:44
  69.7 0.1 copy.9.column_ref
  69.9 2.9 %all_gather.35.own_ref = bf16[128,1152]{1,0:T(8,128)(2,1)S(1)} all-gather(bf16[64,1152]{1,0:T(8,128)(2,1)S(1)} %get-tuple-element.21), channel_id=1, replica_groups=mesh['z'=16,'y_lo'=4,'x'=4,'y_hi'=2,'core'=2] {'core'}, dimensions={0}, use_global_device_ids=true | all-gather | bytes 442368 | tf_op jit(solution)/shard_map/all_gather | solution.py:258
  72.8 1.0 shard_map.88.early_ref
  73.8 6.0 %collective-permute-done.3.fourth_ref = bf16[128,1152]{1,0:T(8,128)(2,1)S(1)} collective-permute-done((bf16[128,1152]{1,0:T(8,128)(2,1)S(1)}, bf16[128,1152]{1,0:T(8,128)(2,1)S(1)}, u32[]{:S(2)}, u32[]{:S(2)}) %collective-permute-start.3) | collective-permute-done | bytes 294944 | tf_op jit(solution)/shard_map/ppermute | solution.py:44
  79.8 1.1 %shard_map.89 = (f32[64,1280]{1,0:T(8,128)S(1)}, bf16[64,1280]{1,0:T(8,128)(2,1)S(1)}) custom-call(bf16[128,1152]{1,0:T(8,128)(2,1)S(1)} %all_gather.35.own_ref, bf16[128,1152]{1,0:T(8,128)(2,1)S(1)} %all_gather.34.moved_ref, bf16[128,1152]{1,0:T(8,128)(2,1)S(1)} %collective-permute-done.1.third_ref, ...), custom_call_target="tpu_custom_call" | custom-call | tf_op jit(solution)/shard_map/pallas_call | solution.py:266
  80.9 2.0 %all-gather.2 = bf16[128,1280]{1,0:T(8,128)(2,1)S(1)} all-gather(bf16[64,1280]{1,0:T(8,128)(2,1)S(1)} %get-tuple-element.24), channel_id=4, replica_groups=mesh['z'=16,'y_lo'=4,'x'=4,'y_hi'=2,'core'=2] {'core'}, dimensions={0}, use_global_device_ids=true | all-gather | bytes 491520 | tf_op jit(solution)/shard_map/all_gather | solution.py:274
  82.9 0.2 shard_map.90
  83.1 11.9 %all-gather.3 = bf16[256,1280]{1,0:T(8,128)(2,1)S(1)} all-gather(bf16[64,1280]{1,0:T(8,128)(2,1)S(1)} %shard_map.90), channel_id=5, replica_groups=mesh['z'=16,'y_lo'=4,'x'=4,'y_hi'=2,'core'=2] {'y_hi','core'}, dimensions={0}, use_global_device_ids=true | all-gather | bytes 819200 | tf_op jit(solution)/shard_map/all_gather | solution.py:280
  95.0 1.8 %shard_map.91 = (bf16[1076,128]{1,0:T(8,128)(2,1)}, bf16[288,128]{1,0:T(8,128)(2,1)}, f32[1,128]{1,0:T(1,128)}) custom-call(bf16[4,64,1280]{2,1,0:T(8,128)(2,1)S(1)} %bitcast.13, f32[1076,128]{1,0:T(8,128)S(1)} %copy-done.3, bf16[1076,1152]{1,0:T(8,128)(2,1)S(1)} %copy-done, bf16[288,1152]{1,0:T(8,128)(2,1)S(1)} %copy-done.1), custom_call_target="tpu_custom_call" | custom-call | tf_op jit(solution)/shard_map/pallas_call | solution.py:276
  (11 shorter events, 0.0 us)
Async XLA Ops:
  5.5 30.2 %copy-start.2 = (bf16[128,1152]{1,0:T(8,128)(2,1)S(1)}, bf16[128,1152]{1,0:T(8,128)(2,1)}, u32[]{:S(2)}) copy-start(bf16[128,1152]{1,0:T(8,128)(2,1)} %images_ref.1) | copy-start | bytes 884740
  5.5 64.2 %copy-start.5 = (s32[128]{0:T(128)S(1)}, s32[128]{0:T(128)}, u32[]{:S(2)}) copy-start(s32[128]{0:T(128)} %param.11) | copy-start | bytes 1540
  21.9 1.0 copy-start.4
  38.8 22.3 %collective-permute-start = (bf16[128,1152]{1,0:T(8,128)(2,1)S(1)}, bf16[128,1152]{1,0:T(8,128)(2,1)S(1)}, u32[]{:S(2)}, u32[]{:S(2)}) collective-permute-start(bf16[128,1152]{1,0:T(8,128)(2,1)S(1)} %all_gather.34.moved_ref), channel_id=1, source_target_pairs={{0,16},{1,13},{2,1008},{3,1013},{4,20},{5,17},{6,1012},{7,1017},{8... | collective-permute-start | bytes 884744 | tf_op jit(solution)/shard_map/ppermute | solution.py:44
  40.7 27.1 %collective-permute-start.2 = (bf16[128,1152]{1,0:T(8,128)(2,1)S(1)}, bf16[128,1152]{1,0:T(8,128)(2,1)S(1)}, u32[]{:S(2)}, u32[]{:S(2)}) collective-permute-start(bf16[128,1152]{1,0:T(8,128)(2,1)S(1)} %all_gather.34.moved_ref), channel_id=1, source_target_pairs={{0,4},{1,9},{2,1020},{3,1017},{4,8},{5,13},{6,2},{7,1021},{8,12},{... | collective-permute-start | bytes 884744 | tf_op jit(solution)/shard_map/ppermute | solution.py:44
  61.1 12.7 %collective-permute-start.1 = (bf16[128,1152]{1,0:T(8,128)(2,1)S(1)}, bf16[128,1152]{1,0:T(8,128)(2,1)S(1)}, u32[]{:S(2)}, u32[]{:S(2)}) collective-permute-start(bf16[128,1152]{1,0:T(8,128)(2,1)S(1)} %collective-permute-done.first_ref), channel_id=1, source_target_pairs={{0,4},{1,17},{2,1020},{3,1009},{4,8},{5,21},{6,2},{7,1013},{8,12},... | collective-permute-start | bytes 884744 | tf_op jit(solution)/shard_map/ppermute | solution.py:44
  67.8 12.0 %collective-permute-start.3 = (bf16[128,1152]{1,0:T(8,128)(2,1)S(1)}, bf16[128,1152]{1,0:T(8,128)(2,1)S(1)}, u32[]{:S(2)}, u32[]{:S(2)}) collective-permute-start(bf16[128,1152]{1,0:T(8,128)(2,1)S(1)} %collective-permute-done.2.second_ref), channel_id=1, source_target_pairs={{1,17},{3,1009},{5,21},{7,1013},{9,25},{11,1017},{13,29},{15,1021}... | collective-permute-start | bytes 884744 | tf_op jit(solution)/shard_map/ppermute | solution.py:44
  73.7 21.3 %copy-start = (bf16[1076,1152]{1,0:T(8,128)(2,1)S(1)}, bf16[1076,1152]{1,0:T(8,128)(2,1)}, u32[]{:S(2)}) copy-start(bf16[1076,1152]{1,0:T(8,128)(2,1)} %fc_out_ref.1) | copy-start | bytes 7437316
  73.7 21.3 %copy-start.1 = (bf16[288,1152]{1,0:T(8,128)(2,1)S(1)}, bf16[288,1152]{1,0:T(8,128)(2,1)}, u32[]{:S(2)}) copy-start(bf16[288,1152]{1,0:T(8,128)(2,1)} %head_ref.1) | copy-start | bytes 1990660
  73.8 21.2 %copy-start.3 = (f32[1076,128]{1,0:T(8,128)S(1)}, f32[1076,128]{1,0:T(8,128)}, u32[]{:S(2)}) copy-start(f32[1076,128]{1,0:T(8,128)} %get-tuple-element.27.slope_ref) | copy-start | bytes 1652740

commit v10 on v8

--- a/solution.py
+++ b/solution.py
@@ -101,26 +101,33 @@
     slope_copy.wait()
 
 
-def core_sum_kernel(kept_ref, swapped_ref, sum_ref):
-    core, unused, unused = here()
+def core_sum_kernel(kept_ref, swapped_ref, own_ref, moved_ref):
+    core, side, unused = here()
     got = swapped_ref[1 - core].astype(jnp.float32)
-    sum_ref[...] = (kept_ref[...].astype(jnp.float32) + got).astype(jnp.bfloat16)
-
-
-def unit_kernel(
-    chips_ref, images_ref, unit_ref, inverse_ref, own_sent_ref, moved_sent_ref
-):
+    sums = (kept_ref[...].astype(jnp.float32) + got).astype(jnp.bfloat16)
+    own_ref[...] = jnp.where(side == 0, sums[:HALF], sums[HALF:])
+    moved_ref[...] = jnp.where(side == 0, sums[HALF:], sums[:HALF])
+
+
+def embed_rows(chip_ref, other_ref, images_ref, image_side):
     core, side, unused = here()
-    embed = chips_ref[0].astype(jnp.float32) + chips_ref[1].astype(jnp.float32)
-    image_embed = own_half(images_ref, core).astype(jnp.float32) + embed[:HALF]
-    units = []
-    for first, rows in ((0, image_embed), (HALF, embed[HALF:])):
-        inverse = lax.rsqrt(jnp.sum(rows * rows, axis=1, keepdims=True) + epsilon)
-        units.append(rows * inverse)
-        unit_ref[first : first + HALF] = units[-1]
-        inverse_ref[first : first + HALF] = jnp.broadcast_to(inverse, (HALF, LANES))
-    own_sent_ref[...] = jnp.where(side == 0, units[0], units[1]).astype(jnp.bfloat16)
-    moved_sent_ref[...] = jnp.where(side == 0, units[1], units[0]).astype(jnp.bfloat16)
+    residual = own_half(images_ref, core).astype(jnp.float32)
+    sums = chip_ref[...].astype(jnp.float32) + other_ref[...].astype(jnp.float32)
+    return sums + jnp.where(side == image_side, residual, 0.0)
+
+
+def moved_unit_kernel(chip_ref, other_ref, images_ref, sent_ref):
+    rows = embed_rows(chip_ref, other_ref, images_ref, 1)
+    inverse = lax.rsqrt(jnp.sum(rows * rows, axis=1, keepdims=True) + epsilon)
+    sent_ref[...] = (rows * inverse).astype(jnp.bfloat16)
+
+
+def own_unit_kernel(chip_ref, other_ref, images_ref, unit_ref, inverse_ref, sent_ref):
+    rows = embed_rows(chip_ref, other_ref, images_ref, 0)
+    inverse = lax.rsqrt(jnp.sum(rows * rows, axis=1, keepdims=True) + epsilon)
+    unit_ref[...] = rows * inverse
+    inverse_ref[...] = jnp.broadcast_to(inverse, (HALF, LANES))
+    sent_ref[...] = (rows * inverse).astype(jnp.bfloat16)
 
 
 def split_loss(loss):
@@ -177,12 +184,11 @@
 
 def tangent_kernel(kept_ref, swapped_ref, unit_ref, inverse_ref, sent_ref):
     width = unit_ref.shape[1]
-    core, side, unused = here()
+    core, unused, unused = here()
     sums = kept_ref[...] + swapped_ref[1 - core].astype(jnp.float32)
-    side = pl.ds(pl.multiple_of(side * HALF, HALF), HALF)
-    grad, unit = sums[:, :width], unit_ref[side, :]
+    grad, unit = sums[:, :width], unit_ref[...]
     along = jnp.sum(unit * grad, axis=1, keepdims=True)
-    tangent = (grad - unit * along) * inverse_ref[side, :][:, :1]
+    tangent = (grad - unit * along) * inverse_ref[:, :1]
     sent_ref[:, :width] = tangent.astype(jnp.bfloat16)
     loss = sums[:, width : width + 1] + sums[:, width + 1 : width + 2]
     sent_ref[:, width:] = split_loss(loss).astype(jnp.bfloat16)
@@ -239,21 +245,21 @@
         vmem=HEADS_VMEM,
         out_places="hvv",
     )(texts.T, head, images, fc_in.T, fc_out)
-    (core_sum,) = kernel(core_sum_kernel, [((rows, width), bf16)], places="vv")(
+    half = ((HALF, width), bf16)
+    own_chip, moved_chip = kernel(core_sum_kernel, [half, half], places="vv")(
         kept, lax.all_gather(sent, "core")
     )
-    chips = lax.all_gather(core_sum, "y_hi")
-
-    unit, inverse, own_sent, moved_sent = kernel(
-        unit_kernel,
-        [((rows, width), f32), ((rows, LANES), f32)] + [((HALF, width), bf16)] * 2,
-        places="vv",
-    )(chips, images)
-
+    moved_other = lax.ppermute(own_chip, "y_hi", [(0, 1), (1, 0)])
+    own_other = lax.ppermute(moved_chip, "y_hi", [(0, 1), (1, 0)])
+    (moved_sent,) = kernel(moved_unit_kernel, [half], places="vvv")(
+        moved_chip, moved_other, images
+    )
     moved = lax.all_gather(moved_sent, "core", tiled=True)
-    moved, own_sent = lax.optimization_barrier((moved, own_sent))
     first = move(moved, FIRST)
     second = move(moved, SECOND)
+    unit, inverse, own_sent = kernel(
+        own_unit_kernel, [((HALF, width), f32), ((HALF, LANES), f32), half], places="vvv"
+    )(own_chip, own_other, images)
     own = lax.all_gather(own_sent, "core", tiled=True)
     third = move(first, (RELAY, RELAY))
     fourth = move(second, (0, RELAY))

time: 97.2 us -> 93.6 us (0.963)
  starting transfers between devices: 7.65 us -> 27.3 us
  blocking collectives: 48 us -> 35.9 us
  waiting for transfers between devices: 30.3 us -> 18.3 us
    ppermute x4, waiting for transfers between devices: 30.3 us -> 9.37 us  [move(): return lax.ppermute(value, AXES, pairs)]
    ppermute x0 -> x2, starting transfers between devices: none -> 19.1 us  [the longest x1 17.2 us: local(): own_other = lax.ppermute(moved_chip, 'y_hi', [(0, 1), (1, 0)])]
    all_gather x1 -> x0, blocking collectives: 12.8 us -> none  [local(): chips = lax.all_gather(core_sum, 'y_hi')]
    ppermute x0 -> x2, waiting for transfers between devices: none -> 8.94 us  [the longest x1 8.93 us: local(): moved_other = lax.ppermute(own_chip, 'y_hi', [(0, 1), (1, 0)])]
  transfers between devices with their start and end apart: 4 -> 6, of which waited for: 3 -> 4; matrix products, arithmetic and copies ran while one was open for 0% -> 0% of each run, Pallas kernels for 1% -> 1%
where the time goes in v10:
time: 93.6 us; the launch traced here: 92.7 us
  blocking collectives  35.9 us (38%)
  starting transfers between devices  27.3 us (29%)
  waiting for transfers between devices  18.3 us (20%)
  Pallas kernels  9.25 us (10%)
  local copies, waits for them, and re-layouts  1.1 us (1%)
    all_gather x2, blocking collectives, local(): lax.all_gather(sent, 'core')  18.3 us
    ppermute x1, starting transfers between devices, local(): own_other = lax.ppermute(moved_chip, 'y_hi', [(0, 1), (1, 0)])  17.2 us
    all_gather x1, blocking collectives, local(): lax.all_gather(grads, MP)  12.8 us
    ppermute x4, waiting for transfers between devices, move(): return lax.ppermute(value, AXES, pairs)  9.37 us
    ppermute x1, waiting for transfers between devices, local(): moved_other = lax.ppermute(own_chip, 'y_hi', [(0, 1), (1, 0)])  8.93 us
    ppermute x4, starting transfers between devices, move(): return lax.ppermute(value, AXES, pairs)  8.22 us
    pallas_call x1, Pallas kernels, local(): kernel(heads_kernel, [((hidden, rows), f32), ((rows, width), bf16), ((row...  4.91 us
    all_gather x1, blocking collectives, local(): moved = lax.all_gather(moved_sent, 'core', tiled=True)  2.85 us
  transfers between devices with their start and end apart: 6, of which 4 were waited for; matrix products, arithmetic and copies ran while one was open for 0% of the time, Pallas kernels for 1%

profile of v10, /device:TPU:1, one launch (start us, length us, event | category | flops | bytes accessed | tf_op | source)
XLA Modules:
  0.0 92.7 jit_solution(2841154035964076515)
XLA Ops:
  0.6 4.9 %shard_map.85 = (f32[1076,128]{1,0:T(8,128)}, bf16[128,1152]{1,0:T(8,128)(2,1)}, bf16[128,1152]{1,0:T(8,128)(2,1)}) custom-call(bf16[288,128]{1,0:T(8,128)(2,1)} %bitcast.16, bf16[288,1152]{1,0:T(8,128)(2,1)} %head_ref.1, bf16[128,1152]{1,0:T(8,128)(2,1)} %images_ref.3, bf16[1076,1152]{1,0:T(8,128)(2,1)} %bitcast.15, bf16[1076,1152]{1,0:T(8,128)(2,1)} %fc_out_ref.1), custom_call_target="tpu_custom_call" | custom-call | tf_op jit(solution)/shard_map/pallas_call | solution.py:230
  5.6 16.2 %all-gather = bf16[256,1152]{1,0:T(8,128)(2,1)S(1)} all-gather(bf16[128,1152]{1,0:T(8,128)(2,1)} %get-tuple-element.17), channel_id=2, replica_groups=mesh['z'=16,'y_lo'=4,'x'=4,'y_hi'=2,'core'=2] {'core'}, dimensions={0}, use_global_device_ids=true | all-gather | bytes 884736 | tf_op jit(solution)/shard_map/all_gather | solution.py:250
  21.8 1.0 %copy-done.4 = bf16[128,1152]{1,0:T(8,128)(2,1)S(1)} copy-done((bf16[128,1152]{1,0:T(8,128)(2,1)S(1)}, bf16[128,1152]{1,0:T(8,128)(2,1)}, u32[]{:S(2)}) %copy-start.4) | copy-done | bytes 294936
  22.9 1.9 %collective-permute-start.1 = (bf16[64,1152]{1,0:T(8,128)(2,1)S(1)}, bf16[64,1152]{1,0:T(8,128)(2,1)S(1)}, u32[]{:S(2)}, u32[]{:S(2)}) collective-permute-start(bf16[64,1152]{1,0:T(8,128)(2,1)S(1)} %get-tuple-element.18.chip_ref), channel_id=1, source_target_pairs={{0,2},{2,0},{1,3},{3,1},{4,6},{6,4},{5,7},{7,5},{8,10},{10,8},{9,1... | collective-permute-start | bytes 442376 | tf_op jit(solution)/shard_map/ppermute | solution.py:252
  24.8 8.9 %collective-permute-done.1.other_ref = bf16[64,1152]{1,0:T(8,128)(2,1)S(1)} collective-permute-done((bf16[64,1152]{1,0:T(8,128)(2,1)S(1)}, bf16[64,1152]{1,0:T(8,128)(2,1)S(1)}, u32[]{:S(2)}, u32[]{:S(2)}) %collective-permute-start.1) | collective-permute-done | bytes 147488 | tf_op jit(solution)/shard_map/ppermute | solution.py:252
  33.7 0.2 shard_map.88
  33.9 2.9 %all_gather.27.moved_ref = bf16[128,1152]{1,0:T(8,128)(2,1)S(1)} all-gather(bf16[64,1152]{1,0:T(8,128)(2,1)S(1)} %shard_map.88), channel_id=1, replica_groups=mesh['z'=16,'y_lo'=4,'x'=4,'y_hi'=2,'core'=2] {'core'}, dimensions={0}, use_global_device_ids=true | all-gather | bytes 442368 | tf_op jit(solution)/shard_map/all_gather | solution.py:257
  36.7 1.9 %collective-permute-start.2 = (bf16[128,1152]{1,0:T(8,128)(2,1)S(1)}, bf16[128,1152]{1,0:T(8,128)(2,1)S(1)}, u32[]{:S(2)}, u32[]{:S(2)}) collective-permute-start(bf16[128,1152]{1,0:T(8,128)(2,1)S(1)} %all_gather.27.moved_ref), channel_id=1, source_target_pairs={{0,4},{1,13},{2,1020},{3,1013},{4,8},{5,17},{6,2},{7,1017},{8,12},... | collective-permute-start | bytes 884744 | tf_op jit(solution)/shard_map/ppermute | solution.py:43
  38.7 1.9 %collective-permute-start.4 = (bf16[128,1152]{1,0:T(8,128)(2,1)S(1)}, bf16[128,1152]{1,0:T(8,128)(2,1)S(1)}, u32[]{:S(2)}, u32[]{:S(2)}) collective-permute-start(bf16[128,1152]{1,0:T(8,128)(2,1)S(1)} %all_gather.27.moved_ref), channel_id=1, source_target_pairs={{0,16},{1,9},{2,1008},{3,1017},{4,20},{5,13},{6,1012},{7,1021},{8,... | collective-permute-start | bytes 884744 | tf_op jit(solution)/shard_map/ppermute | solution.py:43
  40.6 17.2 %collective-permute-start = (bf16[64,1152]{1,0:T(8,128)(2,1)S(1)}, bf16[64,1152]{1,0:T(8,128)(2,1)S(1)}, u32[]{:S(2)}, u32[]{:S(2)}) collective-permute-start(bf16[64,1152]{1,0:T(8,128)(2,1)S(1)} %get-tuple-element.19.chip_ref), channel_id=1, source_target_pairs={{0,2},{2,0},{1,3},{3,1},{4,6},{6,4},{5,7},{7,5},{8,10},{10,8},{9,1... | collective-permute-start | bytes 442376 | tf_op jit(solution)/shard_map/ppermute | solution.py:253
  57.8 2.5 %collective-permute-start.3 = (bf16[128,1152]{1,0:T(8,128)(2,1)S(1)}, bf16[128,1152]{1,0:T(8,128)(2,1)S(1)}, u32[]{:S(2)}, u32[]{:S(2)}) collective-permute-start(bf16[128,1152]{1,0:T(8,128)(2,1)S(1)} %collective-permute-done.2.first_ref), channel_id=1, source_target_pairs={{0,16},{1,17},{2,1008},{3,1009},{4,20},{5,21},{6,1012},{7,1013},{8... | collective-permute-start | bytes 884744 | tf_op jit(solution)/shard_map/ppermute | solution.py:43
  60.3 1.9 %collective-permute-done.4.second_ref = bf16[128,1152]{1,0:T(8,128)(2,1)S(1)} collective-permute-done((bf16[128,1152]{1,0:T(8,128)(2,1)S(1)}, bf16[128,1152]{1,0:T(8,128)(2,1)S(1)}, u32[]{:S(2)}, u32[]{:S(2)}) %collective-permute-start.4) | collective-permute-done | bytes 294944 | tf_op jit(solution)/shard_map/ppermute | solution.py:43
  62.2 1.9 %collective-permute-start.5 = (bf16[128,1152]{1,0:T(8,128)(2,1)S(1)}, bf16[128,1152]{1,0:T(8,128)(2,1)S(1)}, u32[]{:S(2)}, u32[]{:S(2)}) collective-permute-start(bf16[128,1152]{1,0:T(8,128)(2,1)S(1)} %collective-permute-done.4.second_ref), channel_id=1, source_target_pairs={{1,17},{3,1009},{5,21},{7,1013},{9,25},{11,1017},{13,29},{15,1021}... | collective-permute-start | bytes 884744 | tf_op jit(solution)/shard_map/ppermute | solution.py:43
  64.1 0.1 copy.9.column_ref
  64.3 0.2 shard_map.87
  64.4 2.0 %all_gather.26.own_ref = bf16[128,1152]{1,0:T(8,128)(2,1)S(1)} all-gather(bf16[64,1152]{1,0:T(8,128)(2,1)S(1)} %get-tuple-element.20), channel_id=1, replica_groups=mesh['z'=16,'y_lo'=4,'x'=4,'y_hi'=2,'core'=2] {'core'}, dimensions={0}, use_global_device_ids=true | all-gather | bytes 442368 | tf_op jit(solution)/shard_map/all_gather | solution.py:263
  66.5 1.0 %shard_map.89.early_ref = f32[128,1280]{1,0:T(8,128)S(1)} custom-call(bf16[128,1152]{1,0:T(8,128)(2,1)S(1)} %all_gather.26.own_ref, bf16[128,1152]{1,0:T(8,128)(2,1)S(1)} %collective-permute-done.2.first_ref, bf16[128,1152]{1,0:T(8,128)(2,1)S(1)} %collective-permute-done.4.second_ref), custom_call_target="tpu_custom_call" | custom-call | tf_op jit(solution)/shard_map/pallas_call | solution.py:270
  67.4 2.8 %collective-permute-done.3.third_ref = bf16[128,1152]{1,0:T(8,128)(2,1)S(1)} collective-permute-done((bf16[128,1152]{1,0:T(8,128)(2,1)S(1)}, bf16[128,1152]{1,0:T(8,128)(2,1)S(1)}, u32[]{:S(2)}, u32[]{:S(2)}) %collective-permute-start.3) | collective-permute-done | bytes 294944 | tf_op jit(solution)/shard_map/ppermute | solution.py:43
  70.3 4.6 %collective-permute-done.5.fourth_ref = bf16[128,1152]{1,0:T(8,128)(2,1)S(1)} collective-permute-done((bf16[128,1152]{1,0:T(8,128)(2,1)S(1)}, bf16[128,1152]{1,0:T(8,128)(2,1)S(1)}, u32[]{:S(2)}, u32[]{:S(2)}) %collective-permute-start.5) | collective-permute-done | bytes 294944 | tf_op jit(solution)/shard_map/ppermute | solution.py:43
  74.9 1.1 %shard_map.90 = (f32[64,1280]{1,0:T(8,128)S(1)}, bf16[64,1280]{1,0:T(8,128)(2,1)S(1)}) custom-call(bf16[128,1152]{1,0:T(8,128)(2,1)S(1)} %all_gather.26.own_ref, bf16[128,1152]{1,0:T(8,128)(2,1)S(1)} %all_gather.27.moved_ref, bf16[128,1152]{1,0:T(8,128)(2,1)S(1)} %collective-permute-done.3.third_ref, ...), custom_call_target="tpu_custom_call" | custom-call | tf_op jit(solution)/shard_map/pallas_call | solution.py:271
  76.0 2.0 %all-gather.1 = bf16[128,1280]{1,0:T(8,128)(2,1)S(1)} all-gather(bf16[64,1280]{1,0:T(8,128)(2,1)S(1)} %get-tuple-element.22), channel_id=3, replica_groups=mesh['z'=16,'y_lo'=4,'x'=4,'y_hi'=2,'core'=2] {'core'}, dimensions={0}, use_global_device_ids=true | all-gather | bytes 491520 | tf_op jit(solution)/shard_map/all_gather | solution.py:279
  78.0 0.2 shard_map.91
  78.2 12.8 %all-gather.2 = bf16[256,1280]{1,0:T(8,128)(2,1)S(1)} all-gather(bf16[64,1280]{1,0:T(8,128)(2,1)S(1)} %shard_map.91), channel_id=4, replica_groups=mesh['z'=16,'y_lo'=4,'x'=4,'y_hi'=2,'core'=2] {'y_hi','core'}, dimensions={0}, use_global_device_ids=true | all-gather | bytes 819200 | tf_op jit(solution)/shard_map/all_gather | solution.py:285
  90.9 1.7 %shard_map.92 = (bf16[1076,128]{1,0:T(8,128)(2,1)}, bf16[288,128]{1,0:T(8,128)(2,1)}, f32[1,128]{1,0:T(1,128)}) custom-call(bf16[4,64,1280]{2,1,0:T(8,128)(2,1)S(1)} %bitcast.12, f32[1076,128]{1,0:T(8,128)S(1)} %copy-done.3, bf16[1076,1152]{1,0:T(8,128)(2,1)S(1)} %copy-done, bf16[288,1152]{1,0:T(8,128)(2,1)S(1)} %copy-done.2), custom_call_target="tpu_custom_call" | custom-call | tf_op jit(solution)/shard_map/pallas_call | solution.py:281
  (15 shorter events, 0.1 us)
Async XLA Ops:
  0.6 33.1 %copy-start.1 = (bf16[128,1152]{1,0:T(8,128)(2,1)S(1)}, bf16[128,1152]{1,0:T(8,128)(2,1)}, u32[]{:S(2)}) copy-start(bf16[128,1152]{1,0:T(8,128)(2,1)} %images_ref.3) | copy-start | bytes 884740
  5.6 58.6 %copy-start.5 = (s32[128]{0:T(128)S(1)}, s32[128]{0:T(128)}, u32[]{:S(2)}) copy-start(s32[128]{0:T(128)} %param.11) | copy-start | bytes 1540
  21.8 1.0 %copy-start.4 = (bf16[128,1152]{1,0:T(8,128)(2,1)S(1)}, bf16[128,1152]{1,0:T(8,128)(2,1)}, u32[]{:S(2)}) copy-start(bf16[128,1152]{1,0:T(8,128)(2,1)} %get-tuple-element.16.kept_ref) | copy-start | bytes 884740
  22.9 10.9 %collective-permute-start.1 = (bf16[64,1152]{1,0:T(8,128)(2,1)S(1)}, bf16[64,1152]{1,0:T(8,128)(2,1)S(1)}, u32[]{:S(2)}, u32[]{:S(2)}) collective-permute-start(bf16[64,1152]{1,0:T(8,128)(2,1)S(1)} %get-tuple-element.18.chip_ref), channel_id=1, source_target_pairs={{0,2},{2,0},{1,3},{3,1},{4,6},{6,4},{5,7},{7,5},{8,10},{10,8},{9,1... | collective-permute-start | bytes 442376 | tf_op jit(solution)/shard_map/ppermute | solution.py:252
  36.7 21.0 %collective-permute-start.2 = (bf16[128,1152]{1,0:T(8,128)(2,1)S(1)}, bf16[128,1152]{1,0:T(8,128)(2,1)S(1)}, u32[]{:S(2)}, u32[]{:S(2)}) collective-permute-start(bf16[128,1152]{1,0:T(8,128)(2,1)S(1)} %all_gather.27.moved_ref), channel_id=1, source_target_pairs={{0,4},{1,13},{2,1020},{3,1013},{4,8},{5,17},{6,2},{7,1017},{8,12},... | collective-permute-start | bytes 884744 | tf_op jit(solution)/shard_map/ppermute | solution.py:43
  38.7 23.5 %collective-permute-start.4 = (bf16[128,1152]{1,0:T(8,128)(2,1)S(1)}, bf16[128,1152]{1,0:T(8,128)(2,1)S(1)}, u32[]{:S(2)}, u32[]{:S(2)}) collective-permute-start(bf16[128,1152]{1,0:T(8,128)(2,1)S(1)} %all_gather.27.moved_ref), channel_id=1, source_target_pairs={{0,16},{1,9},{2,1008},{3,1017},{4,20},{5,13},{6,1012},{7,1021},{8,... | collective-permute-start | bytes 884744 | tf_op jit(solution)/shard_map/ppermute | solution.py:43
  40.6 23.7 %collective-permute-start = (bf16[64,1152]{1,0:T(8,128)(2,1)S(1)}, bf16[64,1152]{1,0:T(8,128)(2,1)S(1)}, u32[]{:S(2)}, u32[]{:S(2)}) collective-permute-start(bf16[64,1152]{1,0:T(8,128)(2,1)S(1)} %get-tuple-element.19.chip_ref), channel_id=1, source_target_pairs={{0,2},{2,0},{1,3},{3,1},{4,6},{6,4},{5,7},{7,5},{8,10},{10,8},{9,1... | collective-permute-start | bytes 442376 | tf_op jit(solution)/shard_map/ppermute | solution.py:253
  57.8 12.5 %collective-permute-start.3 = (bf16[128,1152]{1,0:T(8,128)(2,1)S(1)}, bf16[128,1152]{1,0:T(8,128)(2,1)S(1)}, u32[]{:S(2)}, u32[]{:S(2)}) collective-permute-start(bf16[128,1152]{1,0:T(8,128)(2,1)S(1)} %collective-permute-done.2.first_ref), channel_id=1, source_target_pairs={{0,16},{1,17},{2,1008},{3,1009},{4,20},{5,21},{6,1012},{7,1013},{8... | collective-permute-start | bytes 884744 | tf_op jit(solution)/shard_map/ppermute | solution.py:43
  62.2 12.7 %collective-permute-start.5 = (bf16[128,1152]{1,0:T(8,128)(2,1)S(1)}, bf16[128,1152]{1,0:T(8,128)(2,1)S(1)}, u32[]{:S(2)}, u32[]{:S(2)}) collective-permute-start(bf16[128,1152]{1,0:T(8,128)(2,1)S(1)} %collective-permute-done.4.second_ref), channel_id=1, source_target_pairs={{1,17},{3,1009},{5,21},{7,1013},{9,25},{11,1017},{13,29},{15,1021}... | collective-permute-start | bytes 884744 | tf_op jit(solution)/shard_map/ppermute | solution.py:43
  67.4 23.5 %copy-start = (bf16[1076,1152]{1,0:T(8,128)(2,1)S(1)}, bf16[1076,1152]{1,0:T(8,128)(2,1)}, u32[]{:S(2)}) copy-start(bf16[1076,1152]{1,0:T(8,128)(2,1)} %fc_out_ref.1) | copy-start | bytes 7437316
  67.4 23.5 %copy-start.2 = (bf16[288,1152]{1,0:T(8,128)(2,1)S(1)}, bf16[288,1152]{1,0:T(8,128)(2,1)}, u32[]{:S(2)}) copy-start(bf16[288,1152]{1,0:T(8,128)(2,1)} %head_ref.1) | copy-start | bytes 1990660
  67.4 23.5 %copy-start.3 = (f32[1076,128]{1,0:T(8,128)S(1)}, f32[1076,128]{1,0:T(8,128)}, u32[]{:S(2)}) copy-start(f32[1076,128]{1,0:T(8,128)} %get-tuple-element.25.slope_ref) | copy-start | bytes 1652740

commit v11 on v10

--- a/solution.py
+++ b/solution.py
@@ -16,9 +16,10 @@
 AXES = ("z", "y_lo", "x", "y_hi", "core")
 SIZES = (16, 4, 4, 2, 2)
 MP = ("y_hi", "core")
-FIRST = (1, 3)
-SECOND = (4, 2)
-RELAY = 4
+FIRST = (4, 3)
+SECOND = (1, 2)
+THIRD = (1, 4)
+FOURTH = (2, 0)
 HALF = 64
 LANES = 128
 HEADS_VMEM = 56
@@ -136,19 +137,19 @@
     return jnp.where(lanes == 0, high, jnp.where(lanes == 1, loss - high, 0.0))
 
 
-def pair_terms(own, others, positive):
+def pair_terms(own, others, positive, weight=1.0):
     logits = logit_scale * dot(own, others, 1, 1) + logit_bias
     if positive is None:
         flipped = logits
     else:
         flipped = jnp.where(positive, -logits, logits)
     small = jnp.exp(-jnp.abs(flipped))
-    loss = jnp.maximum(flipped, 0.0) + jnp.log1p(small)
+    loss = weight * (jnp.maximum(flipped, 0.0) + jnp.log1p(small))
     sigmoid = jnp.where(flipped >= 0.0, 1.0, small) / (1.0 + small)
     if positive is None:
-        pair_grad = loss_scale * sigmoid
+        pair_grad = weight * loss_scale * sigmoid
     else:
-        pair_grad = jnp.where(positive, -loss_scale, loss_scale) * sigmoid
+        pair_grad = weight * jnp.where(positive, -loss_scale, loss_scale) * sigmoid
     return logit_scale * dot(pair_grad.astype(jnp.bfloat16), others, 1, 0), loss
 
 
@@ -173,10 +174,11 @@
     down = lax.broadcasted_iota(jnp.int32, (rows, rows), 0) == row_ref[...]
     paired = jnp.where(side == 0, across.astype(jnp.int32), down.astype(jnp.int32))
     third, third_loss = pair_terms(own, third_ref[...], None)
-    last = jnp.where(core == 0, moved_ref[...], fourth_ref[...])
-    last, last_loss = pair_terms(own, last, paired == 1)
-    part_ref[:, :width] = early_ref[:, :width] + third + last
-    loss = jnp.sum(third_loss + last_loss, axis=1, keepdims=True)
+    weight = jnp.where(core == 0, 1.0, 0.0)
+    fourth, fourth_loss = pair_terms(own, fourth_ref[...], None, weight)
+    near, near_loss = pair_terms(own, moved_ref[...], paired == 1, weight)
+    part_ref[:, :width] = early_ref[:, :width] + third + fourth + near
+    loss = jnp.sum(third_loss + fourth_loss + near_loss, axis=1, keepdims=True)
     part_ref[:, width:] = split_loss(early_ref[:, width : width + 1] + loss)
     kept_ref[...] = own_half(part_ref, core)
     sent_ref[...] = own_half(part_ref, 1 - core).astype(jnp.bfloat16)
@@ -261,8 +263,8 @@
         own_unit_kernel, [((HALF, width), f32), ((HALF, LANES), f32), half], places="vvv"
     )(own_chip, own_other, images)
     own = lax.all_gather(own_sent, "core", tiled=True)
-    third = move(first, (RELAY, RELAY))
-    fourth = move(second, (0, RELAY))
+    third = move(first, THIRD)
+    fourth = move(first, FOURTH)
 
     paired = jnp.where(lax.axis_index("core") == 0, partner, -1)
     columns = width + LANES

time: 93.6 us -> 98.9 us (1.057)
  the two profiles are of different devices: /device:TPU:1 before, /device:TPU:3 now
where the time goes in v11:
time: 98.9 us; the launch traced here: 98.5 us
  starting transfers between devices  40.4 us (41%)
  blocking collectives  36.8 us (37%)
  waiting for transfers between devices  9.78 us (10%)
  Pallas kernels  9.66 us (10%)
  local copies, waits for them, and re-layouts  1.1 us (1%)
    ppermute x1, starting transfers between devices, local(): own_other = lax.ppermute(moved_chip, 'y_hi', [(0, 1), (1, 0)])  22.8 us
    all_gather x2, blocking collectives, local(): lax.all_gather(sent, 'core')  16.7 us
    all_gather x1, blocking collectives, local(): lax.all_gather(grads, MP)  11.9 us
    ppermute x4, starting transfers between devices, move(): return lax.ppermute(value, AXES, pairs)  10.1 us
    ppermute x1, starting transfers between devices, local(): moved_other = lax.ppermute(own_chip, 'y_hi', [(0, 1), (1, 0)])  7.46 us
    ppermute x4, waiting for transfers between devices, move(): return lax.ppermute(value, AXES, pairs)  5.98 us
    all_gather x1, blocking collectives, local(): own = lax.all_gather(own_sent, 'core', tiled=True)  5.45 us
    pallas_call x1, Pallas kernels, local(): kernel(heads_kernel, [((hidden, rows), f32), ((rows, width), bf16), ((row...  4.91 us
  transfers between devices with their start and end apart: 6, of which 3 were waited for; matrix products, arithmetic and copies ran while one was open for 0% of the time, Pallas kernels for 1%

profile of v11, /device:TPU:3, one launch (start us, length us, event | category | flops | bytes accessed | tf_op | source)
XLA Modules:
  0.0 98.5 jit_solution(9039751565981564869)
XLA Ops:
  0.6 4.9 %shard_map.85 = (f32[1076,128]{1,0:T(8,128)}, bf16[128,1152]{1,0:T(8,128)(2,1)}, bf16[128,1152]{1,0:T(8,128)(2,1)}) custom-call(bf16[288,128]{1,0:T(8,128)(2,1)} %bitcast.16, bf16[288,1152]{1,0:T(8,128)(2,1)} %head_ref.1, bf16[128,1152]{1,0:T(8,128)(2,1)} %images_ref.3, bf16[1076,1152]{1,0:T(8,128)(2,1)} %bitcast.15, bf16[1076,1152]{1,0:T(8,128)(2,1)} %fc_out_ref.1), custom_call_target="tpu_custom_call" | custom-call | tf_op jit(solution)/shard_map/pallas_call | solution.py:232
  5.6 2.7 %all-gather = bf16[256,1152]{1,0:T(8,128)(2,1)S(1)} all-gather(bf16[128,1152]{1,0:T(8,128)(2,1)} %get-tuple-element.17), channel_id=2, replica_groups=mesh['z'=16,'y_lo'=4,'x'=4,'y_hi'=2,'core'=2] {'core'}, dimensions={0}, use_global_device_ids=true | all-gather | bytes 884736 | tf_op jit(solution)/shard_map/all_gather | solution.py:252
  8.3 1.0 copy-done.4
  9.3 0.1 shard_map.86
  9.4 7.5 %collective-permute-start.1 = (bf16[64,1152]{1,0:T(8,128)(2,1)S(1)}, bf16[64,1152]{1,0:T(8,128)(2,1)S(1)}, u32[]{:S(2)}, u32[]{:S(2)}) collective-permute-start(bf16[64,1152]{1,0:T(8,128)(2,1)S(1)} %get-tuple-element.18.chip_ref), channel_id=1, source_target_pairs={{0,2},{2,0},{1,3},{3,1},{4,6},{6,4},{5,7},{7,5},{8,10},{10,8},{9,1... | collective-permute-start | bytes 442376 | tf_op jit(solution)/shard_map/ppermute | solution.py:254
  16.8 3.8 %collective-permute-done.1.other_ref = bf16[64,1152]{1,0:T(8,128)(2,1)S(1)} collective-permute-done((bf16[64,1152]{1,0:T(8,128)(2,1)S(1)}, bf16[64,1152]{1,0:T(8,128)(2,1)S(1)}, u32[]{:S(2)}, u32[]{:S(2)}) %collective-permute-start.1) | collective-permute-done | bytes 147488 | tf_op jit(solution)/shard_map/ppermute | solution.py:254
  20.6 0.2 shard_map.88
  20.8 2.7 %all_gather.27.moved_ref = bf16[128,1152]{1,0:T(8,128)(2,1)S(1)} all-gather(bf16[64,1152]{1,0:T(8,128)(2,1)S(1)} %shard_map.88), channel_id=1, replica_groups=mesh['z'=16,'y_lo'=4,'x'=4,'y_hi'=2,'core'=2] {'core'}, dimensions={0}, use_global_device_ids=true | all-gather | bytes 442368 | tf_op jit(solution)/shard_map/all_gather | solution.py:259
  23.5 5.6 %collective-permute-start.2 = (bf16[128,1152]{1,0:T(8,128)(2,1)S(1)}, bf16[128,1152]{1,0:T(8,128)(2,1)S(1)}, u32[]{:S(2)}, u32[]{:S(2)}) collective-permute-start(bf16[128,1152]{1,0:T(8,128)(2,1)S(1)} %all_gather.27.moved_ref), channel_id=1, source_target_pairs={{0,16},{1,13},{2,1008},{3,1013},{4,20},{5,17},{6,1012},{7,1017},{8... | collective-permute-start | bytes 884744 | tf_op jit(solution)/shard_map/ppermute | solution.py:44
  29.1 22.8 %collective-permute-start = (bf16[64,1152]{1,0:T(8,128)(2,1)S(1)}, bf16[64,1152]{1,0:T(8,128)(2,1)S(1)}, u32[]{:S(2)}, u32[]{:S(2)}) collective-permute-start(bf16[64,1152]{1,0:T(8,128)(2,1)S(1)} %get-tuple-element.19.chip_ref), channel_id=1, source_target_pairs={{0,2},{2,0},{1,3},{3,1},{4,6},{6,4},{5,7},{7,5},{8,10},{10,8},{9,1... | collective-permute-start | bytes 442376 | tf_op jit(solution)/shard_map/ppermute | solution.py:255
  52.0 1.9 %collective-permute-start.5 = (bf16[128,1152]{1,0:T(8,128)(2,1)S(1)}, bf16[128,1152]{1,0:T(8,128)(2,1)S(1)}, u32[]{:S(2)}, u32[]{:S(2)}) collective-permute-start(bf16[128,1152]{1,0:T(8,128)(2,1)S(1)} %all_gather.27.moved_ref), channel_id=1, source_target_pairs={{0,4},{1,9},{2,1020},{3,1017},{4,8},{5,13},{6,2},{7,1021},{8,12},{... | collective-permute-start | bytes 884744 | tf_op jit(solution)/shard_map/ppermute | solution.py:44
  53.9 2.4 %collective-permute-done.2.first_ref = bf16[128,1152]{1,0:T(8,128)(2,1)S(1)} collective-permute-done((bf16[128,1152]{1,0:T(8,128)(2,1)S(1)}, bf16[128,1152]{1,0:T(8,128)(2,1)S(1)}, u32[]{:S(2)}, u32[]{:S(2)}) %collective-permute-start.2) | collective-permute-done | bytes 294944 | tf_op jit(solution)/shard_map/ppermute | solution.py:44
  56.3 1.9 %collective-permute-start.3 = (bf16[128,1152]{1,0:T(8,128)(2,1)S(1)}, bf16[128,1152]{1,0:T(8,128)(2,1)S(1)}, u32[]{:S(2)}, u32[]{:S(2)}) collective-permute-start(bf16[128,1152]{1,0:T(8,128)(2,1)S(1)} %collective-permute-done.2.first_ref), channel_id=1, source_target_pairs={{0,4},{1,17},{2,1020},{3,1009},{4,8},{5,21},{6,2},{7,1013},{8,12},... | collective-permute-start | bytes 884744 | tf_op jit(solution)/shard_map/ppermute | solution.py:44
  58.2 0.7 collective-permute-start.4
  59.0 0.1 copy.9.column_ref
  59.1 0.2 shard_map.87
  59.2 5.4 %all_gather.26.own_ref = bf16[128,1152]{1,0:T(8,128)(2,1)S(1)} all-gather(bf16[64,1152]{1,0:T(8,128)(2,1)S(1)} %get-tuple-element.20), channel_id=1, replica_groups=mesh['z'=16,'y_lo'=4,'x'=4,'y_hi'=2,'core'=2] {'core'}, dimensions={0}, use_global_device_ids=true | all-gather | bytes 442368 | tf_op jit(solution)/shard_map/all_gather | solution.py:265
  64.7 3.6 %collective-permute-done.5.second_ref = bf16[128,1152]{1,0:T(8,128)(2,1)S(1)} collective-permute-done((bf16[128,1152]{1,0:T(8,128)(2,1)S(1)}, bf16[128,1152]{1,0:T(8,128)(2,1)S(1)}, u32[]{:S(2)}, u32[]{:S(2)}) %collective-permute-start.5) | collective-permute-done | bytes 294944 | tf_op jit(solution)/shard_map/ppermute | solution.py:44
  68.3 0.9 shard_map.89.early_ref
  69.3 1.5 %shard_map.90 = (f32[64,1280]{1,0:T(8,128)S(1)}, bf16[64,1280]{1,0:T(8,128)(2,1)S(1)}) custom-call(bf16[128,1152]{1,0:T(8,128)(2,1)S(1)} %all_gather.26.own_ref, bf16[128,1152]{1,0:T(8,128)(2,1)S(1)} %all_gather.27.moved_ref, bf16[128,1152]{1,0:T(8,128)(2,1)S(1)} %collective-permute-done.3.third_ref, ...), custom_call_target="tpu_custom_call" | custom-call | tf_op jit(solution)/shard_map/pallas_call | solution.py:273
  70.8 13.9 %all-gather.1 = bf16[128,1280]{1,0:T(8,128)(2,1)S(1)} all-gather(bf16[64,1280]{1,0:T(8,128)(2,1)S(1)} %get-tuple-element.22), channel_id=3, replica_groups=mesh['z'=16,'y_lo'=4,'x'=4,'y_hi'=2,'core'=2] {'core'}, dimensions={0}, use_global_device_ids=true | all-gather | bytes 491520 | tf_op jit(solution)/shard_map/all_gather | solution.py:281
  84.7 0.2 shard_map.91
  84.9 11.9 %all-gather.2 = bf16[256,1280]{1,0:T(8,128)(2,1)S(1)} all-gather(bf16[64,1280]{1,0:T(8,128)(2,1)S(1)} %shard_map.91), channel_id=4, replica_groups=mesh['z'=16,'y_lo'=4,'x'=4,'y_hi'=2,'core'=2] {'y_hi','core'}, dimensions={0}, use_global_device_ids=true | all-gather | bytes 819200 | tf_op jit(solution)/shard_map/all_gather | solution.py:287
  96.8 1.7 %shard_map.92 = (bf16[1076,128]{1,0:T(8,128)(2,1)}, bf16[288,128]{1,0:T(8,128)(2,1)}, f32[1,128]{1,0:T(1,128)}) custom-call(bf16[4,64,1280]{2,1,0:T(8,128)(2,1)S(1)} %bitcast.12, f32[1076,128]{1,0:T(8,128)S(1)} %copy-done.3, bf16[1076,1152]{1,0:T(8,128)(2,1)S(1)} %copy-done, bf16[288,1152]{1,0:T(8,128)(2,1)S(1)} %copy-done.2), custom_call_target="tpu_custom_call" | custom-call | tf_op jit(solution)/shard_map/pallas_call | solution.py:283
  (15 shorter events, 0.0 us)
Async XLA Ops:
  0.6 20.0 %copy-start.1 = (bf16[128,1152]{1,0:T(8,128)(2,1)S(1)}, bf16[128,1152]{1,0:T(8,128)(2,1)}, u32[]{:S(2)}) copy-start(bf16[128,1152]{1,0:T(8,128)(2,1)} %images_ref.3) | copy-start | bytes 884740
  5.6 53.4 %copy-start.5 = (s32[128]{0:T(128)S(1)}, s32[128]{0:T(128)}, u32[]{:S(2)}) copy-start(s32[128]{0:T(128)} %param.11) | copy-start | bytes 1540
  8.3 1.0 copy-start.4
  9.4 11.3 %collective-permute-start.1 = (bf16[64,1152]{1,0:T(8,128)(2,1)S(1)}, bf16[64,1152]{1,0:T(8,128)(2,1)S(1)}, u32[]{:S(2)}, u32[]{:S(2)}) collective-permute-start(bf16[64,1152]{1,0:T(8,128)(2,1)S(1)} %get-tuple-element.18.chip_ref), channel_id=1, source_target_pairs={{0,2},{2,0},{1,3},{3,1},{4,6},{6,4},{5,7},{7,5},{8,10},{10,8},{9,1... | collective-permute-start | bytes 442376 | tf_op jit(solution)/shard_map/ppermute | solution.py:254
  23.5 32.8 %collective-permute-start.2 = (bf16[128,1152]{1,0:T(8,128)(2,1)S(1)}, bf16[128,1152]{1,0:T(8,128)(2,1)S(1)}, u32[]{:S(2)}, u32[]{:S(2)}) collective-permute-start(bf16[128,1152]{1,0:T(8,128)(2,1)S(1)} %all_gather.27.moved_ref), channel_id=1, source_target_pairs={{0,16},{1,13},{2,1008},{3,1013},{4,20},{5,17},{6,1012},{7,1017},{8... | collective-permute-start | bytes 884744 | tf_op jit(solution)/shard_map/ppermute | solution.py:44
  29.1 29.9 %collective-permute-start = (bf16[64,1152]{1,0:T(8,128)(2,1)S(1)}, bf16[64,1152]{1,0:T(8,128)(2,1)S(1)}, u32[]{:S(2)}, u32[]{:S(2)}) collective-permute-start(bf16[64,1152]{1,0:T(8,128)(2,1)S(1)} %get-tuple-element.19.chip_ref), channel_id=1, source_target_pairs={{0,2},{2,0},{1,3},{3,1},{4,6},{6,4},{5,7},{7,5},{8,10},{10,8},{9,1... | collective-permute-start | bytes 442376 | tf_op jit(solution)/shard_map/ppermute | solution.py:255
  52.0 16.3 %collective-permute-start.5 = (bf16[128,1152]{1,0:T(8,128)(2,1)S(1)}, bf16[128,1152]{1,0:T(8,128)(2,1)S(1)}, u32[]{:S(2)}, u32[]{:S(2)}) collective-permute-start(bf16[128,1152]{1,0:T(8,128)(2,1)S(1)} %all_gather.27.moved_ref), channel_id=1, source_target_pairs={{0,4},{1,9},{2,1020},{3,1017},{4,8},{5,13},{6,2},{7,1021},{8,12},{... | collective-permute-start | bytes 884744 | tf_op jit(solution)/shard_map/ppermute | solution.py:44
  56.3 12.9 %collective-permute-start.3 = (bf16[128,1152]{1,0:T(8,128)(2,1)S(1)}, bf16[128,1152]{1,0:T(8,128)(2,1)S(1)}, u32[]{:S(2)}, u32[]{:S(2)}) collective-permute-start(bf16[128,1152]{1,0:T(8,128)(2,1)S(1)} %collective-permute-done.2.first_ref), channel_id=1, source_target_pairs={{0,4},{1,17},{2,1020},{3,1009},{4,8},{5,21},{6,2},{7,1013},{8,12},... | collective-permute-start | bytes 884744 | tf_op jit(solution)/shard_map/ppermute | solution.py:44
  58.2 11.0 %collective-permute-start.4 = (bf16[128,1152]{1,0:T(8,128)(2,1)S(1)}, bf16[128,1152]{1,0:T(8,128)(2,1)S(1)}, u32[]{:S(2)}, u32[]{:S(2)}) collective-permute-start(bf16[128,1152]{1,0:T(8,128)(2,1)S(1)} %collective-permute-done.2.first_ref), channel_id=1, source_target_pairs={{0,8},{2,1016},{4,12},{6,1020},{8,16},{10,2},{12,20},{14,6},{16,24... | collective-permute-start | bytes 884744 | tf_op jit(solution)/shard_map/ppermute | solution.py:44
  69.2 27.5 %copy-start = (bf16[1076,1152]{1,0:T(8,128)(2,1)S(1)}, bf16[1076,1152]{1,0:T(8,128)(2,1)}, u32[]{:S(2)}) copy-start(bf16[1076,1152]{1,0:T(8,128)(2,1)} %fc_out_ref.1) | copy-start | bytes 7437316
  69.2 27.5 %copy-start.2 = (bf16[288,1152]{1,0:T(8,128)(2,1)S(1)}, bf16[288,1152]{1,0:T(8,128)(2,1)}, u32[]{:S(2)}) copy-start(bf16[288,1152]{1,0:T(8,128)(2,1)} %head_ref.1) | copy-start | bytes 1990660
  69.3 27.5 %copy-start.3 = (f32[1076,128]{1,0:T(8,128)S(1)}, f32[1076,128]{1,0:T(8,128)}, u32[]{:S(2)}) copy-start(f32[1076,128]{1,0:T(8,128)} %get-tuple-element.25.slope_ref) | copy-start | bytes 1652740

commit v12 on v10

--- a/solution.py
+++ b/solution.py
@@ -109,21 +109,22 @@
     moved_ref[...] = jnp.where(side == 0, sums[HALF:], sums[:HALF])
 
 
-def embed_rows(chip_ref, other_ref, images_ref, image_side):
+def embed_rows(chip_ref, other, images_ref, image_side):
     core, side, unused = here()
     residual = own_half(images_ref, core).astype(jnp.float32)
-    sums = chip_ref[...].astype(jnp.float32) + other_ref[...].astype(jnp.float32)
+    sums = chip_ref[...].astype(jnp.float32) + other.astype(jnp.float32)
     return sums + jnp.where(side == image_side, residual, 0.0)
 
 
-def moved_unit_kernel(chip_ref, other_ref, images_ref, sent_ref):
-    rows = embed_rows(chip_ref, other_ref, images_ref, 1)
+def moved_unit_kernel(chip_ref, chips_ref, images_ref, sent_ref):
+    other = chips_ref[1 - lax.axis_index("y_hi")]
+    rows = embed_rows(chip_ref, other, images_ref, 1)
     inverse = lax.rsqrt(jnp.sum(rows * rows, axis=1, keepdims=True) + epsilon)
     sent_ref[...] = (rows * inverse).astype(jnp.bfloat16)
 
 
 def own_unit_kernel(chip_ref, other_ref, images_ref, unit_ref, inverse_ref, sent_ref):
-    rows = embed_rows(chip_ref, other_ref, images_ref, 0)
+    rows = embed_rows(chip_ref, other_ref[...], images_ref, 0)
     inverse = lax.rsqrt(jnp.sum(rows * rows, axis=1, keepdims=True) + epsilon)
     unit_ref[...] = rows * inverse
     inverse_ref[...] = jnp.broadcast_to(inverse, (HALF, LANES))
@@ -249,7 +250,7 @@
     own_chip, moved_chip = kernel(core_sum_kernel, [half, half], places="vv")(
         kept, lax.all_gather(sent, "core")
     )
-    moved_other = lax.ppermute(own_chip, "y_hi", [(0, 1), (1, 0)])
+    moved_other = lax.all_gather(own_chip, "y_hi")
     own_other = lax.ppermute(moved_chip, "y_hi", [(0, 1), (1, 0)])
     (moved_sent,) = kernel(moved_unit_kernel, [half], places="vvv")(
         moved_chip, moved_other, images

time: 93.6 us -> 92.4 us (0.987)
  blocking collectives: 35.9 us -> 45.6 us
  waiting for transfers between devices: 18.3 us -> 9.35 us
  starting transfers between devices: 27.3 us -> 25.4 us
    all_gather x0 -> x1, blocking collectives: none -> 9.65 us  [local(): moved_other = lax.all_gather(own_chip, 'y_hi')]
    ppermute x1 -> x0, waiting for transfers between devices: 8.93 us -> none  [local(): moved_other = lax.ppermute(own_chip, 'y_hi', [(0, 1), (1, 0)])]
    ppermute x1 -> x0, starting transfers between devices: 1.92 us -> none  [local(): moved_other = lax.ppermute(own_chip, 'y_hi', [(0, 1), (1, 0)])]
  transfers between devices with their start and end apart: 6 -> 5, of which waited for: 4 -> 3; matrix products, arithmetic and copies ran while one was open for 0% -> 0% of each run, Pallas kernels for 1% -> 1%
where the time goes in v12:
time: 92.4 us; the launch traced here: 91.5 us
  blocking collectives  45.6 us (49%)
  starting transfers between devices  25.4 us (27%)
  waiting for transfers between devices  9.35 us (10%)
  Pallas kernels  9.27 us (10%)
  local copies, waits for them, and re-layouts  1.1 us (1%)
    all_gather x2, blocking collectives, local(): lax.all_gather(sent, 'core')  18.3 us
    ppermute x1, starting transfers between devices, local(): own_other = lax.ppermute(moved_chip, 'y_hi', [(0, 1), (1, 0)])  17.2 us
    all_gather x1, blocking collectives, local(): lax.all_gather(grads, MP)  12.8 us
    all_gather x1, blocking collectives, local(): moved_other = lax.all_gather(own_chip, 'y_hi')  9.65 us
    ppermute x4, waiting for transfers between devices, move(): return lax.ppermute(value, AXES, pairs)  9.35 us
    ppermute x4, starting transfers between devices, move(): return lax.ppermute(value, AXES, pairs)  8.25 us
    pallas_call x1, Pallas kernels, local(): kernel(heads_kernel, [((hidden, rows), f32), ((rows, width), bf16), ((row...  4.93 us
    all_gather x1, blocking collectives, local(): moved = lax.all_gather(moved_sent, 'core', tiled=True)  2.85 us
  transfers between devices with their start and end apart: 5, of which 3 were waited for; matrix products, arithmetic and copies ran while one was open for 0% of the time, Pallas kernels for 1%

profile of v12, /device:TPU:1, one launch (start us, length us, event | category | flops | bytes accessed | tf_op | source)
XLA Modules:
  0.0 91.5 jit_solution(14137779263316944608)
XLA Ops:
  0.6 4.9 %shard_map.85 = (f32[1076,128]{1,0:T(8,128)}, bf16[128,1152]{1,0:T(8,128)(2,1)}, bf16[128,1152]{1,0:T(8,128)(2,1)}) custom-call(bf16[288,128]{1,0:T(8,128)(2,1)} %bitcast.18, bf16[288,1152]{1,0:T(8,128)(2,1)} %head_ref.1, bf16[128,1152]{1,0:T(8,128)(2,1)} %images_ref.3, bf16[1076,1152]{1,0:T(8,128)(2,1)} %bitcast.17, bf16[1076,1152]{1,0:T(8,128)(2,1)} %fc_out_ref.1), custom_call_target="tpu_custom_call" | custom-call | tf_op jit(solution)/shard_map/pallas_call | solution.py:231
  5.6 16.2 %all-gather = bf16[256,1152]{1,0:T(8,128)(2,1)S(1)} all-gather(bf16[128,1152]{1,0:T(8,128)(2,1)} %get-tuple-element.17), channel_id=2, replica_groups=mesh['z'=16,'y_lo'=4,'x'=4,'y_hi'=2,'core'=2] {'core'}, dimensions={0}, use_global_device_ids=true | all-gather | bytes 884736 | tf_op jit(solution)/shard_map/all_gather | solution.py:251
  21.8 1.0 %copy-done.4 = bf16[128,1152]{1,0:T(8,128)(2,1)S(1)} copy-done((bf16[128,1152]{1,0:T(8,128)(2,1)S(1)}, bf16[128,1152]{1,0:T(8,128)(2,1)}, u32[]{:S(2)}) %copy-start.4) | copy-done | bytes 294936
  22.8 0.1 shard_map.86
  22.9 9.6 %all-gather.1 = bf16[128,1152]{1,0:T(8,128)(2,1)S(1)} all-gather(bf16[64,1152]{1,0:T(8,128)(2,1)S(1)} %get-tuple-element.18.chip_ref), channel_id=3, replica_groups=mesh['z'=16,'y_lo'=4,'x'=4,'y_hi'=2,'core'=2] {'y_hi'}, dimensions={0}, use_global_device_ids=true | all-gather | bytes 442368 | tf_op jit(solution)/shard_map/all_gather | solution.py:253
  32.5 0.2 shard_map.88
  32.7 2.9 %all_gather.35.moved_ref = bf16[128,1152]{1,0:T(8,128)(2,1)S(1)} all-gather(bf16[64,1152]{1,0:T(8,128)(2,1)S(1)} %shard_map.88), channel_id=1, replica_groups=mesh['z'=16,'y_lo'=4,'x'=4,'y_hi'=2,'core'=2] {'core'}, dimensions={0}, use_global_device_ids=true | all-gather | bytes 442368 | tf_op jit(solution)/shard_map/all_gather | solution.py:258
  35.5 1.9 %collective-permute-start.1 = (bf16[128,1152]{1,0:T(8,128)(2,1)S(1)}, bf16[128,1152]{1,0:T(8,128)(2,1)S(1)}, u32[]{:S(2)}, u32[]{:S(2)}) collective-permute-start(bf16[128,1152]{1,0:T(8,128)(2,1)S(1)} %all_gather.35.moved_ref), channel_id=1, source_target_pairs={{0,4},{1,13},{2,1020},{3,1013},{4,8},{5,17},{6,2},{7,1017},{8,12},... | collective-permute-start | bytes 884744 | tf_op jit(solution)/shard_map/ppermute | solution.py:43
  37.5 1.9 %collective-permute-start.3 = (bf16[128,1152]{1,0:T(8,128)(2,1)S(1)}, bf16[128,1152]{1,0:T(8,128)(2,1)S(1)}, u32[]{:S(2)}, u32[]{:S(2)}) collective-permute-start(bf16[128,1152]{1,0:T(8,128)(2,1)S(1)} %all_gather.35.moved_ref), channel_id=1, source_target_pairs={{0,16},{1,9},{2,1008},{3,1017},{4,20},{5,13},{6,1012},{7,1021},{8,... | collective-permute-start | bytes 884744 | tf_op jit(solution)/shard_map/ppermute | solution.py:43
  39.4 17.2 %collective-permute-start = (bf16[64,1152]{1,0:T(8,128)(2,1)S(1)}, bf16[64,1152]{1,0:T(8,128)(2,1)S(1)}, u32[]{:S(2)}, u32[]{:S(2)}) collective-permute-start(bf16[64,1152]{1,0:T(8,128)(2,1)S(1)} %get-tuple-element.19.chip_ref), channel_id=1, source_target_pairs={{0,2},{2,0},{1,3},{3,1},{4,6},{6,4},{5,7},{7,5},{8,10},{10,8},{9,1... | collective-permute-start | bytes 442376 | tf_op jit(solution)/shard_map/ppermute | solution.py:254
  56.6 2.5 %collective-permute-start.2 = (bf16[128,1152]{1,0:T(8,128)(2,1)S(1)}, bf16[128,1152]{1,0:T(8,128)(2,1)S(1)}, u32[]{:S(2)}, u32[]{:S(2)}) collective-permute-start(bf16[128,1152]{1,0:T(8,128)(2,1)S(1)} %collective-permute-done.1.first_ref), channel_id=1, source_target_pairs={{0,16},{1,17},{2,1008},{3,1009},{4,20},{5,21},{6,1012},{7,1013},{8... | collective-permute-start | bytes 884744 | tf_op jit(solution)/shard_map/ppermute | solution.py:43
  59.1 1.9 %collective-permute-done.3.second_ref = bf16[128,1152]{1,0:T(8,128)(2,1)S(1)} collective-permute-done((bf16[128,1152]{1,0:T(8,128)(2,1)S(1)}, bf16[128,1152]{1,0:T(8,128)(2,1)S(1)}, u32[]{:S(2)}, u32[]{:S(2)}) %collective-permute-start.3) | collective-permute-done | bytes 294944 | tf_op jit(solution)/shard_map/ppermute | solution.py:43
  61.0 1.9 %collective-permute-start.4 = (bf16[128,1152]{1,0:T(8,128)(2,1)S(1)}, bf16[128,1152]{1,0:T(8,128)(2,1)S(1)}, u32[]{:S(2)}, u32[]{:S(2)}) collective-permute-start(bf16[128,1152]{1,0:T(8,128)(2,1)S(1)} %collective-permute-done.3.second_ref), channel_id=1, source_target_pairs={{1,17},{3,1009},{5,21},{7,1013},{9,25},{11,1017},{13,29},{15,1021}... | collective-permute-start | bytes 884744 | tf_op jit(solution)/shard_map/ppermute | solution.py:43
  62.9 0.1 copy.9.column_ref
  63.1 0.2 shard_map.87
  63.2 2.0 %all_gather.32.own_ref = bf16[128,1152]{1,0:T(8,128)(2,1)S(1)} all-gather(bf16[64,1152]{1,0:T(8,128)(2,1)S(1)} %get-tuple-element.20), channel_id=1, replica_groups=mesh['z'=16,'y_lo'=4,'x'=4,'y_hi'=2,'core'=2] {'core'}, dimensions={0}, use_global_device_ids=true | all-gather | bytes 442368 | tf_op jit(solution)/shard_map/all_gather | solution.py:264
  65.3 1.0 %shard_map.89.early_ref = f32[128,1280]{1,0:T(8,128)S(1)} custom-call(bf16[128,1152]{1,0:T(8,128)(2,1)S(1)} %all_gather.32.own_ref, bf16[128,1152]{1,0:T(8,128)(2,1)S(1)} %collective-permute-done.1.first_ref, bf16[128,1152]{1,0:T(8,128)(2,1)S(1)} %collective-permute-done.3.second_ref), custom_call_target="tpu_custom_call" | custom-call | tf_op jit(solution)/shard_map/pallas_call | solution.py:271
  66.2 2.8 %collective-permute-done.2.third_ref = bf16[128,1152]{1,0:T(8,128)(2,1)S(1)} collective-permute-done((bf16[128,1152]{1,0:T(8,128)(2,1)S(1)}, bf16[128,1152]{1,0:T(8,128)(2,1)S(1)}, u32[]{:S(2)}, u32[]{:S(2)}) %collective-permute-start.2) | collective-permute-done | bytes 294944 | tf_op jit(solution)/shard_map/ppermute | solution.py:43
  69.0 4.7 %collective-permute-done.4.fourth_ref = bf16[128,1152]{1,0:T(8,128)(2,1)S(1)} collective-permute-done((bf16[128,1152]{1,0:T(8,128)(2,1)S(1)}, bf16[128,1152]{1,0:T(8,128)(2,1)S(1)}, u32[]{:S(2)}, u32[]{:S(2)}) %collective-permute-start.4) | collective-permute-done | bytes 294944 | tf_op jit(solution)/shard_map/ppermute | solution.py:43
  73.7 1.1 %shard_map.90 = (f32[64,1280]{1,0:T(8,128)S(1)}, bf16[64,1280]{1,0:T(8,128)(2,1)S(1)}) custom-call(bf16[128,1152]{1,0:T(8,128)(2,1)S(1)} %all_gather.32.own_ref, bf16[128,1152]{1,0:T(8,128)(2,1)S(1)} %all_gather.35.moved_ref, bf16[128,1152]{1,0:T(8,128)(2,1)S(1)} %collective-permute-done.2.third_ref, ...), custom_call_target="tpu_custom_call" | custom-call | tf_op jit(solution)/shard_map/pallas_call | solution.py:272
  74.7 2.0 %all-gather.2 = bf16[128,1280]{1,0:T(8,128)(2,1)S(1)} all-gather(bf16[64,1280]{1,0:T(8,128)(2,1)S(1)} %get-tuple-element.22), channel_id=4, replica_groups=mesh['z'=16,'y_lo'=4,'x'=4,'y_hi'=2,'core'=2] {'core'}, dimensions={0}, use_global_device_ids=true | all-gather | bytes 491520 | tf_op jit(solution)/shard_map/all_gather | solution.py:280
  76.8 0.2 shard_map.91
  76.9 12.8 %all-gather.3 = bf16[256,1280]{1,0:T(8,128)(2,1)S(1)} all-gather(bf16[64,1280]{1,0:T(8,128)(2,1)S(1)} %shard_map.91), channel_id=5, replica_groups=mesh['z'=16,'y_lo'=4,'x'=4,'y_hi'=2,'core'=2] {'y_hi','core'}, dimensions={0}, use_global_device_ids=true | all-gather | bytes 819200 | tf_op jit(solution)/shard_map/all_gather | solution.py:286
  89.7 1.7 %shard_map.92 = (bf16[1076,128]{1,0:T(8,128)(2,1)}, bf16[288,128]{1,0:T(8,128)(2,1)}, f32[1,128]{1,0:T(1,128)}) custom-call(bf16[4,64,1280]{2,1,0:T(8,128)(2,1)S(1)} %bitcast.13, f32[1076,128]{1,0:T(8,128)S(1)} %copy-done.3, bf16[1076,1152]{1,0:T(8,128)(2,1)S(1)} %copy-done, bf16[288,1152]{1,0:T(8,128)(2,1)S(1)} %copy-done.2), custom_call_target="tpu_custom_call" | custom-call | tf_op jit(solution)/shard_map/pallas_call | solution.py:282
  (14 shorter events, 0.0 us)
Async XLA Ops:
  0.6 31.9 %copy-start.1 = (bf16[128,1152]{1,0:T(8,128)(2,1)S(1)}, bf16[128,1152]{1,0:T(8,128)(2,1)}, u32[]{:S(2)}) copy-start(bf16[128,1152]{1,0:T(8,128)(2,1)} %images_ref.3) | copy-start | bytes 884740
  5.6 57.3 %copy-start.5 = (s32[128]{0:T(128)S(1)}, s32[128]{0:T(128)}, u32[]{:S(2)}) copy-start(s32[128]{0:T(128)} %param.11) | copy-start | bytes 1540
  21.8 1.0 %copy-start.4 = (bf16[128,1152]{1,0:T(8,128)(2,1)S(1)}, bf16[128,1152]{1,0:T(8,128)(2,1)}, u32[]{:S(2)}) copy-start(bf16[128,1152]{1,0:T(8,128)(2,1)} %get-tuple-element.16.kept_ref) | copy-start | bytes 884740
  35.5 21.0 %collective-permute-start.1 = (bf16[128,1152]{1,0:T(8,128)(2,1)S(1)}, bf16[128,1152]{1,0:T(8,128)(2,1)S(1)}, u32[]{:S(2)}, u32[]{:S(2)}) collective-permute-start(bf16[128,1152]{1,0:T(8,128)(2,1)S(1)} %all_gather.35.moved_ref), channel_id=1, source_target_pairs={{0,4},{1,13},{2,1020},{3,1013},{4,8},{5,17},{6,2},{7,1017},{8,12},... | collective-permute-start | bytes 884744 | tf_op jit(solution)/shard_map/ppermute | solution.py:43
  37.5 23.5 %collective-permute-start.3 = (bf16[128,1152]{1,0:T(8,128)(2,1)S(1)}, bf16[128,1152]{1,0:T(8,128)(2,1)S(1)}, u32[]{:S(2)}, u32[]{:S(2)}) collective-permute-start(bf16[128,1152]{1,0:T(8,128)(2,1)S(1)} %all_gather.35.moved_ref), channel_id=1, source_target_pairs={{0,16},{1,9},{2,1008},{3,1017},{4,20},{5,13},{6,1012},{7,1021},{8,... | collective-permute-start | bytes 884744 | tf_op jit(solution)/shard_map/ppermute | solution.py:43
  39.4 23.7 %collective-permute-start = (bf16[64,1152]{1,0:T(8,128)(2,1)S(1)}, bf16[64,1152]{1,0:T(8,128)(2,1)S(1)}, u32[]{:S(2)}, u32[]{:S(2)}) collective-permute-start(bf16[64,1152]{1,0:T(8,128)(2,1)S(1)} %get-tuple-element.19.chip_ref), channel_id=1, source_target_pairs={{0,2},{2,0},{1,3},{3,1},{4,6},{6,4},{5,7},{7,5},{8,10},{10,8},{9,1... | collective-permute-start | bytes 442376 | tf_op jit(solution)/shard_map/ppermute | solution.py:254
  56.6 12.4 %collective-permute-start.2 = (bf16[128,1152]{1,0:T(8,128)(2,1)S(1)}, bf16[128,1152]{1,0:T(8,128)(2,1)S(1)}, u32[]{:S(2)}, u32[]{:S(2)}) collective-permute-start(bf16[128,1152]{1,0:T(8,128)(2,1)S(1)} %collective-permute-done.1.first_ref), channel_id=1, source_target_pairs={{0,16},{1,17},{2,1008},{3,1009},{4,20},{5,21},{6,1012},{7,1013},{8... | collective-permute-start | bytes 884744 | tf_op jit(solution)/shard_map/ppermute | solution.py:43
  61.0 12.7 %collective-permute-start.4 = (bf16[128,1152]{1,0:T(8,128)(2,1)S(1)}, bf16[128,1152]{1,0:T(8,128)(2,1)S(1)}, u32[]{:S(2)}, u32[]{:S(2)}) collective-permute-start(bf16[128,1152]{1,0:T(8,128)(2,1)S(1)} %collective-permute-done.3.second_ref), channel_id=1, source_target_pairs={{1,17},{3,1009},{5,21},{7,1013},{9,25},{11,1017},{13,29},{15,1021}... | collective-permute-start | bytes 884744 | tf_op jit(solution)/shard_map/ppermute | solution.py:43
  66.2 23.5 %copy-start = (bf16[1076,1152]{1,0:T(8,128)(2,1)S(1)}, bf16[1076,1152]{1,0:T(8,128)(2,1)}, u32[]{:S(2)}) copy-start(bf16[1076,1152]{1,0:T(8,128)(2,1)} %fc_out_ref.1) | copy-start | bytes 7437316
  66.2 23.5 %copy-start.2 = (bf16[288,1152]{1,0:T(8,128)(2,1)S(1)}, bf16[288,1152]{1,0:T(8,128)(2,1)}, u32[]{:S(2)}) copy-start(bf16[288,1152]{1,0:T(8,128)(2,1)} %head_ref.1) | copy-start | bytes 1990660
  66.2 23.5 %copy-start.3 = (f32[1076,128]{1,0:T(8,128)S(1)}, f32[1076,128]{1,0:T(8,128)}, u32[]{:S(2)}) copy-start(f32[1076,128]{1,0:T(8,128)} %get-tuple-element.25.slope_ref) | copy-start | bytes 1652740
